TPU v7x, 128 devices: a whole 4x4x4 slice. The times are simulated.
128 devices in a mesh: gx: 8 (over y_lo, z), gy: 16 (over y_hi, x, core).
Axes of the slice: x: 4, y: 4 (y_hi: 2, y_lo: 2; y = y_hi * 2 + y_lo), z: 4, core: 2. Of those that a mesh axis runs over, the one named last changes fastest.
Arguments:
- positions: float32 [3, 8, 16, 32768], P(None, 'gx', 'gy'), may hold values from 0 to 1024, as said below
- polarity: float32 [8, 16, 32768], P('gx', 'gy'), may hold values from 0.4 to 2.5
- dipoles: float32 [6, 8, 16, 32768], P(None, 'gx', 'gy'), may hold values from -6 to 6
- perm_fields: float32 [6, 8, 16, 32768], P(None, 'gx', 'gy'), may hold values from -6 to 6
- pair_list: int32 [8, 16, 2, 2048], P('gx', 'gy'), may hold values from 0 to 2303, as said below
- tile_counts: int32 [8, 16], P('gx', 'gy'), may hold values from 256 to 2048, as said below
Outputs:
- field: float32 [6, 8, 16, 32768], P(None, 'gx', 'gy')
- induced: float32 [6, 8, 16, 32768], P(None, 'gx', 'gy')
Inputs may be any that keep to these rules, and one draw needn't show every extreme that they name: `pair_list`: entry [0, p] is a tile of the domain itself; entry [1, p] = s * 256 + t names tile t of image s, the domain at offset (s // 3 - 1, s % 3 - 1) along (gx, gy), s = 4 being the domain itself. Slots at or past the domain's count are unused. `tile_counts`: some domains use all 2048 slots. `positions`: site k of tile t lies within 0.6 along each coordinate of the point (2 (k % 8) + 1, 2 ((k // 8) % 8) + 1, 4 t + 2 (k // 64) + 1); every domain is 16 wide along both periodic directions.
All inputs are finite; a program needn't handle non-finite values.
Results may differ from a plain program's by a relative error of at most 0.0003.
Values sent between devices are 32-bit elements; how exact they have to be, the bound alone decides.
A program may use at most 128 MiB of HBM per device.

v0:
```python
import jax
import jax.numpy as jnp
from jax import lax
from jax.sharding import PartitionSpec as P

TILE = 128


thole = 0.39
domain_edge = 16.0


def with_halo(block, sides, width):
    for axis, dim in sides:
        count = lax.axis_size(axis)
        forward = [(i, i + 1) for i in range(count - 1)]
        forward.append((count - 1, 0))
        backward = [(target, source) for source, target in forward]
        low = lax.ppermute(
            lax.slice_in_dim(block, block.shape[dim] - width, None, axis=dim), axis, forward
        )
        high = lax.ppermute(lax.slice_in_dim(block, 0, width, axis=dim), axis, backward)
        block = jnp.concatenate([low, block, high], axis=dim)
    return block


def shifted(value, axis, steps):
    count = lax.axis_size(axis)
    pairs = [(source, (source + steps) % count) for source in range(count)]
    return lax.ppermute(value, axis, pairs)


def pair_terms(near_sites, far_sites, self_flag):
    diagonal_ones = jnp.eye(TILE, dtype=jnp.float32)
    self_mask = self_flag[:, None, None] * diagonal_ones[None]
    keep_mask = 1.0 - self_mask
    delta_x = near_sites[:, 0, :, None] - far_sites[:, 0, None, :]
    delta_y = near_sites[:, 1, :, None] - far_sites[:, 1, None, :]
    delta_z = near_sites[:, 2, :, None] - far_sites[:, 2, None, :]
    dist_sq = delta_x * delta_x + delta_y * delta_y + delta_z * delta_z + self_mask
    distance = jnp.sqrt(dist_sq)
    inv_sq = 1.0 / dist_sq
    inv_cube = inv_sq / distance
    pol_scale = jnp.sqrt(near_sites[:, 3, :, None] * far_sites[:, 3, None, :])
    damp_arg = thole * dist_sq * distance / pol_scale
    lam_three = -jnp.expm1(-damp_arg)
    lam_five = lam_three - damp_arg * jnp.exp(-damp_arg)
    coef_three = keep_mask * lam_three * inv_cube
    coef_five = 3.0 * keep_mask * lam_five * inv_cube * inv_sq
    deltas = (delta_x, delta_y, delta_z)
    near_out = []
    far_out = []
    for set_row in (4, 7):
        dip_far = far_sites[:, set_row : set_row + 3]
        dip_near = near_sites[:, set_row : set_row + 3]
        dot_far = (
            delta_x * dip_far[:, 0, None, :]
            + delta_y * dip_far[:, 1, None, :]
            + delta_z * dip_far[:, 2, None, :]
        )
        dot_near = (
            delta_x * dip_near[:, 0, :, None]
            + delta_y * dip_near[:, 1, :, None]
            + delta_z * dip_near[:, 2, :, None]
        )
        for column in range(3):
            near_out.append(
                jnp.sum(
                    coef_five * dot_far * deltas[column] - coef_three * dip_far[:, column, None, :],
                    axis=2,
                )
            )
            far_out.append(
                jnp.sum(
                    coef_five * dot_near * deltas[column]
                    - coef_three * dip_near[:, column, :, None],
                    axis=1,
                )
            )
    far_keep = (1.0 - self_flag)[:, None, None]
    return (jnp.stack(near_out, 1), jnp.stack(far_out, 1) * far_keep)


def local(positions, polarity, dipoles, perm_fields, pair_list, tile_counts):
    site_total = positions.shape[3]
    tile_total = site_total // TILE
    slot_total = pair_list.shape[3]
    batch_rows = slot_total // 16
    sites = jnp.concatenate([positions, polarity[None], dipoles], 0)
    halo = with_halo(sites, (("gx", 1), ("gy", 2)), 1)
    offsets = (jnp.arange(3, dtype=jnp.float32) - 1.0) * domain_edge
    halo = halo.at[0].add(offsets[:, None, None]).at[1].add(offsets[None, :, None])
    halo_tiles = (
        halo.reshape(10, 9, tile_total, TILE)
        .transpose(1, 2, 0, 3)
        .reshape(9 * tile_total, 10, TILE)
    )
    own_tiles = sites.reshape(10, tile_total, TILE).transpose(1, 0, 2)
    slot_table = pair_list.reshape(2, slot_total)
    used_count = tile_counts.reshape(())
    row_range = jnp.arange(batch_rows, dtype=jnp.int32)
    rounds = (used_count + batch_rows - 1) // batch_rows

    def one_round(round_index, partial_value):
        near_acc, far_acc = partial_value
        first_row = (round_index * batch_rows).astype(jnp.int32)
        slot_ids = lax.dynamic_slice_in_dim(slot_table, first_row, batch_rows, 1)
        near_sites = own_tiles[slot_ids[0]]
        far_sites = halo_tiles[slot_ids[1]]
        self_flag = (slot_ids[1] == slot_ids[0] + 4 * tile_total).astype(jnp.float32)
        live_rows = (first_row + row_range < used_count).astype(jnp.float32)
        near_part, far_part = pair_terms(near_sites, far_sites, self_flag)
        near_acc = near_acc.at[slot_ids[0]].add(
            near_part.reshape(batch_rows, 6 * TILE) * live_rows[:, None]
        )
        far_acc = far_acc.at[slot_ids[1]].add(
            far_part.reshape(batch_rows, 6 * TILE) * live_rows[:, None]
        )
        return (near_acc, far_acc)

    start_acc = (
        jnp.zeros((tile_total, 6 * TILE), jnp.float32),
        jnp.zeros((9 * tile_total, 6 * TILE), jnp.float32),
    )
    near_acc, far_acc = lax.fori_loop(0, rounds, one_round, start_acc)
    far_grid = far_acc.reshape(3, 3, tile_total * 6 * TILE)
    column_sum = far_grid[:, 1]
    for shift_by, slot_col in ((-1, 0), (1, 2)):
        column_sum = column_sum + shifted(far_grid[:, slot_col], "gy", shift_by)
    gathered_terms = column_sum[1]
    for shift_by, slot_row in ((-1, 0), (1, 2)):
        gathered_terms = gathered_terms + shifted(column_sum[slot_row], "gx", shift_by)
    total_field = near_acc + gathered_terms.reshape(tile_total, 6 * TILE)
    field = total_field.reshape(tile_total, 6, TILE).transpose(1, 0, 2).reshape(6, 1, 1, site_total)
    induced = polarity[None] * (perm_fields + field)
    return (field, induced)


def solution(mesh):
    placed = (
        P(None, "gx", "gy", None),
        P("gx", "gy", None),
        P(None, "gx", "gy", None),
        P(None, "gx", "gy", None),
        P("gx", "gy", None, None),
        P("gx", "gy"),
    )
    return jax.shard_map(
        local,
        mesh=mesh,
        in_specs=placed,
        out_specs=(P(None, "gx", "gy", None), P(None, "gx", "gy", None)),
        check_vma=False,
    )
```

profile of v0, /device:TPU:4, one launch (start us, length us, event | category | flops | bytes accessed | tf_op | source)
XLA Modules:
  0.0 1599.6 jit_solution(3548324599014413970)
XLA Ops:
  0.7 2.6 pad_maximum_fusion.2
  3.3 5.1 collective-permute-start.1
  8.4 28.0 %collective-permute-done.1 = f32[10,1,1,32768]{3,2,1,0:T(1,128)S(1)} collective-permute-done((f32[10,1,1,32768]{3,2,1,0:T(1,128)S(1)}, f32[10,1,1,32768]{3,2,1,0:T(1,128)S(1)}, u32[]{:S(2)}, u32[]{:S(2)}) %collective-permute-start.1) | collective-permute-done | bytes 1310752 | tf_op jit(solution)/shard_map/ppermute | solution.py:22
  36.4 4.3 collective-permute-done
  40.7 1.1 copy-done.2
  41.8 8.2 pad_maximum_fusion.1
  50.0 0.5 collective-permute-start.2
  51.3 2.1 copy.33
  53.4 40.1 %collective-permute-done.3 = f32[10,3,1,32768]{3,2,1,0:T(1,128)} collective-permute-done((f32[10,3,1,32768]{3,2,1,0:T(1,128)}, f32[10,3,1,32768]{3,2,1,0:T(1,128)}, u32[]{:S(2)}, u32[]{:S(2)}) %collective-permute-start.3) | collective-permute-done | bytes 3932192 | tf_op jit(solution)/shard_map/ppermute | solution.py:22
  93.5 1.9 collective-permute-done.2
  95.4 16.0 pad_maximum_fusion
  111.4 2.9 fusion.56
  114.3 2.9 fusion.55
  117.2 17.7 %reshape.217 = f32[10,9,256,128]{3,2,1,0:T(8,128)} reshape(f32[10,3,3,32768]{3,2,1,0:T(4,128)} %fusion.55) | data formatting | bytes 23592960 | tf_op jit(solution)/shard_map/reshape | solution.py:94
  135.0 17.9 %copy.32 = f32[10,9,256,128]{3,0,2,1:T(8,128)} copy(f32[10,9,256,128]{3,2,1,0:T(8,128)} %reshape.217) | data formatting | bytes 23592960 | tf_op jit(solution)/shard_map/reshape | solution.py:94
  152.9 3.3 broadcast_in_dim.7
  156.3 338.5 %while.15 = (s32[]{:T(128)}, f32[256,768]{1,0:T(8,128)S(1)}, f32[2304,768]{1,0:T(8,128)}, s32[]{:T(128)}, s32[2,2048]{1,0:T(2,128)}, /*index=5*/f32[256,10,128]{...) while((s32[]{:T(128)}, f32[256,768]{1,0:T(8,128)S(1)}, ...), condition=%wide.region_15.16_spmd.clone, body=%wide.region_0.15_spmd.clone.sunk | while | flops 268766848 | bytes 16731823 | solution.py:125
  156.3 0.6 compare_convert_fusion.3
  156.9 0.7 constant_dynamic-slice_fusion.2
  157.7 2.2 gather_fusion
  160.4 7.0 gather_fusion.1
  167.9 26.2 %fusion.75 = (f32[128,128]{1,0:T(8,128)S(1)}, f32[128,128]{1,0:T(8,128)S(1)}, f32[128,128]{1,0:T(8,128)S(1)}) fusion(f32[128,128]{1,0:T(8,128)S(1)} %bitcast.201, f32[128,128]{1,0:T(8,128)S(1)} %bitcast.194, f32[128,128]{1,0:T(8,128)S(1)} %bitcast.183, f32[128,128]{1,0:T(8,128)S(1)} %bitcast.202, f32[128,128]{1,0:T(8,128)S(1)} %bitcast.203, ...), kind=kLoop, calls=%fused_computation.75.clone.1 | loop fusion | flops 96419840 | bytes 983552 | tf_op jit(solution)/shard_map/while/body/reduce_sum | solution.py:68
  194.1 36.9 %fusion.74 = (f32[128,128]{1,0:T(8,128)S(1)}, f32[128,128]{1,0:T(8,128)S(1)}, f32[128,128]{1,0:T(8,128)S(1)}, f32[128,128]{1,0:T(8,128)S(1)}, f32[128,128]{1,0:T...) fusion(f32[128,128]{1,0:T(8,128)S(1)} %bitcast.189, ...), kind=kLoop, calls=%fused_computation.81.clone.1 | loop fusion | flops 171819008 | bytes 1769984 | tf_op jit(solution)/shard_map/while/body/reduce_sum | solution.py:74
  231.8 1.7 scatter_fusion
  233.7 7.2 scatter_fusion.1
  240.9 0.6 compare_convert_fusion.3
  241.6 0.7 constant_dynamic-slice_fusion.2
  242.3 2.2 gather_fusion
  245.0 7.0 gather_fusion.1
  252.5 26.2 %fusion.75 = (f32[128,128]{1,0:T(8,128)S(1)}, f32[128,128]{1,0:T(8,128)S(1)}, f32[128,128]{1,0:T(8,128)S(1)}) fusion(f32[128,128]{1,0:T(8,128)S(1)} %bitcast.201, f32[128,128]{1,0:T(8,128)S(1)} %bitcast.194, f32[128,128]{1,0:T(8,128)S(1)} %bitcast.183, f32[128,128]{1,0:T(8,128)S(1)} %bitcast.202, f32[128,128]{1,0:T(8,128)S(1)} %bitcast.203, ...), kind=kLoop, calls=%fused_computation.75.clone.1 | loop fusion | flops 96419840 | bytes 983552 | tf_op jit(solution)/shard_map/while/body/reduce_sum | solution.py:68
  278.8 36.9 %fusion.74 = (f32[128,128]{1,0:T(8,128)S(1)}, f32[128,128]{1,0:T(8,128)S(1)}, f32[128,128]{1,0:T(8,128)S(1)}, f32[128,128]{1,0:T(8,128)S(1)}, f32[128,128]{1,0:T...) fusion(f32[128,128]{1,0:T(8,128)S(1)} %bitcast.189, ...), kind=kLoop, calls=%fused_computation.81.clone.1 | loop fusion | flops 171819008 | bytes 1769984 | tf_op jit(solution)/shard_map/while/body/reduce_sum | solution.py:74
  316.4 1.7 scatter_fusion
  318.3 7.2 scatter_fusion.1
  325.5 0.6 compare_convert_fusion.3
  326.2 0.7 constant_dynamic-slice_fusion.2
  326.9 2.2 gather_fusion
  329.6 7.0 gather_fusion.1
  337.1 26.2 %fusion.75 = (f32[128,128]{1,0:T(8,128)S(1)}, f32[128,128]{1,0:T(8,128)S(1)}, f32[128,128]{1,0:T(8,128)S(1)}) fusion(f32[128,128]{1,0:T(8,128)S(1)} %bitcast.201, f32[128,128]{1,0:T(8,128)S(1)} %bitcast.194, f32[128,128]{1,0:T(8,128)S(1)} %bitcast.183, f32[128,128]{1,0:T(8,128)S(1)} %bitcast.202, f32[128,128]{1,0:T(8,128)S(1)} %bitcast.203, ...), kind=kLoop, calls=%fused_computation.75.clone.1 | loop fusion | flops 96419840 | bytes 983552 | tf_op jit(solution)/shard_map/while/body/reduce_sum | solution.py:68
  363.4 36.9 %fusion.74 = (f32[128,128]{1,0:T(8,128)S(1)}, f32[128,128]{1,0:T(8,128)S(1)}, f32[128,128]{1,0:T(8,128)S(1)}, f32[128,128]{1,0:T(8,128)S(1)}, f32[128,128]{1,0:T...) fusion(f32[128,128]{1,0:T(8,128)S(1)} %bitcast.189, ...), kind=kLoop, calls=%fused_computation.81.clone.1 | loop fusion | flops 171819008 | bytes 1769984 | tf_op jit(solution)/shard_map/while/body/reduce_sum | solution.py:74
  401.0 1.7 scatter_fusion
  402.9 7.2 scatter_fusion.1
  410.1 0.6 compare_convert_fusion.3
  410.8 0.7 constant_dynamic-slice_fusion.2
  411.5 2.2 gather_fusion
  414.3 7.0 gather_fusion.1
  421.8 26.2 %fusion.75 = (f32[128,128]{1,0:T(8,128)S(1)}, f32[128,128]{1,0:T(8,128)S(1)}, f32[128,128]{1,0:T(8,128)S(1)}) fusion(f32[128,128]{1,0:T(8,128)S(1)} %bitcast.201, f32[128,128]{1,0:T(8,128)S(1)} %bitcast.194, f32[128,128]{1,0:T(8,128)S(1)} %bitcast.183, f32[128,128]{1,0:T(8,128)S(1)} %bitcast.202, f32[128,128]{1,0:T(8,128)S(1)} %bitcast.203, ...), kind=kLoop, calls=%fused_computation.75.clone.1 | loop fusion | flops 96419840 | bytes 983552 | tf_op jit(solution)/shard_map/while/body/reduce_sum | solution.py:68
  448.0 36.9 %fusion.74 = (f32[128,128]{1,0:T(8,128)S(1)}, f32[128,128]{1,0:T(8,128)S(1)}, f32[128,128]{1,0:T(8,128)S(1)}, f32[128,128]{1,0:T(8,128)S(1)}, f32[128,128]{1,0:T...) fusion(f32[128,128]{1,0:T(8,128)S(1)} %bitcast.189, ...), kind=kLoop, calls=%fused_computation.81.clone.1 | loop fusion | flops 171819008 | bytes 1769984 | tf_op jit(solution)/shard_map/while/body/reduce_sum | solution.py:74
  485.6 1.7 scatter_fusion
  487.5 7.2 scatter_fusion.1
  494.8 9.4 reshape.219
  504.2 12.8 fusion.61
  517.0 3.3 copy.55
  520.3 3.3 copy.54
  523.7 0.5 collective-permute-start.5
  524.2 34.3 %collective-permute-done.4 = f32[3,196608]{1,0:T(4,128)S(1)} collective-permute-done((f32[3,196608]{1,0:T(4,128)S(1)}, f32[3,196608]{1,0:T(4,128)S(1)}, u32[]{:S(2)}, u32[]{:S(2)}) %collective-permute-start.4) | collective-permute-done | bytes 2359328 | tf_op jit(solution)/shard_map/ppermute | solution.py:30
  558.5 170.1 %collective-permute-done.5 = f32[3,196608]{1,0:T(4,128)S(1)} collective-permute-done((f32[3,196608]{1,0:T(4,128)S(1)}, f32[3,196608]{1,0:T(4,128)S(1)}, u32[]{:S(2)}, u32[]{:S(2)}) %collective-permute-start.5) | collective-permute-done | bytes 2359328 | tf_op jit(solution)/shard_map/ppermute | solution.py:30
  728.5 3.3 fusion.54
  731.8 1.7 fusion.62
  733.5 845.7 %collective-permute-start.7 = (f32[196608]{0:T(1024)S(1)}, f32[196608]{0:T(1024)S(1)}, u32[]{:S(2)}, u32[]{:S(2)}) collective-permute-start(f32[196608]{0:T(1024)S(1)} %bitcast.205), channel_id=1, source_target_pairs={{0,16},{16,32},{32,48},{48,64},{64,80},{80,96},{96,112},{112,0},{1... | collective-permute-start | bytes 2359304 | tf_op jit(solution)/shard_map/ppermute | solution.py:30
  1579.1 2.4 collective-permute-start.6
  1581.5 12.5 collective-permute-done.7
  1594.1 2.2 collective-permute-done.6
  1597.4 0.5 fusion.57
  1598.0 1.7 copy.40
  (115 shorter events, 8.4 us)
Async XLA Ops:
  0.6 50.6 %copy-start = (f32[6,1,1,32768]{3,2,1,0:T(1,128)S(1)}, f32[6,1,1,32768]{3,2,1,0:T(1,128)}, u32[]{:S(2)}) copy-start(f32[6,1,1,32768]{3,2,1,0:T(1,128)} %param.14) | copy-start | bytes 2359300
  0.6 50.6 %copy-start.1 = (f32[3,1,1,32768]{3,2,1,0:T(1,128)S(1)}, f32[3,1,1,32768]{3,2,1,0:T(1,128)}, u32[]{:S(2)}) copy-start(f32[3,1,1,32768]{3,2,1,0:T(1,128)} %param.12) | copy-start | bytes 1179652
  0.7 50.6 %copy-start.3 = (f32[1,1,32768]{2,1,0:T(1,128)S(1)}, f32[1,1,32768]{2,1,0:T(1,128)}, u32[]{:S(2)}) copy-start(f32[1,1,32768]{2,1,0:T(1,128)} %param.13) | copy-start | bytes 393220
  3.3 33.2 %collective-permute-start.1 = (f32[10,1,1,32768]{3,2,1,0:T(1,128)S(1)}, f32[10,1,1,32768]{3,2,1,0:T(1,128)S(1)}, u32[]{:S(2)}, u32[]{:S(2)}) collective-permute-start(f32[10,1,1,32768]{3,2,1,0:T(1,128)S(1)} %pad_maximum_fusion.2), channel_id=1, source_target_pairs={{16,0},{32,16},{48,32},{64,48},{80,64},{96,80},{112,96},{0,112},{1... | collective-permute-start | bytes 3932168 | tf_op jit(solution)/shard_map/ppermute | solution.py:22
  8.4 32.3 %collective-permute-start = (f32[10,1,1,32768]{3,2,1,0:T(1,128)S(1)}, f32[10,1,1,32768]{3,2,1,0:T(1,128)S(1)}, u32[]{:S(2)}, u32[]{:S(2)}) collective-permute-start(f32[10,1,1,32768]{3,2,1,0:T(1,128)S(1)} %pad_maximum_fusion.2), channel_id=1, source_target_pairs={{0,16},{16,32},{32,48},{48,64},{64,80},{80,96},{96,112},{112,0},{1... | collective-permute-start | bytes 3932168 | tf_op jit(solution)/shard_map/ppermute | solution.py:19
  40.7 1.1 copy-start.2
  50.0 43.5 %collective-permute-start.3 = (f32[10,3,1,32768]{3,2,1,0:T(1,128)}, f32[10,3,1,32768]{3,2,1,0:T(1,128)}, u32[]{:S(2)}, u32[]{:S(2)}) collective-permute-start(f32[10,3,1,32768]{3,2,1,0:T(1,128)} %pad_maximum_fusion.1), channel_id=1, source_target_pairs={{1,0},{2,1},{3,2},{4,3},{5,4},{6,5},{7,6},{8,7},{9,8},{10,9},{11,1... | collective-permute-start | bytes 11796488 | tf_op jit(solution)/shard_map/ppermute | solution.py:22
  50.0 45.4 %collective-permute-start.2 = (f32[10,3,1,32768]{3,2,1,0:T(1,128)}, f32[10,3,1,32768]{3,2,1,0:T(1,128)}, u32[]{:S(2)}, u32[]{:S(2)}) collective-permute-start(f32[10,3,1,32768]{3,2,1,0:T(1,128)} %pad_maximum_fusion.1), channel_id=1, source_target_pairs={{0,1},{1,2},{2,3},{3,4},{4,5},{5,6},{6,7},{7,8},{8,9},{9,10},{10,1... | collective-permute-start | bytes 11796488 | tf_op jit(solution)/shard_map/ppermute | solution.py:19
  523.6 34.9 %collective-permute-start.4 = (f32[3,196608]{1,0:T(4,128)S(1)}, f32[3,196608]{1,0:T(4,128)S(1)}, u32[]{:S(2)}, u32[]{:S(2)}) collective-permute-start(f32[3,196608]{1,0:T(4,128)S(1)} %bitcast.175), channel_id=1, source_target_pairs={{0,15},{1,0},{2,1},{3,2},{4,3},{5,4},{6,5},{7,6},{8,7},{9,8},{10,9... | collective-permute-start | bytes 7077896 | tf_op jit(solution)/shard_map/ppermute | solution.py:30
  523.7 204.8 %collective-permute-start.5 = (f32[3,196608]{1,0:T(4,128)S(1)}, f32[3,196608]{1,0:T(4,128)S(1)}, u32[]{:S(2)}, u32[]{:S(2)}) collective-permute-start(f32[3,196608]{1,0:T(4,128)S(1)} %bitcast.174), channel_id=1, source_target_pairs={{0,1},{1,2},{2,3},{3,4},{4,5},{5,6},{6,7},{7,8},{8,9},{9,10},{10,1... | collective-permute-start | bytes 7077896 | tf_op jit(solution)/shard_map/ppermute | solution.py:30
  731.8 865.6 %copy-start.5 = (f32[6,1,1,32768]{3,2,1,0:T(1,128)S(1)}, f32[6,1,1,32768]{3,2,1,0:T(1,128)}, u32[]{:S(2)}) copy-start(f32[6,1,1,32768]{3,2,1,0:T(1,128)} %param.15) | copy-start | bytes 2359300
  733.5 860.6 %collective-permute-start.7 = (f32[196608]{0:T(1024)S(1)}, f32[196608]{0:T(1024)S(1)}, u32[]{:S(2)}, u32[]{:S(2)}) collective-permute-start(f32[196608]{0:T(1024)S(1)} %bitcast.205), channel_id=1, source_target_pairs={{0,16},{16,32},{32,48},{48,64},{64,80},{80,96},{96,112},{112,0},{1... | collective-permute-start | bytes 2359304 | tf_op jit(solution)/shard_map/ppermute | solution.py:30
  1579.1 17.1 %collective-permute-start.6 = (f32[196608]{0:T(1024)S(1)}, f32[196608]{0:T(1024)S(1)}, u32[]{:S(2)}, u32[]{:S(2)}) collective-permute-start(f32[196608]{0:T(1024)S(1)} %bitcast.204), channel_id=1, source_target_pairs={{0,112},{16,0},{32,16},{48,32},{64,48},{80,64},{96,80},{112,96},{1... | collective-permute-start | bytes 2359304 | tf_op jit(solution)/shard_map/ppermute | solution.py:30
  1597.2 2.5 copy-start.4
where the time goes:
time: 1600 us
  starting transfers between devices  854 us (53%)
  other arithmetic  328 us (20%)
  waiting for transfers between devices  293 us (18%)
  local copies, waits for them, and re-layouts  122 us (8%)
    ppermute x4, starting transfers between devices, shifted(): return lax.ppermute(value, axis, pairs)  849 us
    ppermute x4, waiting for transfers between devices, shifted(): return lax.ppermute(value, axis, pairs)  219 us
    reduce_sum x4, other arithmetic, pair_terms(): jnp.sum(coef_five * dot_near * deltas[column] - coef_three * dip_near[:,...  147 us
    reduce_sum x4, other arithmetic, pair_terms(): jnp.sum(coef_five * dot_far * deltas[column] - coef_three * dip_far[:, co...  105 us
    ppermute x2, waiting for transfers between devices, with_halo(): lax.ppermute(lax.slice_in_dim(block, 0, width, axis=dim), axis, backward)  68.1 us
    reshape x2, local copies, waits for them, and re-layouts, local(): halo.reshape(10, 9, tile_total, TILE).transpose(1, 2, 0, 3)  35.7 us
  transfers between devices with their start and end apart: 8, of which 8 were waited for; matrix products, arithmetic and copies ran while one was open for 0% of the time, Pallas kernels for 0%

commit v1 on v0

v1 whole, which is shorter than its diff:
```python
import jax
import jax.numpy as jnp
from jax import lax
from jax.experimental import pallas as pl
from jax.experimental.pallas import tpu as pltpu
from jax.sharding import PartitionSpec as P

TILE = 128
TILES = 256
ROWS = 10 * TILES
UNROLL = 4

thole = 0.39
domain_edge = 16.0

F32 = jnp.float32
BF16 = jnp.bfloat16


def three_parts(value):
    high = value.astype(BF16)
    rest = value - high.astype(F32)
    middle = rest.astype(BF16)
    low = (rest - middle.astype(F32)).astype(BF16)
    return high, middle, low


def rows_of():
    sub = lax.broadcasted_iota(jnp.int32, (8, TILE), 0)
    second = (sub == 3) | (sub == 4) | (sub == 5) | (sub == 7)
    is_x = (sub == 0) | (sub == 3)
    is_y = (sub == 1) | (sub == 4)
    is_z = (sub == 2) | (sub == 5)
    return sub, second, is_x, is_y, is_z


def load_row(ref, row):
    return jnp.broadcast_to(ref[pl.ds(row, 1), :], (8, TILE))


def site_vectors(ref, base, centre):
    sub, second, is_x, is_y, is_z = rows_of()
    dips = [load_row(ref, base + k * TILES) for k in range(6)]
    pos = [load_row(ref, base + (6 + k) * TILES) - centre[k] for k in range(3)]
    pol = load_row(ref, base + 9 * TILES)
    mu = [jnp.where(second, dips[3 + j], dips[j]) for j in range(3)]
    mixed = jnp.where(is_x, pos[0], jnp.where(is_y, pos[1], jnp.where(is_z, pos[2], 1.0)))
    own = jnp.where(is_x, mu[0], jnp.where(is_y, mu[1], jnp.where(is_z, mu[2], 0.0)))
    return mu, pos, pol, mixed, own


def dipole_rows(mu, pos, mixed, own):
    dots = pos[0] * mu[0] + pos[1] * mu[1] + pos[2] * mu[2]
    tripled = 3.0 * mixed
    left = jnp.concatenate([tripled * mu[0], tripled * mu[1], tripled * mu[2], tripled * dots], 0)
    blank = jnp.zeros((16, TILE), BF16)
    right = jnp.concatenate([jnp.zeros((8, TILE), F32), -own], 0)
    out = []
    for l, r in zip(three_parts(left), three_parts(right)):
        out.append(jnp.concatenate([l, jnp.concatenate([blank, r], 0)], 1))
    return jnp.concatenate(out, 0)


def geometry_rows(first_three, fourth, fifth):
    sub = lax.broadcasted_iota(jnp.int32, (8, TILE), 0)
    rows = jnp.where(sub == 0, first_three[0], jnp.where(sub == 1, first_three[1], jnp.where(sub == 2, first_three[2], jnp.where(sub == 3, fourth, jnp.where(sub == 4, fifth, 0.0)))))
    return tuple(p.astype(F32) for p in three_parts(rows))


def scale_rows(scale, pattern):
    sub = lax.broadcasted_iota(jnp.int32, (8, TILE), 0)
    parts = [p.astype(F32) for p in three_parts(scale)]
    out = jnp.zeros((8, TILE), F32)
    for row, part in enumerate(pattern):
        out = jnp.where(sub == row, parts[part], out)
    return out


def squared(pos):
    return pos[0] * pos[0] + pos[1] * pos[1] + pos[2] * pos[2]


def assemble(parts, pos, mixed):
    sub, second, _, _, _ = rows_of()
    g = pos[0] * parts[0] + pos[1] * parts[1] + pos[2] * parts[2] - parts[3]
    s0 = jnp.broadcast_to(g[6:7], (8, TILE))
    s1 = jnp.broadcast_to(g[7:8], (8, TILE))
    s = jnp.where(second, s1, s0)
    return mixed * s - g


def kernel(starts_ref, homes_ref, remotes_ref, x_ref, out_ref, geo_ref, dip_ref, acc_ref):
    eye = (
        lax.broadcasted_iota(jnp.int32, (TILE, TILE), 0) == lax.broadcasted_iota(jnp.int32, (TILE, TILE), 1)
    )
    eye16 = jnp.where(eye, 1.0, 0.0).astype(BF16)
    zero8 = jnp.zeros((8, TILE), F32)
    own_base = 4 * ROWS

    def clear(i, _):
        out_ref[pl.ds(pl.multiple_of(i * 64, 64), 64), :] = jnp.zeros((64, TILE), F32)
        return 0

    lax.fori_loop(0, out_ref.shape[0] // 64, clear, 0)

    def prepare(t, _):
        centre = (8.0, 8.0, (4 * t + 2).astype(F32))
        mu, pos, pol, mixed, own = site_vectors(x_ref, own_base + t, centre)
        dip_ref[t] = dipole_rows(mu, pos, mixed, own)
        hi, mid, lo = geometry_rows([-2.0 * p for p in pos], 1.0, squared(pos))
        scale = (-thole) * lax.rsqrt(pol)
        q = scale_rows(scale, (0, 1, 0, 1, 0, 2))
        stack = jnp.concatenate([hi, mid, hi, mid, hi, lo, q, zero8], 0).astype(BF16)
        geo_ref[t] = lax.dot_general(
            eye16, stack, (((1,), (1,)), ((), ())), preferred_element_type=F32
        ).astype(BF16)
        acc_ref[t] = jnp.zeros((32, TILE), F32)
        return 0

    lax.fori_loop(0, TILES, prepare, 0)

    def pair(home, remote_base, shift, self_flag):
        centre = (8.0 - shift[0], 8.0 - shift[1], (4 * home + 2).astype(F32))
        mu, pos, pol, mixed, own = site_vectors(x_ref, remote_base, centre)
        hi, mid, lo = geometry_rows(pos, squared(pos), 1.0)
        q = scale_rows(lax.rsqrt(pol), (0, 0, 1, 1, 2, 0))
        left = jnp.concatenate([hi, hi, mid, mid, lo, hi, zero8, zero8], 0).astype(BF16)
        right = jnp.concatenate([jnp.zeros((48, TILE), F32), q, zero8], 0).astype(BF16)
        both = jnp.dot(
            geo_ref[home], jnp.concatenate([left, right], 1), preferred_element_type=F32
        )
        dist_sq = both[:, :TILE]
        if self_flag is not None:
            mask = jnp.where(eye, self_flag, 0.0)
            dist_sq = jnp.where(mask > 0.5, 1.0, dist_sq)
        inv = lax.rsqrt(dist_sq)
        inv_sq = inv * inv
        inv_cube = inv_sq * inv
        cube = dist_sq * inv * dist_sq
        damp = cube * both[:, TILE:]
        decay = jnp.exp(damp)
        lam_three = 1.0 - decay
        lam_five = lam_three + damp * decay
        three = lam_three * inv_cube
        five = lam_five * inv_cube * inv_sq
        if self_flag is not None:
            three = three * (1.0 - mask)
            five = five * (1.0 - mask)
        three_hi = three.astype(BF16)
        three_lo = (three - three_hi.astype(F32)).astype(BF16)
        five_hi = five.astype(BF16)
        five_lo = (five - five_hi.astype(F32)).astype(BF16)
        rem = dipole_rows(mu, pos, mixed, own)
        nt = (((1,), (1,)), ((), ()))
        square = jnp.concatenate(
            [jnp.concatenate([five_hi, three_hi], 1), jnp.concatenate([five_lo, three_lo], 1)], 0
        )
        h1 = lax.dot_general(rem, square, nt, preferred_element_type=F32)
        home_dip = dip_ref[home]
        square = jnp.concatenate(
            [jnp.concatenate([five_hi, five_lo], 1), jnp.concatenate([three_hi, three_lo], 1)], 0
        )
        r1 = jnp.dot(home_dip, square, preferred_element_type=F32)
        h = h1[0:32, :TILE] + (h1[32:64, :TILE] + h1[0:32, TILE:]) + (h1[64:96, :TILE] + h1[32:64, TILE:])
        r = r1[0:32, :TILE] + (r1[32:64, :TILE] + r1[0:32, TILE:]) + (r1[64:96, :TILE] + r1[32:64, TILE:])
        field = assemble([r[8 * j:8 * j + 8] for j in range(4)], pos, mixed)
        if self_flag is not None:
            field = field * (1.0 - self_flag)
        return h, field

    for g in range(9):
        shift = (domain_edge * (g // 3 - 1), domain_edge * (g % 3 - 1))
        first = starts_ref[2 * g]
        last = starts_ref[2 * g + 1]

        def step(i, _, g=g, shift=shift, first=first, last=last):
            todo = []
            for k in range(UNROLL):
                p = first + i * UNROLL + k
                live = p < last
                slot = jnp.minimum(p, last - 1)
                home = homes_ref[g, slot]
                remote = remotes_ref[g, slot]
                flag = None
                if g == 4:
                    flag = (home == remote).astype(F32)
                h, field = pair(home, g * ROWS + remote, shift, flag)
                todo.append((jnp.where(live, home, TILES), jnp.where(live, remote, TILES), h, field))
            for home, remote, h, field in todo:
                acc_ref[home] += h
                at = pl.ds(g * OUT_ROWS + remote, 8, stride=OUT_STRIDE)
                out_ref[at, :] += field
            return 0

        lax.fori_loop(0, (last - first + UNROLL - 1) // UNROLL, step, 0)

    def finish(t, _):
        centre = (8.0, 8.0, (4 * t + 2).astype(F32))
        mu, pos, pol, mixed, own = site_vectors(x_ref, own_base + t, centre)
        field = assemble([acc_ref[t, 8 * j:8 * j + 8] for j in range(4)], pos, mixed)
        at = pl.ds(4 * OUT_ROWS + t, 8, stride=OUT_STRIDE)
        out_ref[at, :] += field
        return 0

    lax.fori_loop(0, TILES, finish, 0)


OUT_STRIDE = TILES + 8
OUT_ROWS = 8 * OUT_STRIDE


def field_kernel(starts, homes, remotes, x):
    smem = pl.BlockSpec(memory_space=pltpu.SMEM)
    vmem = pl.BlockSpec(memory_space=pltpu.VMEM)
    return pl.pallas_call(
        kernel,
        out_shape=jax.ShapeDtypeStruct((9 * OUT_ROWS, TILE), F32),
        in_specs=[smem, smem, smem, vmem],
        out_specs=vmem,
        scratch_shapes=[
            pltpu.VMEM((TILES, TILE, 64), BF16),
            pltpu.VMEM((TILES, 96, 2 * TILE), BF16),
            pltpu.VMEM((TILES + 1, 32, TILE), F32),
        ],
        compiler_params=pltpu.CompilerParams(vmem_limit_bytes=60 * 1024 * 1024),
        name="pair_fields",
    )(starts, homes, remotes, x)


def around(value, axis):
    count = lax.axis_size(axis)
    forward = [(i, (i + 1) % count) for i in range(count)]
    backward = [((i + 1) % count, i) for i in range(count)]
    return [lax.ppermute(value, axis, forward), value, lax.ppermute(value, axis, backward)]


def shifted(value, axis, steps):
    count = lax.axis_size(axis)
    pairs = [(source, (source + steps) % count) for source in range(count)]
    return lax.ppermute(value, axis, pairs)


def local(positions, polarity, dipoles, perm_fields, pair_list, tile_counts):
    slot_total = pair_list.shape[3]
    sites = jnp.concatenate([dipoles, positions, polarity[None]], 0).reshape(1, 10 * TILES, TILE)
    rows = jnp.concatenate(around(sites, "gx"), 0)[:, None]
    halo = jnp.concatenate(around(rows, "gy"), 1).reshape(9 * ROWS, TILE)

    table = pair_list.reshape(2, slot_total)
    live = jnp.arange(slot_total, dtype=jnp.int32) < tile_counts.reshape(())
    far = jnp.where(live, table[1], 16 * TILES)
    far, near = lax.sort((far, table[0]), num_keys=1)
    bounds = jnp.arange(slot_total, dtype=jnp.int32)[:16] * TILES
    bounds = jnp.sum((far[None, :] < bounds[:, None]).astype(jnp.int32), 1)
    bounds = jnp.concatenate([bounds, jnp.zeros((slot_total - 16,), jnp.int32)])
    lists = jnp.stack([far, near, bounds])[None]
    lists = jnp.concatenate(around(lists, "gx"), 0)[:, None]
    lists = jnp.concatenate(around(lists, "gy"), 1).reshape(9, 3, slot_total)
    starts = []
    for g in range(9):
        starts += [lists[g, 2, 8 - g], lists[g, 2, 9 - g]]
    homes = lists[:, 0] & (TILES - 1)
    remotes = lists[:, 1]

    terms = field_kernel(jnp.stack(starts), homes, remotes, halo)
    terms = terms.reshape(3, 3, 8, OUT_STRIDE, TILE)[:, :, :6, :TILES]
    column = terms[:, 1] + shifted(terms[:, 0], "gy", -1) + shifted(terms[:, 2], "gy", 1)
    field = column[1] + shifted(column[0], "gx", -1) + shifted(column[2], "gx", 1)
    field = field.reshape(6, 1, 1, TILES * TILE)
    induced = polarity[None] * (perm_fields + field)
    return (field, induced)


def solution(mesh):
    placed = (
        P(None, "gx", "gy", None),
        P("gx", "gy", None),
        P(None, "gx", "gy", None),
        P(None, "gx", "gy", None),
        P("gx", "gy", None, None),
        P("gx", "gy"),
    )
    return jax.shard_map(
        local,
        mesh=mesh,
        in_specs=placed,
        out_specs=(P(None, "gx", "gy", None), P(None, "gx", "gy", None)),
        check_vma=False,
    )
```

time: 1600 us -> 482 us (0.30)
  the two profiles are of different devices: /device:TPU:4 before, /device:TPU:28 now
where the time goes in v1:
time: 482 us
  Pallas kernels  256 us (53%)
  waiting for transfers between devices  110 us (23%)
  starting transfers between devices  74 us (15%)
  other arithmetic  24.7 us (5%)
  local copies, waits for them, and re-layouts  15.7 us (3%)
    pallas_call x1, Pallas kernels, field_kernel(): pl.pallas_call(kernel, out_shape=jax.ShapeDtypeStruct((9 * OUT_ROWS, TILE...  256 us
    ppermute x4, starting transfers between devices, shifted(): return lax.ppermute(value, axis, pairs)  66.5 us
    ppermute x4, waiting for transfers between devices, around(): lax.ppermute(value, axis, backward)  61 us
    ppermute x4, waiting for transfers between devices, shifted(): return lax.ppermute(value, axis, pairs)  40.4 us
    another operation x1, local copies, waits for them, and re-layouts, local(): terms = field_kernel(jnp.stack(starts), homes, remotes, halo)  11.9 us
    concatenate x1, other arithmetic, local(): halo = jnp.concatenate(around(rows, 'gy'), 1).reshape(9 * ROWS, TILE)  9.71 us
  transfers between devices with their start and end apart: 12, of which 10 were waited for; matrix products, arithmetic and copies ran while one was open for 4% of the time, Pallas kernels for 0%

profile of v1, /device:TPU:28, one launch (start us, length us, event | category | flops | bytes accessed | tf_op | source)
XLA Modules:
  0.0 482.0 jit_solution(4294595098257317752)
XLA Ops:
  0.6 2.5 pad_maximum_fusion.1
  3.1 0.0 copy-start.3
  3.1 4.3 collective-permute-start.5
  7.4 0.0 collective-permute-start.4
  7.4 28.0 %collective-permute-done.5 = f32[1,2560,128]{2,1,0:T(8,128)S(1)} collective-permute-done((f32[1,2560,128]{2,1,0:T(8,128)S(1)}, f32[1,2560,128]{2,1,0:T(8,128)S(1)}, u32[]{:S(2)}, u32[]{:S(2)}) %collective-permute-start.5) | collective-permute-done | bytes 1310752 | tf_op jit(solution)/shard_map/ppermute | solution.py:234
  35.4 4.3 collective-permute-done.4
  39.8 2.3 maximum_bitcast_fusion
  42.1 0.0 collective-permute-start.7
  42.1 0.5 collective-permute-start.6
  43.3 0.0 copy-done.3
  43.3 5.1 %sort.23 = (s32[2048]{0:T(1024)S(1)}, s32[2048]{0:T(1024)S(1)}, s32[2048]{0:T(1024)}) sort(s32[2048]{0:T(1024)S(1)} %fusion.5, s32[2048]{0:T(1024)S(1)} %bitcast.80, s32[2048]{0:T(1024)S(1)} %iota.10), dimensions={0}, to_apply=%region_0.1 | sort | flops 22528 | bytes 49152 | tf_op jit(solution)/shard_map/sort | solution.py:252
  48.5 0.2 convert_reduce_fusion
  48.7 0.4 collective-permute-start.1
  49.1 1.7 collective-permute-start
  50.8 2.1 collective-permute-done.1
  52.9 2.2 collective-permute-done
  55.1 0.5 collective-permute-start.3
  55.6 0.1 collective-permute-start.2
  55.7 30.9 %collective-permute-done.3 = s32[3,1,3,2048]{3,2,1,0:T(4,128)S(1)} collective-permute-done((s32[3,1,3,2048]{3,2,1,0:T(4,128)S(1)}, s32[3,1,3,2048]{3,2,1,0:T(4,128)S(1)}, u32[]{:S(2)}, u32[]{:S(2)}) %collective-permute-start.3) | collective-permute-done | bytes 73760 | tf_op jit(solution)/shard_map/ppermute | solution.py:234
  86.6 1.9 collective-permute-done.2
  88.5 0.1 pad_add_fusion
  88.6 0.7 fusion.7
  89.3 11.9 %stack.19.starts_ref = s32[18]{0:T(128)} concatenate(s32[1]{0:T(128)} %bitcast.9, s32[1]{0:T(128)} %bitcast.10, s32[1]{0:T(128)} %bitcast.11, s32[1]{0:T(128)} %bitcast.12, s32[1]{0:T(128)} %bitcast.13, s32[1]{0:T(128)} %bitcast.14, s32[1]{0:T(128)} %bitcast.15, s32[1]{0:T(128)} %bitcast.16, s32[1]{0:T(128)} %bitcast.17, s32[1]{0:T(128)} %bitcast.18, s32[1]{0:T(128)} %bitcast.19, ...), dimensions={0} | concatenate | bytes 144 | tf_op jit(solution)/shard_map/stack | solution.py:265
  101.1 0.1 fusion.6
  101.3 0.8 copy_bitcast_fusion
  102.0 0.0 collective-permute-done.7
  102.0 0.0 collective-permute-done.6
  102.0 9.7 %pad_maximum_fusion = f32[3,3,2560,128]{3,2,1,0:T(8,128)} fusion(f32[3,1,2560,128]{3,2,1,0:T(8,128)} %collective-permute-done.7, f32[3,1,2560,128]{3,2,1,0:T(8,128)} %maximum_bitcast_fusion, f32[3,1,2560,128]{3,2,1,0:T(8,128)} %collective-permute-done.6), kind=kLoop, calls=%fused_computation | loop fusion | flops 5898240 | bytes 23592960 | tf_op jit(solution)/shard_map/concatenate | solution.py:247
  111.7 256.3 %pair_fields.1 = f32[19008,128]{1,0:T(8,128)} custom-call(s32[18]{0:T(128)} %stack.19.starts_ref, s32[9,2048]{1,0:T(8,128)} %get-tuple-element.35.homes_ref, s32[9,2048]{1,0:T(8,128)} %get-tuple-element.34.remotes_ref, f32[23040,128]{1,0:T(8,128)} %bitcast.66), custom_call_target="tpu_custom_call" | custom-call | tf_op jit(solution)/shard_map/pair_fields/pallas_call | solution.py:215
  368.0 2.9 slice_bitcast_fusion.1
  370.9 64.4 %collective-permute-start.8 = (f32[3,6,256,128]{3,2,1,0:T(8,128)S(1)}, f32[3,6,256,128]{3,2,1,0:T(8,128)S(1)}, u32[]{:S(2)}, u32[]{:S(2)}) collective-permute-start(f32[3,6,256,128]{3,2,1,0:T(8,128)S(1)} %get-tuple-element.8), channel_id=1, source_target_pairs={{0,15},{1,0},{2,1},{3,2},{4,3},{5,4},{6,5},{7,6},{8,7},{9,8},{10,9... | collective-permute-start | bytes 7077896 | tf_op jit(solution)/shard_map/ppermute | solution.py:240
  435.3 0.0 collective-permute-start.9
  435.3 26.4 %collective-permute-done.8 = f32[3,6,256,128]{3,2,1,0:T(8,128)S(1)} collective-permute-done((f32[3,6,256,128]{3,2,1,0:T(8,128)S(1)}, f32[3,6,256,128]{3,2,1,0:T(8,128)S(1)}, u32[]{:S(2)}, u32[]{:S(2)}) %collective-permute-start.8) | collective-permute-done | bytes 2359328 | tf_op jit(solution)/shard_map/ppermute | solution.py:240
  461.7 1.9 collective-permute-done.9
  463.6 2.1 fusion.1
  465.7 0.1 slice_bitcast_fusion.4
  465.8 0.0 copy-start.1
  465.8 0.0 copy-start.2
  465.8 0.1 collective-permute-start.10
  465.9 2.0 collective-permute-start.11
  467.9 10.0 %collective-permute-done.10 = f32[6,256,128]{2,1,0:T(8,128)S(1)} collective-permute-done((f32[6,256,128]{2,1,0:T(8,128)S(1)}, f32[6,256,128]{2,1,0:T(8,128)S(1)}, u32[]{:S(2)}, u32[]{:S(2)}) %collective-permute-start.10) | collective-permute-done | bytes 786464 | tf_op jit(solution)/shard_map/ppermute | solution.py:240
  477.9 2.2 collective-permute-done.11
  480.1 0.2 fusion.3
  480.2 0.0 copy-start
  480.2 0.0 copy-done.1
  480.2 0.0 copy-done.2
  480.3 1.7 add_multiply_fusion
  482.0 0.0 copy-done
  (7 shorter events, 0.1 us)
Async XLA Ops:
  3.1 40.2 %copy-start.3 = (s32[1,1,2,2048]{3,2,1,0:T(2,128)S(1)}, s32[1,1,2,2048]{3,2,1,0:T(2,128)}, u32[]{:S(2)}) copy-start(s32[1,1,2,2048]{3,2,1,0:T(2,128)} %param.10) | copy-start | bytes 49156
  3.1 32.3 %collective-permute-start.5 = (f32[1,2560,128]{2,1,0:T(8,128)S(1)}, f32[1,2560,128]{2,1,0:T(8,128)S(1)}, u32[]{:S(2)}, u32[]{:S(2)}) collective-permute-start(f32[1,2560,128]{2,1,0:T(8,128)S(1)} %bitcast.69), channel_id=1, source_target_pairs={{16,0},{32,16},{48,32},{64,48},{80,64},{96,80},{112,96},{0,112},{1... | collective-permute-start | bytes 3932168 | tf_op jit(solution)/shard_map/ppermute | solution.py:234
  7.4 32.3 %collective-permute-start.4 = (f32[1,2560,128]{2,1,0:T(8,128)S(1)}, f32[1,2560,128]{2,1,0:T(8,128)S(1)}, u32[]{:S(2)}, u32[]{:S(2)}) collective-permute-start(f32[1,2560,128]{2,1,0:T(8,128)S(1)} %bitcast.70), channel_id=1, source_target_pairs={{0,16},{16,32},{32,48},{48,64},{64,80},{80,96},{96,112},{112,0},{1... | collective-permute-start | bytes 3932168 | tf_op jit(solution)/shard_map/ppermute | solution.py:234
  42.1 59.9 %collective-permute-start.7 = (f32[3,1,2560,128]{3,2,1,0:T(8,128)}, f32[3,1,2560,128]{3,2,1,0:T(8,128)}, u32[]{:S(2)}, u32[]{:S(2)}) collective-permute-start(f32[3,1,2560,128]{3,2,1,0:T(8,128)} %maximum_bitcast_fusion), channel_id=1, source_target_pairs={{1,0},{2,1},{3,2},{4,3},{5,4},{6,5},{7,6},{8,7},{9,8},{10,9},{11,1... | collective-permute-start | bytes 11796488 | tf_op jit(solution)/shard_map/ppermute | solution.py:234
  42.1 59.9 %collective-permute-start.6 = (f32[3,1,2560,128]{3,2,1,0:T(8,128)}, f32[3,1,2560,128]{3,2,1,0:T(8,128)}, u32[]{:S(2)}, u32[]{:S(2)}) collective-permute-start(f32[3,1,2560,128]{3,2,1,0:T(8,128)} %maximum_bitcast_fusion), channel_id=1, source_target_pairs={{0,1},{1,2},{2,3},{3,4},{4,5},{5,6},{6,7},{7,8},{8,9},{9,10},{10,1... | collective-permute-start | bytes 11796488 | tf_op jit(solution)/shard_map/ppermute | solution.py:234
  48.7 4.2 collective-permute-start.1
  49.1 6.0 %collective-permute-start = (s32[1,3,2048]{2,1,0:T(4,128)S(1)}, s32[1,3,2048]{2,1,0:T(4,128)S(1)}, u32[]{:S(2)}, u32[]{:S(2)}) collective-permute-start(s32[1,3,2048]{2,1,0:T(4,128)S(1)} %add_bitcast_fusion.1), channel_id=1, source_target_pairs={{0,16},{16,32},{32,48},{48,64},{64,80},{80,96},{96,112},{112,0},{1... | collective-permute-start | bytes 73736 | tf_op jit(solution)/shard_map/ppermute | solution.py:234
  55.1 31.5 %collective-permute-start.3 = (s32[3,1,3,2048]{3,2,1,0:T(4,128)S(1)}, s32[3,1,3,2048]{3,2,1,0:T(4,128)S(1)}, u32[]{:S(2)}, u32[]{:S(2)}) collective-permute-start(s32[3,1,3,2048]{3,2,1,0:T(4,128)S(1)} %add_bitcast_fusion), channel_id=1, source_target_pairs={{1,0},{2,1},{3,2},{4,3},{5,4},{6,5},{7,6},{8,7},{9,8},{10,9},{11,1... | collective-permute-start | bytes 221192 | tf_op jit(solution)/shard_map/ppermute | solution.py:234
  55.6 32.9 %collective-permute-start.2 = (s32[3,1,3,2048]{3,2,1,0:T(4,128)S(1)}, s32[3,1,3,2048]{3,2,1,0:T(4,128)S(1)}, u32[]{:S(2)}, u32[]{:S(2)}) collective-permute-start(s32[3,1,3,2048]{3,2,1,0:T(4,128)S(1)} %add_bitcast_fusion), channel_id=1, source_target_pairs={{0,1},{1,2},{2,3},{3,4},{4,5},{5,6},{6,7},{7,8},{8,9},{9,10},{10,1... | collective-permute-start | bytes 221192 | tf_op jit(solution)/shard_map/ppermute | solution.py:234
  370.9 90.8 %collective-permute-start.8 = (f32[3,6,256,128]{3,2,1,0:T(8,128)S(1)}, f32[3,6,256,128]{3,2,1,0:T(8,128)S(1)}, u32[]{:S(2)}, u32[]{:S(2)}) collective-permute-start(f32[3,6,256,128]{3,2,1,0:T(8,128)S(1)} %get-tuple-element.8), channel_id=1, source_target_pairs={{0,15},{1,0},{2,1},{3,2},{4,3},{5,4},{6,5},{7,6},{8,7},{9,8},{10,9... | collective-permute-start | bytes 7077896 | tf_op jit(solution)/shard_map/ppermute | solution.py:240
  435.3 28.3 %collective-permute-start.9 = (f32[3,6,256,128]{3,2,1,0:T(8,128)S(1)}, f32[3,6,256,128]{3,2,1,0:T(8,128)S(1)}, u32[]{:S(2)}, u32[]{:S(2)}) collective-permute-start(f32[3,6,256,128]{3,2,1,0:T(8,128)S(1)} %get-tuple-element.9), channel_id=1, source_target_pairs={{0,1},{1,2},{2,3},{3,4},{4,5},{5,6},{6,7},{7,8},{8,9},{9,10},{10,1... | collective-permute-start | bytes 7077896 | tf_op jit(solution)/shard_map/ppermute | solution.py:240
  465.8 14.5 %copy-start.1 = (f32[6,1,1,32768]{3,2,1,0:T(1,128)S(1)}, f32[6,1,1,32768]{3,2,1,0:T(1,128)}, u32[]{:S(2)}) copy-start(f32[6,1,1,32768]{3,2,1,0:T(1,128)} %param.9) | copy-start | bytes 2359300
  465.8 14.5 %copy-start.2 = (f32[1,1,32768]{2,1,0:T(1,128)S(1)}, f32[1,1,32768]{2,1,0:T(1,128)}, u32[]{:S(2)}) copy-start(f32[1,1,32768]{2,1,0:T(1,128)} %param.7) | copy-start | bytes 393220
  465.8 12.1 %collective-permute-start.10 = (f32[6,256,128]{2,1,0:T(8,128)S(1)}, f32[6,256,128]{2,1,0:T(8,128)S(1)}, u32[]{:S(2)}, u32[]{:S(2)}) collective-permute-start(f32[6,256,128]{2,1,0:T(8,128)S(1)} %get-tuple-element.10), channel_id=1, source_target_pairs={{0,112},{16,0},{32,16},{48,32},{64,48},{80,64},{96,80},{112,96},{1... | collective-permute-start | bytes 2359304 | tf_op jit(solution)/shard_map/ppermute | solution.py:240
  465.9 14.2 %collective-permute-start.11 = (f32[6,256,128]{2,1,0:T(8,128)S(1)}, f32[6,256,128]{2,1,0:T(8,128)S(1)}, u32[]{:S(2)}, u32[]{:S(2)}) collective-permute-start(f32[6,256,128]{2,1,0:T(8,128)S(1)} %get-tuple-element.11), channel_id=1, source_target_pairs={{0,16},{16,32},{32,48},{48,64},{64,80},{80,96},{96,112},{112,0},{1... | collective-permute-start | bytes 2359304 | tf_op jit(solution)/shard_map/ppermute | solution.py:240
  480.2 1.8 copy-start

commit v2 on v1

--- a/solution.py
+++ b/solution.py
@@ -9,6 +9,8 @@
 TILES = 256
 ROWS = 10 * TILES
 UNROLL = 4
+PARTS = 3
+DUMMY = TILES
 
 thole = 0.39
 domain_edge = 16.0
@@ -58,7 +60,7 @@
     out = []
     for l, r in zip(three_parts(left), three_parts(right)):
         out.append(jnp.concatenate([l, jnp.concatenate([blank, r], 0)], 1))
-    return jnp.concatenate(out, 0)
+    return jnp.concatenate(out[:PARTS], 0)
 
 
 def geometry_rows(first_three, fourth, fifth):
@@ -89,19 +91,35 @@
     return mixed * s - g
 
 
-def kernel(starts_ref, homes_ref, remotes_ref, x_ref, out_ref, geo_ref, dip_ref, acc_ref):
+def kernel(
+    lists_ref, low_ref, mid_ref, high_ref, out_ref,
+    copy_sem, x_ref, geo_ref, dip_ref, acc_ref, eye_ref, near_ref, far_ref, dist_ref, coef_ref,
+):
     eye = (
         lax.broadcasted_iota(jnp.int32, (TILE, TILE), 0) == lax.broadcasted_iota(jnp.int32, (TILE, TILE), 1)
     )
     eye16 = jnp.where(eye, 1.0, 0.0).astype(BF16)
     zero8 = jnp.zeros((8, TILE), F32)
     own_base = 4 * ROWS
+    copies = []
+    for column, source in enumerate((low_ref, mid_ref, high_ref)):
+        for row in range(3):
+            place = x_ref.at[pl.ds((3 * row + column) * ROWS, ROWS), :]
+            copies.append(pltpu.make_async_copy(source.at[row], place, copy_sem.at[3 * row + column]))
+            copies[-1].start()
+    nt = (((1,), (1,)), ((), ()))
+    eye_ref[0] = jnp.zeros((TILE, 2 * TILE), BF16)
+    eye_ref[1] = jnp.concatenate(
+        [jnp.where(eye, FAR_AWAY, 0.0).astype(BF16), jnp.zeros((TILE, TILE), BF16)], 1
+    )
 
     def clear(i, _):
         out_ref[pl.ds(pl.multiple_of(i * 64, 64), 64), :] = jnp.zeros((64, TILE), F32)
         return 0
 
     lax.fori_loop(0, out_ref.shape[0] // 64, clear, 0)
+    for copy in copies:
+        copy.wait()
 
     def prepare(t, _):
         centre = (8.0, 8.0, (4 * t + 2).astype(F32))
@@ -111,120 +129,160 @@
         scale = (-thole) * lax.rsqrt(pol)
         q = scale_rows(scale, (0, 1, 0, 1, 0, 2))
         stack = jnp.concatenate([hi, mid, hi, mid, hi, lo, q, zero8], 0).astype(BF16)
-        geo_ref[t] = lax.dot_general(
-            eye16, stack, (((1,), (1,)), ((), ())), preferred_element_type=F32
-        ).astype(BF16)
+        moved = lax.dot_general(eye16, stack, nt, preferred_element_type=F32).astype(BF16)
+        geo_ref[t] = jnp.concatenate([moved, eye16], 1)
         acc_ref[t] = jnp.zeros((32, TILE), F32)
         return 0
 
-    lax.fori_loop(0, TILES, prepare, 0)
-
-    def pair(home, remote_base, shift, self_flag):
-        centre = (8.0 - shift[0], 8.0 - shift[1], (4 * home + 2).astype(F32))
-        mu, pos, pol, mixed, own = site_vectors(x_ref, remote_base, centre)
+    lax.fori_loop(0, TILES, prepare, 0, unroll=4)
+    geo_ref[DUMMY] = geo_ref[0]
+    dip_ref[DUMMY] = dip_ref[0]
+
+    def blank(first):
+        for k in range(first[1]):
+            near_ref[first[0] + k] = DUMMY
+            far_ref[first[0] + k] = 4 * TILES
+
+    blank((0, 2 * UNROLL))
+    total = jnp.int32(2 * UNROLL)
+    for g in range(9):
+        first = lists_ref[3 * g + 2, 8 - g]
+        last = lists_ref[3 * g + 2, 9 - g]
+
+        def place(p, at, g=g):
+            near_ref[at] = lists_ref[3 * g, p] & (TILES - 1)
+            far_ref[at] = lists_ref[3 * g + 1, p] + g * TILES
+            return at + 1
+
+        total = lax.fori_loop(first, last, place, total)
+    blank((total, 3 * UNROLL))
+    groups = (total - 2 * UNROLL + UNROLL - 1) // UNROLL
+
+    def origin(home, far):
+        grid = far // TILES
+        row = (grid * 11) // 32
+        column = grid - 3 * row
+        return (
+            8.0 - domain_edge * (row - 1).astype(F32),
+            8.0 - domain_edge * (column - 1).astype(F32),
+            (4 * home + 2).astype(F32),
+        )
+
+    def distances(u, at):
+        home = near_ref[at]
+        far = far_ref[at]
+        grid = far // TILES
+        base = grid * ROWS + (far - grid * TILES)
+        pos = [load_row(x_ref, base + (6 + k) * TILES) - c for k, c in enumerate(origin(home, far))]
+        pol = load_row(x_ref, base + 9 * TILES)
         hi, mid, lo = geometry_rows(pos, squared(pos), 1.0)
         q = scale_rows(lax.rsqrt(pol), (0, 0, 1, 1, 2, 0))
         left = jnp.concatenate([hi, hi, mid, mid, lo, hi, zero8, zero8], 0).astype(BF16)
         right = jnp.concatenate([jnp.zeros((48, TILE), F32), q, zero8], 0).astype(BF16)
-        both = jnp.dot(
-            geo_ref[home], jnp.concatenate([left, right], 1), preferred_element_type=F32
-        )
-        dist_sq = both[:, :TILE]
-        if self_flag is not None:
-            mask = jnp.where(eye, self_flag, 0.0)
-            dist_sq = jnp.where(mask > 0.5, 1.0, dist_sq)
+        same = (far == 4 * TILES + home).astype(jnp.int32)
+        operand = jnp.concatenate([jnp.concatenate([left, right], 1), eye_ref[same]], 0)
+        dist_ref[u] = jnp.dot(geo_ref[home], operand, preferred_element_type=F32)
+
+    def coefficients(u):
+        dist_sq = dist_ref[u, :, :TILE]
         inv = lax.rsqrt(dist_sq)
         inv_sq = inv * inv
         inv_cube = inv_sq * inv
         cube = dist_sq * inv * dist_sq
-        damp = cube * both[:, TILE:]
+        damp = cube * dist_ref[u, :, TILE:]
         decay = jnp.exp(damp)
         lam_three = 1.0 - decay
         lam_five = lam_three + damp * decay
         three = lam_three * inv_cube
         five = lam_five * inv_cube * inv_sq
-        if self_flag is not None:
-            three = three * (1.0 - mask)
-            five = five * (1.0 - mask)
         three_hi = three.astype(BF16)
-        three_lo = (three - three_hi.astype(F32)).astype(BF16)
         five_hi = five.astype(BF16)
-        five_lo = (five - five_hi.astype(F32)).astype(BF16)
+        coef_ref[u, 0] = five_hi
+        coef_ref[u, 1] = (five - five_hi.astype(F32)).astype(BF16)
+        coef_ref[u, 2] = three_hi
+        coef_ref[u, 3] = (three - three_hi.astype(F32)).astype(BF16)
+
+    def folded(sums):
+        total = sums[0:32, :TILE]
+        for k in range(1, PARTS):
+            total = total + (sums[32 * k:32 * k + 32, :TILE] + sums[32 * k - 32:32 * k, TILE:])
+        return total
+
+    def sums(u, at):
+        home = near_ref[at]
+        far = far_ref[at]
+        grid = far // TILES
+        remote = far - grid * TILES
+        mu, pos, pol, mixed, own = site_vectors(x_ref, grid * ROWS + remote, origin(home, far))
         rem = dipole_rows(mu, pos, mixed, own)
-        nt = (((1,), (1,)), ((), ()))
+        five_hi, five_lo, three_hi, three_lo = [coef_ref[u, k] for k in range(4)]
         square = jnp.concatenate(
             [jnp.concatenate([five_hi, three_hi], 1), jnp.concatenate([five_lo, three_lo], 1)], 0
         )
-        h1 = lax.dot_general(rem, square, nt, preferred_element_type=F32)
-        home_dip = dip_ref[home]
+        h = folded(lax.dot_general(rem, square, nt, preferred_element_type=F32))
         square = jnp.concatenate(
             [jnp.concatenate([five_hi, five_lo], 1), jnp.concatenate([three_hi, three_lo], 1)], 0
         )
-        r1 = jnp.dot(home_dip, square, preferred_element_type=F32)
-        h = h1[0:32, :TILE] + (h1[32:64, :TILE] + h1[0:32, TILE:]) + (h1[64:96, :TILE] + h1[32:64, TILE:])
-        r = r1[0:32, :TILE] + (r1[32:64, :TILE] + r1[0:32, TILE:]) + (r1[64:96, :TILE] + r1[32:64, TILE:])
+        r = folded(jnp.dot(dip_ref[home], square, preferred_element_type=F32))
         field = assemble([r[8 * j:8 * j + 8] for j in range(4)], pos, mixed)
-        if self_flag is not None:
-            field = field * (1.0 - self_flag)
-        return h, field
-
-    for g in range(9):
-        shift = (domain_edge * (g // 3 - 1), domain_edge * (g % 3 - 1))
-        first = starts_ref[2 * g]
-        last = starts_ref[2 * g + 1]
-
-        def step(i, _, g=g, shift=shift, first=first, last=last):
-            todo = []
-            for k in range(UNROLL):
-                p = first + i * UNROLL + k
-                live = p < last
-                slot = jnp.minimum(p, last - 1)
-                home = homes_ref[g, slot]
-                remote = remotes_ref[g, slot]
-                flag = None
-                if g == 4:
-                    flag = (home == remote).astype(F32)
-                h, field = pair(home, g * ROWS + remote, shift, flag)
-                todo.append((jnp.where(live, home, TILES), jnp.where(live, remote, TILES), h, field))
-            for home, remote, h, field in todo:
-                acc_ref[home] += h
-                at = pl.ds(g * OUT_ROWS + remote, 8, stride=OUT_STRIDE)
-                out_ref[at, :] += field
-            return 0
-
-        lax.fori_loop(0, (last - first + UNROLL - 1) // UNROLL, step, 0)
+        unused = (home == DUMMY) | (far == 4 * TILES + home)
+        target = jnp.where(unused, 4 * OUT_ROWS + DUMMY, grid * OUT_ROWS + remote)
+        return home, target, h, field
+
+    def step(i, _):
+        first = i * UNROLL
+        done = [sums(u, first + u) for u in range(UNROLL)]
+        for u in range(UNROLL):
+            coefficients(u)
+        for u in range(UNROLL):
+            distances(u, first + 2 * UNROLL + u)
+        for home, target, h, field in done:
+            acc_ref[home] += h
+            out_ref[pl.ds(target, 8, stride=OUT_STRIDE), :] += field
+        return 0
+
+    lax.fori_loop(0, groups + 2, step, 0)
 
     def finish(t, _):
         centre = (8.0, 8.0, (4 * t + 2).astype(F32))
         mu, pos, pol, mixed, own = site_vectors(x_ref, own_base + t, centre)
         field = assemble([acc_ref[t, 8 * j:8 * j + 8] for j in range(4)], pos, mixed)
-        at = pl.ds(4 * OUT_ROWS + t, 8, stride=OUT_STRIDE)
-        out_ref[at, :] += field
+        out_ref[pl.ds(4 * OUT_ROWS + t, 8, stride=OUT_STRIDE), :] += field
         return 0
 
-    lax.fori_loop(0, TILES, finish, 0)
-
-
+    lax.fori_loop(0, TILES, finish, 0, unroll=4)
+
+
+FAR_AWAY = 2.0 ** 60
+LIST = 9 * 2048 + 5 * UNROLL
 OUT_STRIDE = TILES + 8
 OUT_ROWS = 8 * OUT_STRIDE
 
 
-def field_kernel(starts, homes, remotes, x):
+def field_kernel(lists, low, middle, high):
     smem = pl.BlockSpec(memory_space=pltpu.SMEM)
+    away = pl.BlockSpec(memory_space=pl.ANY)
     vmem = pl.BlockSpec(memory_space=pltpu.VMEM)
     return pl.pallas_call(
         kernel,
         out_shape=jax.ShapeDtypeStruct((9 * OUT_ROWS, TILE), F32),
-        in_specs=[smem, smem, smem, vmem],
+        in_specs=[smem, away, away, away],
         out_specs=vmem,
         scratch_shapes=[
-            pltpu.VMEM((TILES, TILE, 64), BF16),
-            pltpu.VMEM((TILES, 96, 2 * TILE), BF16),
+            pltpu.SemaphoreType.DMA((9,)),
+            pltpu.VMEM((9 * ROWS, TILE), F32),
+            pltpu.VMEM((TILES + 1, TILE, 64 + TILE), BF16),
+            pltpu.VMEM((TILES + 1, 32 * PARTS, 2 * TILE), BF16),
             pltpu.VMEM((TILES + 1, 32, TILE), F32),
+            pltpu.VMEM((2, TILE, 2 * TILE), BF16),
+            pltpu.SMEM((LIST,), jnp.int32),
+            pltpu.SMEM((LIST,), jnp.int32),
+            pltpu.VMEM((UNROLL, TILE, 2 * TILE), F32),
+            pltpu.VMEM((UNROLL, 4, TILE, TILE), BF16),
         ],
-        compiler_params=pltpu.CompilerParams(vmem_limit_bytes=60 * 1024 * 1024),
+        compiler_params=pltpu.CompilerParams(vmem_limit_bytes=63 * 1024 * 1024),
         name="pair_fields",
-    )(starts, homes, remotes, x)
+    )(lists, low, middle, high)
 
 
 def around(value, axis):
@@ -243,8 +301,8 @@
 def local(positions, polarity, dipoles, perm_fields, pair_list, tile_counts):
     slot_total = pair_list.shape[3]
     sites = jnp.concatenate([dipoles, positions, polarity[None]], 0).reshape(1, 10 * TILES, TILE)
-    rows = jnp.concatenate(around(sites, "gx"), 0)[:, None]
-    halo = jnp.concatenate(around(rows, "gy"), 1).reshape(9 * ROWS, TILE)
+    rows = jnp.concatenate(around(sites, "gx"), 0)
+    columns = around(rows, "gy")
 
     table = pair_list.reshape(2, slot_total)
     live = jnp.arange(slot_total, dtype=jnp.int32) < tile_counts.reshape(())
@@ -255,14 +313,8 @@
     bounds = jnp.concatenate([bounds, jnp.zeros((slot_total - 16,), jnp.int32)])
     lists = jnp.stack([far, near, bounds])[None]
     lists = jnp.concatenate(around(lists, "gx"), 0)[:, None]
-    lists = jnp.concatenate(around(lists, "gy"), 1).reshape(9, 3, slot_total)
-    starts = []
-    for g in range(9):
-        starts += [lists[g, 2, 8 - g], lists[g, 2, 9 - g]]
-    homes = lists[:, 0] & (TILES - 1)
-    remotes = lists[:, 1]
-
-    terms = field_kernel(jnp.stack(starts), homes, remotes, halo)
+    lists = jnp.concatenate(around(lists, "gy"), 1).reshape(27, slot_total)
+    terms = field_kernel(lists, *columns)
     terms = terms.reshape(3, 3, 8, OUT_STRIDE, TILE)[:, :, :6, :TILES]
     column = terms[:, 1] + shifted(terms[:, 0], "gy", -1) + shifted(terms[:, 2], "gy", 1)
     field = column[1] + shifted(column[0], "gx", -1) + shifted(column[2], "gx", 1)

time: 482 us -> 319 us (0.66)
  the two profiles are of different devices: /device:TPU:28 before, /device:TPU:2 now
where the time goes in v2:
time: 319 us; the launch traced here: 318 us
  Pallas kernels  131 us (41%)
  waiting for transfers between devices  88.4 us (28%)
  starting transfers between devices  79.2 us (25%)
  other arithmetic  14.3 us (4%)
  local copies, waits for them, and re-layouts  3.86 us (1%)
    pallas_call x1, Pallas kernels, field_kernel(): pl.pallas_call(kernel, out_shape=jax.ShapeDtypeStruct((9 * OUT_ROWS, TILE...  131 us
    ppermute x4, waiting for transfers between devices, shifted(): return lax.ppermute(value, axis, pairs)  47.5 us
    ppermute x4, starting transfers between devices, around(): lax.ppermute(value, axis, backward)  43.2 us
    ppermute x4, starting transfers between devices, shifted(): return lax.ppermute(value, axis, pairs)  33.7 us
    ppermute x4, waiting for transfers between devices, around(): lax.ppermute(value, axis, backward)  32.4 us
    ppermute x4, waiting for transfers between devices, around(): lax.ppermute(value, axis, forward)  8.59 us
  transfers between devices with their start and end apart: 12, of which 10 were waited for; matrix products, arithmetic and copies ran while one was open for 2% of the time, Pallas kernels for 0%

profile of v2, /device:TPU:2, one launch (start us, length us, event | category | flops | bytes accessed | tf_op | source)
XLA Modules:
  0.0 318.3 jit_solution(8536520258643487427)
XLA Ops:
  0.6 2.5 pad_maximum_fusion.1
  3.1 0.0 copy-start.3
  3.1 5.1 %collective-permute-start.5 = (f32[1,2560,128]{2,1,0:T(8,128)S(1)}, f32[1,2560,128]{2,1,0:T(8,128)S(1)}, u32[]{:S(2)}, u32[]{:S(2)}) collective-permute-start(f32[1,2560,128]{2,1,0:T(8,128)S(1)} %bitcast.42), channel_id=1, source_target_pairs={{16,0},{32,16},{48,32},{64,48},{80,64},{96,80},{112,96},{0,112},{1... | collective-permute-start | bytes 3932168 | tf_op jit(solution)/shard_map/ppermute | solution.py:292
  8.2 0.0 collective-permute-start.4
  8.2 28.0 %collective-permute-done.5 = f32[1,2560,128]{2,1,0:T(8,128)S(1)} collective-permute-done((f32[1,2560,128]{2,1,0:T(8,128)S(1)}, f32[1,2560,128]{2,1,0:T(8,128)S(1)}, u32[]{:S(2)}, u32[]{:S(2)}) %collective-permute-start.5) | collective-permute-done | bytes 1310752 | tf_op jit(solution)/shard_map/ppermute | solution.py:292
  36.3 4.3 %collective-permute-done.4 = f32[1,2560,128]{2,1,0:T(8,128)S(1)} collective-permute-done((f32[1,2560,128]{2,1,0:T(8,128)S(1)}, f32[1,2560,128]{2,1,0:T(8,128)S(1)}, u32[]{:S(2)}, u32[]{:S(2)}) %collective-permute-start.4) | collective-permute-done | bytes 1310752 | tf_op jit(solution)/shard_map/ppermute | solution.py:292
  40.6 2.4 pad_maximum_fusion.mid_ref
  43.0 0.0 collective-permute-start.7
  43.0 0.5 collective-permute-start.6
  44.2 0.0 copy-done.3
  44.2 5.1 %sort.23 = (s32[2048]{0:T(1024)S(1)}, s32[2048]{0:T(1024)S(1)}, s32[2048]{0:T(1024)}) sort(s32[2048]{0:T(1024)S(1)} %fusion.4, s32[2048]{0:T(1024)S(1)} %bitcast.51, s32[2048]{0:T(1024)S(1)} %iota.10), dimensions={0}, to_apply=%region_0.1 | sort | flops 22528 | bytes 49152 | tf_op jit(solution)/shard_map/sort | solution.py:310
  49.4 0.2 convert_reduce_fusion
  49.6 0.4 collective-permute-start.1
  49.9 1.7 collective-permute-start
  51.7 2.1 collective-permute-done.1
  53.8 2.5 collective-permute-done
  56.3 37.8 %collective-permute-start.3 = (s32[3,1,3,2048]{3,2,1,0:T(4,128)S(1)}, s32[3,1,3,2048]{3,2,1,0:T(4,128)S(1)}, u32[]{:S(2)}, u32[]{:S(2)}) collective-permute-start(s32[3,1,3,2048]{3,2,1,0:T(4,128)S(1)} %add_bitcast_fusion), channel_id=1, source_target_pairs={{1,0},{2,1},{3,2},{4,3},{5,4},{6,5},{7,6},{8,7},{9,8},{10,9},{11,1... | collective-permute-start | bytes 221192 | tf_op jit(solution)/shard_map/ppermute | solution.py:292
  94.0 0.0 collective-permute-start.2
  94.0 2.2 collective-permute-done.3
  96.3 1.8 collective-permute-done.2
  98.1 0.1 pad_add_fusion
  98.1 0.8 reshape.30.lists_ref
  99.0 0.0 collective-permute-done.7.high_ref
  99.0 0.0 collective-permute-done.6.low_ref
  99.0 131.1 %pair_fields.1 = f32[19008,128]{1,0:T(8,128)} custom-call(s32[27,2048]{1,0:T(8,128)} %reshape.30.lists_ref, f32[3,2560,128]{2,1,0:T(8,128)} %collective-permute-done.6.low_ref, f32[3,2560,128]{2,1,0:T(8,128)} %pad_maximum_fusion.mid_ref, f32[3,2560,128]{2,1,0:T(8,128)} %collective-permute-done.7.high_ref), custom_call_target="tpu_custom_call" | custom-call | tf_op jit(solution)/shard_map/pair_fields/pallas_call | solution.py:266
  230.0 2.9 slice_bitcast_fusion.1
  232.9 1.7 collective-permute-start.8
  234.6 0.0 collective-permute-start.9
  234.6 26.4 %collective-permute-done.8 = f32[3,6,256,128]{3,2,1,0:T(8,128)S(1)} collective-permute-done((f32[3,6,256,128]{3,2,1,0:T(8,128)S(1)}, f32[3,6,256,128]{3,2,1,0:T(8,128)S(1)}, u32[]{:S(2)}, u32[]{:S(2)}) %collective-permute-start.8) | collective-permute-done | bytes 2359328 | tf_op jit(solution)/shard_map/ppermute | solution.py:298
  261.0 1.9 collective-permute-done.9
  262.9 2.1 fusion.1
  265.0 0.1 slice_bitcast_fusion.4
  265.1 0.0 copy-start.1
  265.1 0.0 copy-start.2
  265.1 32.0 %collective-permute-start.10 = (f32[6,256,128]{2,1,0:T(8,128)S(1)}, f32[6,256,128]{2,1,0:T(8,128)S(1)}, u32[]{:S(2)}, u32[]{:S(2)}) collective-permute-start(f32[6,256,128]{2,1,0:T(8,128)S(1)} %get-tuple-element.10), channel_id=1, source_target_pairs={{0,112},{16,0},{32,16},{48,32},{64,48},{80,64},{96,80},{112,96},{1... | collective-permute-start | bytes 2359304 | tf_op jit(solution)/shard_map/ppermute | solution.py:298
  297.1 0.0 collective-permute-start.11
  297.1 14.9 %collective-permute-done.10 = f32[6,256,128]{2,1,0:T(8,128)S(1)} collective-permute-done((f32[6,256,128]{2,1,0:T(8,128)S(1)}, f32[6,256,128]{2,1,0:T(8,128)S(1)}, u32[]{:S(2)}, u32[]{:S(2)}) %collective-permute-start.10) | collective-permute-done | bytes 786464 | tf_op jit(solution)/shard_map/ppermute | solution.py:298
  312.0 4.3 %collective-permute-done.11 = f32[6,256,128]{2,1,0:T(8,128)S(1)} collective-permute-done((f32[6,256,128]{2,1,0:T(8,128)S(1)}, f32[6,256,128]{2,1,0:T(8,128)S(1)}, u32[]{:S(2)}, u32[]{:S(2)}) %collective-permute-start.11) | collective-permute-done | bytes 786464 | tf_op jit(solution)/shard_map/ppermute | solution.py:298
  316.4 0.2 fusion.3
  316.5 0.0 copy-start
  316.5 0.0 copy-done.1
  316.5 0.0 copy-done.2
  316.6 1.7 add_multiply_fusion
  318.3 0.0 copy-done
  (7 shorter events, 0.1 us)
Async XLA Ops:
  3.1 41.0 %copy-start.3 = (s32[1,1,2,2048]{3,2,1,0:T(2,128)S(1)}, s32[1,1,2,2048]{3,2,1,0:T(2,128)}, u32[]{:S(2)}) copy-start(s32[1,1,2,2048]{3,2,1,0:T(2,128)} %param.10) | copy-start | bytes 49156
  3.1 33.2 %collective-permute-start.5 = (f32[1,2560,128]{2,1,0:T(8,128)S(1)}, f32[1,2560,128]{2,1,0:T(8,128)S(1)}, u32[]{:S(2)}, u32[]{:S(2)}) collective-permute-start(f32[1,2560,128]{2,1,0:T(8,128)S(1)} %bitcast.42), channel_id=1, source_target_pairs={{16,0},{32,16},{48,32},{64,48},{80,64},{96,80},{112,96},{0,112},{1... | collective-permute-start | bytes 3932168 | tf_op jit(solution)/shard_map/ppermute | solution.py:292
  8.2 32.3 %collective-permute-start.4 = (f32[1,2560,128]{2,1,0:T(8,128)S(1)}, f32[1,2560,128]{2,1,0:T(8,128)S(1)}, u32[]{:S(2)}, u32[]{:S(2)}) collective-permute-start(f32[1,2560,128]{2,1,0:T(8,128)S(1)} %bitcast.43), channel_id=1, source_target_pairs={{0,16},{16,32},{32,48},{48,64},{64,80},{80,96},{96,112},{112,0},{1... | collective-permute-start | bytes 3932168 | tf_op jit(solution)/shard_map/ppermute | solution.py:292
  43.0 56.0 %collective-permute-start.7 = (f32[3,2560,128]{2,1,0:T(8,128)}, f32[3,2560,128]{2,1,0:T(8,128)}, u32[]{:S(2)}, u32[]{:S(2)}) collective-permute-start(f32[3,2560,128]{2,1,0:T(8,128)} %pad_maximum_fusion.mid_ref), channel_id=1, source_target_pairs={{1,0},{2,1},{3,2},{4,3},{5,4},{6,5},{7,6},{8,7},{9,8},{10,9},{11,1... | collective-permute-start | bytes 11796488 | tf_op jit(solution)/shard_map/ppermute | solution.py:292
  43.0 56.0 %collective-permute-start.6 = (f32[3,2560,128]{2,1,0:T(8,128)}, f32[3,2560,128]{2,1,0:T(8,128)}, u32[]{:S(2)}, u32[]{:S(2)}) collective-permute-start(f32[3,2560,128]{2,1,0:T(8,128)} %pad_maximum_fusion.mid_ref), channel_id=1, source_target_pairs={{0,1},{1,2},{2,3},{3,4},{4,5},{5,6},{6,7},{7,8},{8,9},{9,10},{10,1... | collective-permute-start | bytes 11796488 | tf_op jit(solution)/shard_map/ppermute | solution.py:292
  49.6 4.2 %collective-permute-start.1 = (s32[1,3,2048]{2,1,0:T(4,128)S(1)}, s32[1,3,2048]{2,1,0:T(4,128)S(1)}, u32[]{:S(2)}, u32[]{:S(2)}) collective-permute-start(s32[1,3,2048]{2,1,0:T(4,128)S(1)} %add_bitcast_fusion.1), channel_id=1, source_target_pairs={{16,0},{32,16},{48,32},{64,48},{80,64},{96,80},{112,96},{0,112},{1... | collective-permute-start | bytes 73736 | tf_op jit(solution)/shard_map/ppermute | solution.py:292
  49.9 6.3 %collective-permute-start = (s32[1,3,2048]{2,1,0:T(4,128)S(1)}, s32[1,3,2048]{2,1,0:T(4,128)S(1)}, u32[]{:S(2)}, u32[]{:S(2)}) collective-permute-start(s32[1,3,2048]{2,1,0:T(4,128)S(1)} %add_bitcast_fusion.1), channel_id=1, source_target_pairs={{0,16},{16,32},{32,48},{48,64},{64,80},{80,96},{96,112},{112,0},{1... | collective-permute-start | bytes 73736 | tf_op jit(solution)/shard_map/ppermute | solution.py:292
  56.3 40.0 %collective-permute-start.3 = (s32[3,1,3,2048]{3,2,1,0:T(4,128)S(1)}, s32[3,1,3,2048]{3,2,1,0:T(4,128)S(1)}, u32[]{:S(2)}, u32[]{:S(2)}) collective-permute-start(s32[3,1,3,2048]{3,2,1,0:T(4,128)S(1)} %add_bitcast_fusion), channel_id=1, source_target_pairs={{1,0},{2,1},{3,2},{4,3},{5,4},{6,5},{7,6},{8,7},{9,8},{10,9},{11,1... | collective-permute-start | bytes 221192 | tf_op jit(solution)/shard_map/ppermute | solution.py:292
  94.0 4.0 %collective-permute-start.2 = (s32[3,1,3,2048]{3,2,1,0:T(4,128)S(1)}, s32[3,1,3,2048]{3,2,1,0:T(4,128)S(1)}, u32[]{:S(2)}, u32[]{:S(2)}) collective-permute-start(s32[3,1,3,2048]{3,2,1,0:T(4,128)S(1)} %add_bitcast_fusion), channel_id=1, source_target_pairs={{0,1},{1,2},{2,3},{3,4},{4,5},{5,6},{6,7},{7,8},{8,9},{9,10},{10,1... | collective-permute-start | bytes 221192 | tf_op jit(solution)/shard_map/ppermute | solution.py:292
  232.9 28.1 %collective-permute-start.8 = (f32[3,6,256,128]{3,2,1,0:T(8,128)S(1)}, f32[3,6,256,128]{3,2,1,0:T(8,128)S(1)}, u32[]{:S(2)}, u32[]{:S(2)}) collective-permute-start(f32[3,6,256,128]{3,2,1,0:T(8,128)S(1)} %get-tuple-element.8), channel_id=1, source_target_pairs={{0,15},{1,0},{2,1},{3,2},{4,3},{5,4},{6,5},{7,6},{8,7},{9,8},{10,9... | collective-permute-start | bytes 7077896 | tf_op jit(solution)/shard_map/ppermute | solution.py:298
  234.6 28.3 %collective-permute-start.9 = (f32[3,6,256,128]{3,2,1,0:T(8,128)S(1)}, f32[3,6,256,128]{3,2,1,0:T(8,128)S(1)}, u32[]{:S(2)}, u32[]{:S(2)}) collective-permute-start(f32[3,6,256,128]{3,2,1,0:T(8,128)S(1)} %get-tuple-element.9), channel_id=1, source_target_pairs={{0,1},{1,2},{2,3},{3,4},{4,5},{5,6},{6,7},{7,8},{8,9},{9,10},{10,1... | collective-permute-start | bytes 7077896 | tf_op jit(solution)/shard_map/ppermute | solution.py:298
  265.1 51.4 %copy-start.1 = (f32[6,1,1,32768]{3,2,1,0:T(1,128)S(1)}, f32[6,1,1,32768]{3,2,1,0:T(1,128)}, u32[]{:S(2)}) copy-start(f32[6,1,1,32768]{3,2,1,0:T(1,128)} %param.9) | copy-start | bytes 2359300
  265.1 51.4 %copy-start.2 = (f32[1,1,32768]{2,1,0:T(1,128)S(1)}, f32[1,1,32768]{2,1,0:T(1,128)}, u32[]{:S(2)}) copy-start(f32[1,1,32768]{2,1,0:T(1,128)} %param.7) | copy-start | bytes 393220
  265.1 46.9 %collective-permute-start.10 = (f32[6,256,128]{2,1,0:T(8,128)S(1)}, f32[6,256,128]{2,1,0:T(8,128)S(1)}, u32[]{:S(2)}, u32[]{:S(2)}) collective-permute-start(f32[6,256,128]{2,1,0:T(8,128)S(1)} %get-tuple-element.10), channel_id=1, source_target_pairs={{0,112},{16,0},{32,16},{48,32},{64,48},{80,64},{96,80},{112,96},{1... | collective-permute-start | bytes 2359304 | tf_op jit(solution)/shard_map/ppermute | solution.py:298
  297.1 19.2 %collective-permute-start.11 = (f32[6,256,128]{2,1,0:T(8,128)S(1)}, f32[6,256,128]{2,1,0:T(8,128)S(1)}, u32[]{:S(2)}, u32[]{:S(2)}) collective-permute-start(f32[6,256,128]{2,1,0:T(8,128)S(1)} %get-tuple-element.11), channel_id=1, source_target_pairs={{0,16},{16,32},{32,48},{48,64},{64,80},{80,96},{96,112},{112,0},{1... | collective-permute-start | bytes 2359304 | tf_op jit(solution)/shard_map/ppermute | solution.py:298
  316.5 1.8 copy-start

commit v3 on v2

--- a/solution.py
+++ b/solution.py
@@ -8,7 +8,8 @@
 TILE = 128
 TILES = 256
 ROWS = 10 * TILES
-UNROLL = 4
+UNROLL = 2
+HALVES = 6
 PARTS = 3
 DUMMY = TILES
 
@@ -92,9 +93,13 @@
 
 
 def kernel(
-    lists_ref, low_ref, mid_ref, high_ref, out_ref,
-    copy_sem, x_ref, geo_ref, dip_ref, acc_ref, eye_ref, near_ref, far_ref, dist_ref, coef_ref,
+    lists_ref, split_ref, *refs
 ):
+    sources, refs = refs[:9], refs[9:]
+    outs, refs = refs[:3], refs[3:]
+    (
+    out_ref, copy_sem, out_sem, x_ref, geo_ref, dip_ref, acc_ref, eye_ref, near_ref, base_ref, target_ref, grid_ref, dist_even, dist_odd, coef_even, coef_odd,
+    ) = refs
     eye = (
         lax.broadcasted_iota(jnp.int32, (TILE, TILE), 0) == lax.broadcasted_iota(jnp.int32, (TILE, TILE), 1)
     )
@@ -102,24 +107,24 @@
     zero8 = jnp.zeros((8, TILE), F32)
     own_base = 4 * ROWS
     copies = []
-    for column, source in enumerate((low_ref, mid_ref, high_ref)):
-        for row in range(3):
-            place = x_ref.at[pl.ds((3 * row + column) * ROWS, ROWS), :]
-            copies.append(pltpu.make_async_copy(source.at[row], place, copy_sem.at[3 * row + column]))
-            copies[-1].start()
+    for g, source in enumerate(sources):
+        place = x_ref.at[pl.ds(g * ROWS, ROWS), :]
+        copies.append(pltpu.make_async_copy(source, place, copy_sem.at[g]))
+        copies[-1].start()
     nt = (((1,), (1,)), ((), ()))
     eye_ref[0] = jnp.zeros((TILE, 2 * TILE), BF16)
     eye_ref[1] = jnp.concatenate(
         [jnp.where(eye, FAR_AWAY, 0.0).astype(BF16), jnp.zeros((TILE, TILE), BF16)], 1
     )
 
+    eye_ref[2] = jnp.concatenate([eye16, eye16], 1)
+
     def clear(i, _):
         out_ref[pl.ds(pl.multiple_of(i * 64, 64), 64), :] = jnp.zeros((64, TILE), F32)
         return 0
 
     lax.fori_loop(0, out_ref.shape[0] // 64, clear, 0)
-    for copy in copies:
-        copy.wait()
+    copies[4].wait()
 
     def prepare(t, _):
         centre = (8.0, 8.0, (4 * t + 2).astype(F32))
@@ -130,60 +135,82 @@
         q = scale_rows(scale, (0, 1, 0, 1, 0, 2))
         stack = jnp.concatenate([hi, mid, hi, mid, hi, lo, q, zero8], 0).astype(BF16)
         moved = lax.dot_general(eye16, stack, nt, preferred_element_type=F32).astype(BF16)
-        geo_ref[t] = jnp.concatenate([moved, eye16], 1)
+        geo_ref[t] = moved
         acc_ref[t] = jnp.zeros((32, TILE), F32)
         return 0
 
     lax.fori_loop(0, TILES, prepare, 0, unroll=4)
+    for g in range(9):
+        if g != 4:
+            copies[g].wait()
     geo_ref[DUMMY] = geo_ref[0]
     dip_ref[DUMMY] = dip_ref[0]
 
-    def blank(first):
-        for k in range(first[1]):
-            near_ref[first[0] + k] = DUMMY
-            far_ref[first[0] + k] = 4 * TILES
-
-    blank((0, 2 * UNROLL))
+    def blank(at):
+        near_ref[at] = DUMMY
+        base_ref[at] = own_base
+        target_ref[at] = UNUSED
+        grid_ref[at] = 4
+
+    for k in range(2 * UNROLL):
+        blank(k)
     total = jnp.int32(2 * UNROLL)
+    def put(at, home, remote, g):
+        target = remote + g * OUT_ROWS
+        if g == 4:
+            target = jnp.where(remote == home, UNUSED, target)
+        near_ref[at] = home
+        base_ref[at] = remote + g * ROWS
+        target_ref[at] = target
+        grid_ref[at] = g
+        return at + 1
+
     for g in range(9):
         first = lists_ref[3 * g + 2, 8 - g]
         last = lists_ref[3 * g + 2, 9 - g]
-
-        def place(p, at, g=g):
-            near_ref[at] = lists_ref[3 * g, p] & (TILES - 1)
-            far_ref[at] = lists_ref[3 * g + 1, p] + g * TILES
-            return at + 1
-
-        total = lax.fori_loop(first, last, place, total)
-    blank((total, 3 * UNROLL))
+        if g != 4:
+            last = first + split_ref[g]
+
+        def incoming(p, at, g=g):
+            return put(at, lists_ref[3 * g, p] & (TILES - 1), lists_ref[3 * g + 1, p], g)
+
+        total = lax.fori_loop(first, last, incoming, total)
+        if g != 4:
+            first = lists_ref[14, g] + split_ref[9 + g]
+            last = lists_ref[14, g + 1]
+
+            def kept(p, at, g=g):
+                return put(at, lists_ref[13, p], lists_ref[12, p] & (TILES - 1), g)
+
+            total = lax.fori_loop(first, last, kept, total)
+    for k in range((HALVES + 2) * UNROLL):
+        blank(total + k)
     groups = (total - 2 * UNROLL + UNROLL - 1) // UNROLL
 
-    def origin(home, far):
-        grid = far // TILES
+    def origin(at):
+        grid = grid_ref[at]
         row = (grid * 11) // 32
         column = grid - 3 * row
         return (
-            8.0 - domain_edge * (row - 1).astype(F32),
-            8.0 - domain_edge * (column - 1).astype(F32),
-            (4 * home + 2).astype(F32),
+            24.0 - domain_edge * row.astype(F32),
+            24.0 - domain_edge * column.astype(F32),
+            (4 * near_ref[at] + 2).astype(F32),
         )
 
-    def distances(u, at):
-        home = near_ref[at]
-        far = far_ref[at]
-        grid = far // TILES
-        base = grid * ROWS + (far - grid * TILES)
-        pos = [load_row(x_ref, base + (6 + k) * TILES) - c for k, c in enumerate(origin(home, far))]
+    def distances(dist_ref, u, at):
+        base = base_ref[at]
+        pos = [load_row(x_ref, base + (6 + k) * TILES) - c for k, c in enumerate(origin(at))]
         pol = load_row(x_ref, base + 9 * TILES)
         hi, mid, lo = geometry_rows(pos, squared(pos), 1.0)
         q = scale_rows(lax.rsqrt(pol), (0, 0, 1, 1, 2, 0))
         left = jnp.concatenate([hi, hi, mid, mid, lo, hi, zero8, zero8], 0).astype(BF16)
         right = jnp.concatenate([jnp.zeros((48, TILE), F32), q, zero8], 0).astype(BF16)
-        same = (far == 4 * TILES + home).astype(jnp.int32)
-        operand = jnp.concatenate([jnp.concatenate([left, right], 1), eye_ref[same]], 0)
-        dist_ref[u] = jnp.dot(geo_ref[home], operand, preferred_element_type=F32)
-
-    def coefficients(u):
+        same = (target_ref[at] == UNUSED).astype(jnp.int32)
+        operand = jnp.concatenate([eye_ref[same], jnp.concatenate([left, right], 1)], 0)
+        rows = jnp.concatenate([eye_ref[2, :, :TILE], geo_ref[near_ref[at]]], 1)
+        dist_ref[u] = jnp.dot(rows, operand, preferred_element_type=F32)
+
+    def coefficients(dist_ref, coef_ref, u):
         dist_sq = dist_ref[u, :, :TILE]
         inv = lax.rsqrt(dist_sq)
         inv_sq = inv * inv
@@ -208,12 +235,8 @@
             total = total + (sums[32 * k:32 * k + 32, :TILE] + sums[32 * k - 32:32 * k, TILE:])
         return total
 
-    def sums(u, at):
-        home = near_ref[at]
-        far = far_ref[at]
-        grid = far // TILES
-        remote = far - grid * TILES
-        mu, pos, pol, mixed, own = site_vectors(x_ref, grid * ROWS + remote, origin(home, far))
+    def sums(coef_ref, u, at):
+        mu, pos, pol, mixed, own = site_vectors(x_ref, base_ref[at], origin(at))
         rem = dipole_rows(mu, pos, mixed, own)
         five_hi, five_lo, three_hi, three_lo = [coef_ref[u, k] for k in range(4)]
         square = jnp.concatenate(
@@ -223,25 +246,39 @@
         square = jnp.concatenate(
             [jnp.concatenate([five_hi, five_lo], 1), jnp.concatenate([three_hi, three_lo], 1)], 0
         )
-        r = folded(jnp.dot(dip_ref[home], square, preferred_element_type=F32))
+        r = folded(jnp.dot(dip_ref[near_ref[at]], square, preferred_element_type=F32))
         field = assemble([r[8 * j:8 * j + 8] for j in range(4)], pos, mixed)
-        unused = (home == DUMMY) | (far == 4 * TILES + home)
-        target = jnp.where(unused, 4 * OUT_ROWS + DUMMY, grid * OUT_ROWS + remote)
-        return home, target, h, field
-
-    def step(i, _):
-        first = i * UNROLL
-        done = [sums(u, first + u) for u in range(UNROLL)]
+        return near_ref[at], target_ref[at], h, field
+
+    def half(first, dist_now, dist_next, coef_now, coef_next):
+        done = [sums(coef_now, u, first + u) for u in range(UNROLL)]
         for u in range(UNROLL):
-            coefficients(u)
+            coefficients(dist_now, coef_next, u)
         for u in range(UNROLL):
-            distances(u, first + 2 * UNROLL + u)
+            distances(dist_next, u, first + 2 * UNROLL + u)
         for home, target, h, field in done:
             acc_ref[home] += h
             out_ref[pl.ds(target, 8, stride=OUT_STRIDE), :] += field
+
+    even = (dist_even, dist_odd, coef_even, coef_odd)
+    odd = (dist_odd, dist_even, coef_odd, coef_even)
+
+    def step(i, _):
+        for k in range(HALVES):
+            half((HALVES * i + k) * UNROLL, *(odd if k % 2 else even))
         return 0
 
-    lax.fori_loop(0, groups + 2, step, 0)
+    lax.fori_loop(0, (groups + 1 + HALVES) // HALVES, step, 0)
+
+    sends = []
+    for g in range(9):
+        for k in range(6):
+            source = out_ref.at[pl.ds(g * OUT_ROWS + k * OUT_STRIDE, TILES), :]
+            place = outs[g % 3].at[g // 3, k]
+            sends.append(pltpu.make_async_copy(source, place, out_sem.at[6 * g + k]))
+    for k, send in enumerate(sends):
+        if k // 6 != 4:
+            send.start()
 
     def finish(t, _):
         centre = (8.0, 8.0, (4 * t + 2).astype(F32))
@@ -251,38 +288,93 @@
         return 0
 
     lax.fori_loop(0, TILES, finish, 0, unroll=4)
+    for send in sends[24:30]:
+        send.start()
+    for send in sends:
+        send.wait()
 
 
 FAR_AWAY = 2.0 ** 60
-LIST = 9 * 2048 + 5 * UNROLL
+LIST = 18 * 2048 + (HALVES + 4) * UNROLL
 OUT_STRIDE = TILES + 8
 OUT_ROWS = 8 * OUT_STRIDE
-
-
-def field_kernel(lists, low, middle, high):
+UNUSED = 4 * OUT_ROWS + DUMMY
+
+
+def field_kernel(lists, split, *sites):
     smem = pl.BlockSpec(memory_space=pltpu.SMEM)
     away = pl.BlockSpec(memory_space=pl.ANY)
-    vmem = pl.BlockSpec(memory_space=pltpu.VMEM)
     return pl.pallas_call(
         kernel,
-        out_shape=jax.ShapeDtypeStruct((9 * OUT_ROWS, TILE), F32),
-        in_specs=[smem, away, away, away],
-        out_specs=vmem,
+        out_shape=[jax.ShapeDtypeStruct((3, 6, TILES, TILE), F32)] * 3,
+        in_specs=[smem, smem] + [away] * 9,
+        out_specs=[away] * 3,
         scratch_shapes=[
+            pltpu.VMEM((9 * OUT_ROWS, TILE), F32),
             pltpu.SemaphoreType.DMA((9,)),
+            pltpu.SemaphoreType.DMA((54,)),
             pltpu.VMEM((9 * ROWS, TILE), F32),
-            pltpu.VMEM((TILES + 1, TILE, 64 + TILE), BF16),
+            pltpu.VMEM((TILES + 1, TILE, 64), BF16),
             pltpu.VMEM((TILES + 1, 32 * PARTS, 2 * TILE), BF16),
             pltpu.VMEM((TILES + 1, 32, TILE), F32),
-            pltpu.VMEM((2, TILE, 2 * TILE), BF16),
+            pltpu.VMEM((3, TILE, 2 * TILE), BF16),
+            pltpu.SMEM((LIST,), jnp.int32),
+            pltpu.SMEM((LIST,), jnp.int32),
             pltpu.SMEM((LIST,), jnp.int32),
             pltpu.SMEM((LIST,), jnp.int32),
             pltpu.VMEM((UNROLL, TILE, 2 * TILE), F32),
+            pltpu.VMEM((UNROLL, TILE, 2 * TILE), F32),
+            pltpu.VMEM((UNROLL, 4, TILE, TILE), BF16),
             pltpu.VMEM((UNROLL, 4, TILE, TILE), BF16),
         ],
         compiler_params=pltpu.CompilerParams(vmem_limit_bytes=63 * 1024 * 1024),
         name="pair_fields",
-    )(lists, low, middle, high)
+    )(lists, split, *sites)
+
+
+def grid_roll(value, row, column):
+    if row:
+        value = pltpu.roll(value, (-row) % 8, 0)
+    if column:
+        value = pltpu.roll(value, (-column) % TILE, 1)
+    return value
+
+
+def balance_kernel(counts_ref, split_ref):
+    steps = [(s // 3 - 1, s % 3 - 1) for s in range(9)]
+    counts = [counts_ref[8 * s:8 * s + 8, :] for s in range(9)]
+    others = [s for s in range(9) if s != 4]
+
+    def arriving(given, s):
+        return grid_roll(given, -steps[s][0], -steps[s][1])
+
+    def relax(_, given):
+        load = counts[4]
+        for s, part in zip(others, given):
+            load = load + (counts[s] - part) + arriving(part, s)
+        out = []
+        for s, part in zip(others, given):
+            excess = load - grid_roll(load, *steps[s])
+            out.append(jnp.clip(part + excess * 0.055, 0.0, counts[s]))
+        return tuple(out)
+
+    given = lax.fori_loop(0, 32, relax, tuple(counts[s] for s in others))
+    zero = jnp.zeros((8, TILE), F32)
+    split_ref[32:40, :] = zero
+    split_ref[104:112, :] = zero
+    for s, part in zip(others, given):
+        part = jnp.floor(part)
+        g = 8 - s
+        split_ref[8 * g:8 * g + 8, :] = arriving(part, s)
+        split_ref[72 + 8 * s:80 + 8 * s, :] = part
+
+
+def balance(counts):
+    return pl.pallas_call(
+        balance_kernel,
+        out_shape=jax.ShapeDtypeStruct((144, TILE), F32),
+        name="balance",
+    )(counts)
 
 
 def around(value, axis):
@@ -300,9 +392,7 @@
 
 def local(positions, polarity, dipoles, perm_fields, pair_list, tile_counts):
     slot_total = pair_list.shape[3]
-    sites = jnp.concatenate([dipoles, positions, polarity[None]], 0).reshape(1, 10 * TILES, TILE)
-    rows = jnp.concatenate(around(sites, "gx"), 0)
-    columns = around(rows, "gy")
+    sites = jnp.concatenate([dipoles, positions, polarity[None]], 0).reshape(10 * TILES, TILE)
 
     table = pair_list.reshape(2, slot_total)
     live = jnp.arange(slot_total, dtype=jnp.int32) < tile_counts.reshape(())
@@ -310,13 +400,26 @@
     far, near = lax.sort((far, table[0]), num_keys=1)
     bounds = jnp.arange(slot_total, dtype=jnp.int32)[:16] * TILES
     bounds = jnp.sum((far[None, :] < bounds[:, None]).astype(jnp.int32), 1)
+    counts = (bounds[1:10] - bounds[:9]).astype(F32)
     bounds = jnp.concatenate([bounds, jnp.zeros((slot_total - 16,), jnp.int32)])
     lists = jnp.stack([far, near, bounds])[None]
     lists = jnp.concatenate(around(lists, "gx"), 0)[:, None]
+
+    middle = around(sites, "gx")
+    sides = around(sites, "gy")
+    middle[0], middle[2], lists, sides[0], sides[2] = lax.optimization_barrier(
+        (middle[0], middle[2], lists, sides[0], sides[2])
+    )
     lists = jnp.concatenate(around(lists, "gy"), 1).reshape(27, slot_total)
-    terms = field_kernel(lists, *columns)
-    terms = terms.reshape(3, 3, 8, OUT_STRIDE, TILE)[:, :, :6, :TILES]
-    column = terms[:, 1] + shifted(terms[:, 0], "gy", -1) + shifted(terms[:, 2], "gy", 1)
+    everyone = lax.all_gather(lax.all_gather(counts, "gy"), "gx")
+    everyone = jnp.tile(everyone.transpose(2, 0, 1), (1, 1, 8)).reshape(72, TILE)
+    split = balance(everyone).reshape(18, 8, TILE)
+    here = (0, lax.axis_index("gx"), lax.axis_index("gy"))
+    split = lax.dynamic_slice(split, here, (18, 1, 1)).reshape(18).astype(jnp.int32)
+    upper = around(middle[0], "gy")
+    lower = around(middle[2], "gy")
+    low, mid, high = field_kernel(lists, split, *upper, *sides, *lower)
+    column = mid + shifted(low, "gy", -1) + shifted(high, "gy", 1)
     field = column[1] + shifted(column[0], "gx", -1) + shifted(column[2], "gx", 1)
     field = field.reshape(6, 1, 1, TILES * TILE)
     induced = polarity[None] * (perm_fields + field)

time: 319 us -> 806 us (2.53)
  the two profiles are of different devices: /device:TPU:2 before, /device:TPU:0 now
where the time goes in v3:
time: 806 us; the launch traced here: 802 us
  Pallas kernels  574 us (71%)
  waiting for transfers between devices  92.7 us (12%)
  blocking collectives  81.6 us (10%)
  starting transfers between devices  32.3 us (4%)
  other arithmetic  11.4 us (1%)
    pallas_call x1, Pallas kernels, field_kernel(): pl.pallas_call(kernel, out_shape=[jax.ShapeDtypeStruct((3, 6, TILES, TILE...  567 us
    unnamed x1, blocking collectives  53.4 us
    ppermute x4, waiting for transfers between devices, shifted(): return lax.ppermute(value, axis, pairs)  47.4 us
    ppermute x6, waiting for transfers between devices, around(): lax.ppermute(value, axis, backward)  31.6 us
    all_gather x1, blocking collectives, local(): everyone = lax.all_gather(lax.all_gather(counts, 'gy'), 'gx')  28.2 us
    ppermute x6, starting transfers between devices, around(): lax.ppermute(value, axis, backward)  18.7 us
  transfers between devices with their start and end apart: 16, of which 8 were waited for; matrix products, arithmetic and copies ran while one was open for 1% of the time, Pallas kernels for 1%

profile of v3, /device:TPU:0, one launch (start us, length us, event | category | flops | bytes accessed | tf_op | source)
XLA Modules:
  0.0 801.5 jit_solution(7874170397920809234)
XLA Ops:
  0.6 0.0 copy-start.5
  0.6 0.0 copy-start.6
  0.7 2.5 pad_maximum_fusion
  3.1 5.0 collective-permute-start.5
  8.1 0.0 collective-permute-start.4
  8.1 4.2 collective-permute-start.1
  12.3 0.0 collective-permute-start
  13.0 5.1 sort.23
  18.1 0.2 convert_reduce_fusion
  18.4 4.2 collective-permute-start.3
  22.6 30.4 %collective-permute-done.3 = s32[1,3,2048]{2,1,0:T(4,128)S(1)} collective-permute-done((s32[1,3,2048]{2,1,0:T(4,128)S(1)}, s32[1,3,2048]{2,1,0:T(4,128)S(1)}, u32[]{:S(2)}, u32[]{:S(2)}) %collective-permute-start.3) | collective-permute-done | bytes 24608 | tf_op jit(solution)/shard_map/ppermute | solution.py:384
  53.0 0.0 collective-permute-start.2
  53.0 6.5 collective-permute-done.2
  59.5 0.0 collective-permute-done.5.refs_5_
  59.5 0.0 collective-permute-done.4.refs_3_
  59.5 0.0 collective-permute-done.1.refs_7_
  59.5 0.0 collective-permute-done.refs_1_
  59.5 1.0 copy-done.2
  60.6 0.3 collective-permute-start.9
  60.8 0.3 collective-permute-start.8
  61.1 5.1 collective-permute-start.11
  66.2 0.0 collective-permute-start.10
  66.2 0.6 dynamic-slice
  67.4 0.2 convert_dynamic-update-slice_fusion
  67.6 53.4 %all-reduce.1 = f32[144]{0:T(256)S(1)} all-reduce(f32[144]{0:T(256)S(1)} %convert_dynamic-update-slice_fusion), channel_id=2, replica_groups=mesh['gx'=8,'gy'=16] {'gy'}, use_global_device_ids=true, to_apply=%add.1 | all-reduce | flops 144 | bytes 1152
  121.0 0.1 reshape.40
  121.1 28.2 %all-gather.1 = f32[128,9]{1,0:T(8,128)S(1)} all-gather(f32[16,9]{1,0:T(8,128)S(1)} %reshape.40), channel_id=3, replica_groups=mesh['gx'=8,'gy'=16] {'gx'}, dimensions={0}, use_global_device_ids=true | all-gather | bytes 5184 | tf_op jit(solution)/shard_map/all_gather | solution.py:414
  149.3 0.1 copy.16
  149.4 0.8 tile.9.counts_ref
  150.2 6.7 balance.1
  156.8 0.0 collective-permute-start.7
  156.8 1.0 constant_dynamic-slice_fusion
  157.8 0.1 copy.21
  157.9 1.2 collective-permute-done.7
  159.0 0.0 collective-permute-start.6
  159.0 0.5 convert_bitcast_fusion.split_ref
  159.6 7.2 collective-permute-done.6
  166.8 0.1 pad_add_fusion
  166.8 0.8 reshape.37.lists_ref
  167.7 0.0 collective-permute-done.9.refs_2_
  167.7 0.0 collective-permute-done.8.refs_0_
  167.7 0.0 collective-permute-done.11.refs_8_
  167.7 0.0 collective-permute-done.10.refs_6_
  167.7 567.1 %pair_fields.1 = (f32[3,6,256,128]{3,2,1,0:T(8,128)}, f32[3,6,256,128]{3,2,1,0:T(8,128)}, f32[3,6,256,128]{3,2,1,0:T(8,128)}) custom-call(s32[27,2048]{1,0:T(8,128)} %reshape.37.lists_ref, s32[18]{0:T(128)} %convert_bitcast_fusion.split_ref, f32[2560,128]{1,0:T(8,128)} %collective-permute-done.8.refs_0_, f32[2560,128]{1,0:T(8,128)} %collective-permute-done.refs_1_, ...), custom_call_target="tpu_custom_call" | custom-call | tf_op jit(solution)/shard_map/pair_fields/pallas_call | solution.py:307
  734.8 0.1 collective-permute-start.12
  734.9 0.5 collective-permute-start.13
  735.4 26.2 %collective-permute-done.12 = f32[3,6,256,128]{3,2,1,0:T(8,128)S(1)} collective-permute-done((f32[3,6,256,128]{3,2,1,0:T(8,128)}, f32[3,6,256,128]{3,2,1,0:T(8,128)S(1)}, u32[]{:S(2)}, u32[]{:S(2)}) %collective-permute-start.12) | collective-permute-done | bytes 2359328 | tf_op jit(solution)/shard_map/ppermute | solution.py:390
  761.6 5.5 collective-permute-done.13
  767.0 2.1 add_add_fusion
  769.1 0.1 slice_bitcast_fusion.1
  769.2 12.8 %collective-permute-start.14 = (f32[6,256,128]{2,1,0:T(8,128)S(1)}, f32[6,256,128]{2,1,0:T(8,128)S(1)}, u32[]{:S(2)}, u32[]{:S(2)}) collective-permute-start(f32[6,256,128]{2,1,0:T(8,128)S(1)} %get-tuple-element.30), channel_id=1, source_target_pairs={{0,112},{16,0},{32,16},{48,32},{64,48},{80,64},{96,80},{112,96},{1... | collective-permute-start | bytes 2359304 | tf_op jit(solution)/shard_map/ppermute | solution.py:390
  782.0 0.0 collective-permute-start.15
  782.0 11.4 %collective-permute-done.14 = f32[6,256,128]{2,1,0:T(8,128)S(1)} collective-permute-done((f32[6,256,128]{2,1,0:T(8,128)S(1)}, f32[6,256,128]{2,1,0:T(8,128)S(1)}, u32[]{:S(2)}, u32[]{:S(2)}) %collective-permute-start.14) | collective-permute-done | bytes 786464 | tf_op jit(solution)/shard_map/ppermute | solution.py:390
  793.4 4.3 collective-permute-done.15
  797.8 0.1 fusion.2
  797.9 0.0 copy-start.1
  797.9 0.0 copy-start.3
  797.9 0.0 copy-start.4
  797.9 0.2 reshape.39
  798.1 1.2 copy-done.3
  799.3 0.0 copy-done.4
  799.3 0.5 fusion
  799.8 0.0 copy-done.1
  799.9 1.7 copy.20
  (14 shorter events, 0.1 us)
Async XLA Ops:
  0.6 12.3 %copy-start.5 = (s32[1,1,2,2048]{3,2,1,0:T(2,128)S(1)}, s32[1,1,2,2048]{3,2,1,0:T(2,128)}, u32[]{:S(2)}) copy-start(s32[1,1,2,2048]{3,2,1,0:T(2,128)} %param.10) | copy-start | bytes 49156
  0.6 65.5 %copy-start.6 = (u32[128]{0:T(128)S(1)}, u32[128]{0:T(128)}, u32[]{:S(2)}) copy-start(u32[128]{0:T(128)} %constant.30) | copy-start | bytes 1540
  3.1 9.1 %copy-start = (f32[10,1,1,32768]{3,2,1,0:T(1,128)}, f32[10,1,1,32768]{3,2,1,0:T(1,128)S(1)}, u32[]{:S(2)}) copy-start(f32[10,1,1,32768]{3,2,1,0:T(1,128)S(1)} %pad_maximum_fusion) | copy-start | bytes 3932164
  3.1 56.3 %collective-permute-start.5 = (f32[2560,128]{1,0:T(8,128)S(1)}, f32[2560,128]{1,0:T(8,128)S(1)}, u32[]{:S(2)}, u32[]{:S(2)}) collective-permute-start(f32[2560,128]{1,0:T(8,128)S(1)} %bitcast.36), channel_id=1, source_target_pairs={{1,0},{2,1},{3,2},{4,3},{5,4},{6,5},{7,6},{8,7},{9,8},{10,9},{11,1... | collective-permute-start | bytes 3932168 | tf_op jit(solution)/shard_map/ppermute | solution.py:384
  8.1 51.4 %collective-permute-start.4 = (f32[2560,128]{1,0:T(8,128)S(1)}, f32[2560,128]{1,0:T(8,128)}, u32[]{:S(2)}, u32[]{:S(2)}) collective-permute-start(f32[2560,128]{1,0:T(8,128)S(1)} %bitcast.37), channel_id=1, source_target_pairs={{0,1},{1,2},{2,3},{3,4},{4,5},{5,6},{6,7},{7,8},{8,9},{9,10},{10,1... | collective-permute-start | bytes 3932168 | tf_op jit(solution)/shard_map/ppermute | solution.py:384
  8.1 51.4 %collective-permute-start.1 = (f32[2560,128]{1,0:T(8,128)S(1)}, f32[2560,128]{1,0:T(8,128)}, u32[]{:S(2)}, u32[]{:S(2)}) collective-permute-start(f32[2560,128]{1,0:T(8,128)S(1)} %bitcast.38), channel_id=1, source_target_pairs={{16,0},{32,16},{48,32},{64,48},{80,64},{96,80},{112,96},{0,112},{1... | collective-permute-start | bytes 3932168 | tf_op jit(solution)/shard_map/ppermute | solution.py:384
  12.3 47.3 %collective-permute-start = (f32[2560,128]{1,0:T(8,128)S(1)}, f32[2560,128]{1,0:T(8,128)}, u32[]{:S(2)}, u32[]{:S(2)}) collective-permute-start(f32[2560,128]{1,0:T(8,128)S(1)} %bitcast.39), channel_id=1, source_target_pairs={{0,16},{16,32},{32,48},{48,64},{64,80},{80,96},{96,112},{112,0},{1... | collective-permute-start | bytes 3932168 | tf_op jit(solution)/shard_map/ppermute | solution.py:384
  18.4 34.6 %collective-permute-start.3 = (s32[1,3,2048]{2,1,0:T(4,128)S(1)}, s32[1,3,2048]{2,1,0:T(4,128)S(1)}, u32[]{:S(2)}, u32[]{:S(2)}) collective-permute-start(s32[1,3,2048]{2,1,0:T(4,128)S(1)} %add_bitcast_fusion.1), channel_id=1, source_target_pairs={{16,0},{32,16},{48,32},{64,48},{80,64},{96,80},{112,96},{0,112},{1... | collective-permute-start | bytes 73736 | tf_op jit(solution)/shard_map/ppermute | solution.py:384
  53.0 6.5 collective-permute-start.2
  59.5 1.1 copy-start.2
  60.6 107.1 %collective-permute-start.9 = (f32[2560,128]{1,0:T(8,128)}, f32[2560,128]{1,0:T(8,128)}, u32[]{:S(2)}, u32[]{:S(2)}) collective-permute-start(f32[2560,128]{1,0:T(8,128)} %collective-permute-done.refs_1_), channel_id=1, source_target_pairs={{1,0},{2,1},{3,2},{4,3},{5,4},{6,5},{7,6},{8,7},{9,8},{10,9},{11,1... | collective-permute-start | bytes 3932168 | tf_op jit(solution)/shard_map/ppermute | solution.py:384
  60.8 106.8 %collective-permute-start.8 = (f32[2560,128]{1,0:T(8,128)}, f32[2560,128]{1,0:T(8,128)}, u32[]{:S(2)}, u32[]{:S(2)}) collective-permute-start(f32[2560,128]{1,0:T(8,128)} %collective-permute-done.refs_1_), channel_id=1, source_target_pairs={{0,1},{1,2},{2,3},{3,4},{4,5},{5,6},{6,7},{7,8},{8,9},{9,10},{10,1... | collective-permute-start | bytes 3932168 | tf_op jit(solution)/shard_map/ppermute | solution.py:384
  61.1 106.6 %collective-permute-start.11 = (f32[2560,128]{1,0:T(8,128)}, f32[2560,128]{1,0:T(8,128)}, u32[]{:S(2)}, u32[]{:S(2)}) collective-permute-start(f32[2560,128]{1,0:T(8,128)} %collective-permute-done.1.refs_7_), channel_id=1, source_target_pairs={{1,0},{2,1},{3,2},{4,3},{5,4},{6,5},{7,6},{8,7},{9,8},{10,9},{11,1... | collective-permute-start | bytes 3932168 | tf_op jit(solution)/shard_map/ppermute | solution.py:384
  66.2 101.5 %collective-permute-start.10 = (f32[2560,128]{1,0:T(8,128)}, f32[2560,128]{1,0:T(8,128)}, u32[]{:S(2)}, u32[]{:S(2)}) collective-permute-start(f32[2560,128]{1,0:T(8,128)} %collective-permute-done.1.refs_7_), channel_id=1, source_target_pairs={{0,1},{1,2},{2,3},{3,4},{4,5},{5,6},{6,7},{7,8},{8,9},{9,10},{10,1... | collective-permute-start | bytes 3932168 | tf_op jit(solution)/shard_map/ppermute | solution.py:384
  156.8 2.2 collective-permute-start.7
  159.0 7.7 collective-permute-start.6
  734.8 26.8 %collective-permute-start.12 = (f32[3,6,256,128]{3,2,1,0:T(8,128)}, f32[3,6,256,128]{3,2,1,0:T(8,128)S(1)}, u32[]{:S(2)}, u32[]{:S(2)}) collective-permute-start(f32[3,6,256,128]{3,2,1,0:T(8,128)} %get-tuple-element.22), channel_id=1, source_target_pairs={{0,15},{1,0},{2,1},{3,2},{4,3},{5,4},{6,5},{7,6},{8,7},{9,8},{10,9... | collective-permute-start | bytes 7077896 | tf_op jit(solution)/shard_map/ppermute | solution.py:390
  734.9 32.2 %collective-permute-start.13 = (f32[3,6,256,128]{3,2,1,0:T(8,128)}, f32[3,6,256,128]{3,2,1,0:T(8,128)S(1)}, u32[]{:S(2)}, u32[]{:S(2)}) collective-permute-start(f32[3,6,256,128]{3,2,1,0:T(8,128)} %get-tuple-element.23), channel_id=1, source_target_pairs={{0,1},{1,2},{2,3},{3,4},{4,5},{5,6},{6,7},{7,8},{8,9},{9,10},{10,1... | collective-permute-start | bytes 7077896 | tf_op jit(solution)/shard_map/ppermute | solution.py:390
  769.2 24.2 %collective-permute-start.14 = (f32[6,256,128]{2,1,0:T(8,128)S(1)}, f32[6,256,128]{2,1,0:T(8,128)S(1)}, u32[]{:S(2)}, u32[]{:S(2)}) collective-permute-start(f32[6,256,128]{2,1,0:T(8,128)S(1)} %get-tuple-element.30), channel_id=1, source_target_pairs={{0,112},{16,0},{32,16},{48,32},{64,48},{80,64},{96,80},{112,96},{1... | collective-permute-start | bytes 2359304 | tf_op jit(solution)/shard_map/ppermute | solution.py:390
  782.0 15.7 %collective-permute-start.15 = (f32[6,256,128]{2,1,0:T(8,128)S(1)}, f32[6,256,128]{2,1,0:T(8,128)S(1)}, u32[]{:S(2)}, u32[]{:S(2)}) collective-permute-start(f32[6,256,128]{2,1,0:T(8,128)S(1)} %get-tuple-element.31), channel_id=1, source_target_pairs={{0,16},{16,32},{32,48},{48,64},{64,80},{80,96},{96,112},{112,0},{1... | collective-permute-start | bytes 2359304 | tf_op jit(solution)/shard_map/ppermute | solution.py:390
  797.9 2.0 copy-start.1
  797.9 1.4 copy-start.3
  797.9 1.4 copy-start.4

commit v4 on v3

--- a/solution.py
+++ b/solution.py
@@ -12,6 +12,7 @@
 HALVES = 6
 PARTS = 3
 DUMMY = TILES
+GRID = 2 * TILES
 
 thole = 0.39
 domain_edge = 16.0
@@ -93,12 +94,12 @@
 
 
 def kernel(
-    lists_ref, split_ref, *refs
+    lists_ref, *refs
 ):
     sources, refs = refs[:9], refs[9:]
     outs, refs = refs[:3], refs[3:]
     (
-    out_ref, copy_sem, out_sem, x_ref, geo_ref, dip_ref, acc_ref, eye_ref, near_ref, base_ref, target_ref, grid_ref, dist_even, dist_odd, coef_even, coef_odd,
+    out_ref, copy_sem, out_sem, x_ref, geo_ref, dip_ref, acc_ref, eye_ref, near_ref, base_ref, target_ref, dist_even, dist_odd, coef_even, coef_odd,
     ) = refs
     eye = (
         lax.broadcasted_iota(jnp.int32, (TILE, TILE), 0) == lax.broadcasted_iota(jnp.int32, (TILE, TILE), 1)
@@ -147,10 +148,9 @@
     dip_ref[DUMMY] = dip_ref[0]
 
     def blank(at):
-        near_ref[at] = DUMMY
+        near_ref[at] = DUMMY + 4 * GRID
         base_ref[at] = own_base
         target_ref[at] = UNUSED
-        grid_ref[at] = 4
 
     for k in range(2 * UNROLL):
         blank(k)
@@ -159,42 +159,34 @@
         target = remote + g * OUT_ROWS
         if g == 4:
             target = jnp.where(remote == home, UNUSED, target)
-        near_ref[at] = home
+        near_ref[at] = home + g * GRID
         base_ref[at] = remote + g * ROWS
         target_ref[at] = target
-        grid_ref[at] = g
         return at + 1
 
     for g in range(9):
         first = lists_ref[3 * g + 2, 8 - g]
         last = lists_ref[3 * g + 2, 9 - g]
-        if g != 4:
-            last = first + split_ref[g]
 
         def incoming(p, at, g=g):
             return put(at, lists_ref[3 * g, p] & (TILES - 1), lists_ref[3 * g + 1, p], g)
 
         total = lax.fori_loop(first, last, incoming, total)
-        if g != 4:
-            first = lists_ref[14, g] + split_ref[9 + g]
-            last = lists_ref[14, g + 1]
-
-            def kept(p, at, g=g):
-                return put(at, lists_ref[13, p], lists_ref[12, p] & (TILES - 1), g)
-
-            total = lax.fori_loop(first, last, kept, total)
     for k in range((HALVES + 2) * UNROLL):
         blank(total + k)
     groups = (total - 2 * UNROLL + UNROLL - 1) // UNROLL
 
+    def home_of(at):
+        return near_ref[at] & (GRID - 1)
+
     def origin(at):
-        grid = grid_ref[at]
+        grid = near_ref[at] // GRID
         row = (grid * 11) // 32
         column = grid - 3 * row
         return (
             24.0 - domain_edge * row.astype(F32),
             24.0 - domain_edge * column.astype(F32),
-            (4 * near_ref[at] + 2).astype(F32),
+            (4 * home_of(at) + 2).astype(F32),
         )
 
     def distances(dist_ref, u, at):
@@ -207,7 +199,7 @@
         right = jnp.concatenate([jnp.zeros((48, TILE), F32), q, zero8], 0).astype(BF16)
         same = (target_ref[at] == UNUSED).astype(jnp.int32)
         operand = jnp.concatenate([eye_ref[same], jnp.concatenate([left, right], 1)], 0)
-        rows = jnp.concatenate([eye_ref[2, :, :TILE], geo_ref[near_ref[at]]], 1)
+        rows = jnp.concatenate([eye_ref[2, :, :TILE], geo_ref[home_of(at)]], 1)
         dist_ref[u] = jnp.dot(rows, operand, preferred_element_type=F32)
 
     def coefficients(dist_ref, coef_ref, u):
@@ -246,9 +238,9 @@
         square = jnp.concatenate(
             [jnp.concatenate([five_hi, five_lo], 1), jnp.concatenate([three_hi, three_lo], 1)], 0
         )
-        r = folded(jnp.dot(dip_ref[near_ref[at]], square, preferred_element_type=F32))
+        r = folded(jnp.dot(dip_ref[home_of(at)], square, preferred_element_type=F32))
         field = assemble([r[8 * j:8 * j + 8] for j in range(4)], pos, mixed)
-        return near_ref[at], target_ref[at], h, field
+        return home_of(at), target_ref[at], h, field
 
     def half(first, dist_now, dist_next, coef_now, coef_next):
         done = [sums(coef_now, u, first + u) for u in range(UNROLL)]
@@ -295,19 +287,19 @@
 
 
 FAR_AWAY = 2.0 ** 60
-LIST = 18 * 2048 + (HALVES + 4) * UNROLL
+LIST = 9 * 2048 + (HALVES + 4) * UNROLL
 OUT_STRIDE = TILES + 8
 OUT_ROWS = 8 * OUT_STRIDE
 UNUSED = 4 * OUT_ROWS + DUMMY
 
 
-def field_kernel(lists, split, *sites):
+def field_kernel(lists, *sites):
     smem = pl.BlockSpec(memory_space=pltpu.SMEM)
     away = pl.BlockSpec(memory_space=pl.ANY)
     return pl.pallas_call(
         kernel,
         out_shape=[jax.ShapeDtypeStruct((3, 6, TILES, TILE), F32)] * 3,
-        in_specs=[smem, smem] + [away] * 9,
+        in_specs=[smem] + [away] * 9,
         out_specs=[away] * 3,
         scratch_shapes=[
             pltpu.VMEM((9 * OUT_ROWS, TILE), F32),
@@ -321,7 +313,6 @@
             pltpu.SMEM((LIST,), jnp.int32),
             pltpu.SMEM((LIST,), jnp.int32),
             pltpu.SMEM((LIST,), jnp.int32),
-            pltpu.SMEM((LIST,), jnp.int32),
             pltpu.VMEM((UNROLL, TILE, 2 * TILE), F32),
             pltpu.VMEM((UNROLL, TILE, 2 * TILE), F32),
             pltpu.VMEM((UNROLL, 4, TILE, TILE), BF16),
@@ -329,52 +320,7 @@
         ],
         compiler_params=pltpu.CompilerParams(vmem_limit_bytes=63 * 1024 * 1024),
         name="pair_fields",
-    )(lists, split, *sites)
-
-
-def grid_roll(value, row, column):
-    if row:
-        value = pltpu.roll(value, (-row) % 8, 0)
-    if column:
-        value = pltpu.roll(value, (-column) % TILE, 1)
-    return value
-
-
-def balance_kernel(counts_ref, split_ref):
-    steps = [(s // 3 - 1, s % 3 - 1) for s in range(9)]
-    counts = [counts_ref[8 * s:8 * s + 8, :] for s in range(9)]
-    others = [s for s in range(9) if s != 4]
-
-    def arriving(given, s):
-        return grid_roll(given, -steps[s][0], -steps[s][1])
-
-    def relax(_, given):
-        load = counts[4]
-        for s, part in zip(others, given):
-            load = load + (counts[s] - part) + arriving(part, s)
-        out = []
-        for s, part in zip(others, given):
-            excess = load - grid_roll(load, *steps[s])
-            out.append(jnp.clip(part + excess * 0.055, 0.0, counts[s]))
-        return tuple(out)
-
-    given = lax.fori_loop(0, 32, relax, tuple(counts[s] for s in others))
-    zero = jnp.zeros((8, TILE), F32)
-    split_ref[32:40, :] = zero
-    split_ref[104:112, :] = zero
-    for s, part in zip(others, given):
-        part = jnp.floor(part)
-        g = 8 - s
-        split_ref[8 * g:8 * g + 8, :] = arriving(part, s)
-        split_ref[72 + 8 * s:80 + 8 * s, :] = part
-
-
-def balance(counts):
-    return pl.pallas_call(
-        balance_kernel,
-        out_shape=jax.ShapeDtypeStruct((144, TILE), F32),
-        name="balance",
-    )(counts)
+    )(lists, *sites)
 
 
 def around(value, axis):
@@ -400,7 +346,6 @@
     far, near = lax.sort((far, table[0]), num_keys=1)
     bounds = jnp.arange(slot_total, dtype=jnp.int32)[:16] * TILES
     bounds = jnp.sum((far[None, :] < bounds[:, None]).astype(jnp.int32), 1)
-    counts = (bounds[1:10] - bounds[:9]).astype(F32)
     bounds = jnp.concatenate([bounds, jnp.zeros((slot_total - 16,), jnp.int32)])
     lists = jnp.stack([far, near, bounds])[None]
     lists = jnp.concatenate(around(lists, "gx"), 0)[:, None]
@@ -411,14 +356,9 @@
         (middle[0], middle[2], lists, sides[0], sides[2])
     )
     lists = jnp.concatenate(around(lists, "gy"), 1).reshape(27, slot_total)
-    everyone = lax.all_gather(lax.all_gather(counts, "gy"), "gx")
-    everyone = jnp.tile(everyone.transpose(2, 0, 1), (1, 1, 8)).reshape(72, TILE)
-    split = balance(everyone).reshape(18, 8, TILE)
-    here = (0, lax.axis_index("gx"), lax.axis_index("gy"))
-    split = lax.dynamic_slice(split, here, (18, 1, 1)).reshape(18).astype(jnp.int32)
     upper = around(middle[0], "gy")
     lower = around(middle[2], "gy")
-    low, mid, high = field_kernel(lists, split, *upper, *sides, *lower)
+    low, mid, high = field_kernel(lists, *upper, *sides, *lower)
     column = mid + shifted(low, "gy", -1) + shifted(high, "gy", 1)
     field = column[1] + shifted(column[0], "gx", -1) + shifted(column[2], "gx", 1)
     field = field.reshape(6, 1, 1, TILES * TILE)

time: 806 us -> 258 us (0.32)
  the two profiles are of different devices: /device:TPU:0 before, /device:TPU:85 now
where the time goes in v4:
time: 258 us
  Pallas kernels  103 us (40%)
  waiting for transfers between devices  95.2 us (37%)
  starting transfers between devices  42.3 us (16%)
  other arithmetic  10.7 us (4%)
  local copies, waits for them, and re-layouts  5.06 us (2%)
    pallas_call x1, Pallas kernels, field_kernel(): pl.pallas_call(kernel, out_shape=[jax.ShapeDtypeStruct((3, 6, TILES, TILE...  103 us
    ppermute x6, waiting for transfers between devices, around(): lax.ppermute(value, axis, backward)  52.5 us
    ppermute x4, waiting for transfers between devices, shifted(): return lax.ppermute(value, axis, pairs)  40 us
    ppermute x6, starting transfers between devices, around(): lax.ppermute(value, axis, forward)  20.6 us
    ppermute x4, starting transfers between devices, shifted(): return lax.ppermute(value, axis, pairs)  19.6 us
  transfers between devices with their start and end apart: 16, of which 7 were waited for; matrix products, arithmetic and copies ran while one was open for 2% of the time, Pallas kernels for 0%

profile of v4, /device:TPU:85, one launch (start us, length us, event | category | flops | bytes accessed | tf_op | source)
XLA Modules:
  0.0 257.7 jit_solution(9228248607268834357)
XLA Ops:
  0.6 0.0 copy-start.5
  0.6 2.5 pad_maximum_fusion
  3.1 0.0 copy-start
  3.1 0.7 collective-permute-start.5
  3.9 1.1 collective-permute-start.4
  4.9 0.0 collective-permute-start.1
  5.0 0.0 copy-done
  5.0 1.5 collective-permute-start
  7.1 0.0 copy-done.5
  7.1 5.1 %sort.23 = (s32[2048]{0:T(1024)S(1)}, s32[2048]{0:T(1024)S(1)}, s32[2048]{0:T(1024)}) sort(s32[2048]{0:T(1024)S(1)} %fusion.3, s32[2048]{0:T(1024)S(1)} %bitcast.35, s32[2048]{0:T(1024)S(1)} %iota.10), dimensions={0}, to_apply=%region_0.1 | sort | flops 22528 | bytes 49152 | tf_op jit(solution)/shard_map/sort | solution.py:346
  12.3 0.2 convert_reduce_fusion
  12.5 0.1 collective-permute-start.3
  12.6 23.7 %collective-permute-done.3 = s32[1,3,2048]{2,1,0:T(4,128)S(1)} collective-permute-done((s32[1,3,2048]{2,1,0:T(4,128)S(1)}, s32[1,3,2048]{2,1,0:T(4,128)S(1)}, u32[]{:S(2)}, u32[]{:S(2)}) %collective-permute-start.3) | collective-permute-done | bytes 24608 | tf_op jit(solution)/shard_map/ppermute | solution.py:330
  36.2 3.5 %collective-permute-start.2 = (s32[1,3,2048]{2,1,0:T(4,128)S(1)}, s32[1,3,2048]{2,1,0:T(4,128)S(1)}, u32[]{:S(2)}, u32[]{:S(2)}) collective-permute-start(s32[1,3,2048]{2,1,0:T(4,128)S(1)} %add_bitcast_fusion.1), channel_id=1, source_target_pairs={{0,16},{16,32},{32,48},{48,64},{64,80},{80,96},{96,112},{112,0},{1... | collective-permute-start | bytes 73736 | tf_op jit(solution)/shard_map/ppermute | solution.py:330
  39.7 1.0 collective-permute-done.2
  40.7 0.0 collective-permute-done.5.refs_5_
  40.8 0.0 copy-start.2
  40.8 0.0 collective-permute-done.4.refs_3_
  40.8 0.0 collective-permute-done.1.refs_7_
  40.8 0.0 collective-permute-done.refs_1_
  40.8 1.0 copy-done.2
  41.8 1.2 collective-permute-start.9
  43.1 12.9 %collective-permute-start.8 = (f32[2560,128]{1,0:T(8,128)}, f32[2560,128]{1,0:T(8,128)}, u32[]{:S(2)}, u32[]{:S(2)}) collective-permute-start(f32[2560,128]{1,0:T(8,128)} %collective-permute-done.refs_1_), channel_id=1, source_target_pairs={{0,1},{1,2},{2,3},{3,4},{4,5},{5,6},{6,7},{7,8},{8,9},{9,10},{10,1... | collective-permute-start | bytes 3932168 | tf_op jit(solution)/shard_map/ppermute | solution.py:330
  56.0 0.0 collective-permute-start.11
  56.0 1.7 collective-permute-start.10
  57.7 0.0 collective-permute-start.7
  57.7 28.8 %collective-permute-done.7 = s32[3,1,3,2048]{3,2,1,0:T(4,128)S(1)} collective-permute-done((s32[3,1,3,2048]{3,2,1,0:T(4,128)S(1)}, s32[3,1,3,2048]{3,2,1,0:T(4,128)S(1)}, u32[]{:S(2)}, u32[]{:S(2)}) %collective-permute-start.7) | collective-permute-done | bytes 73760 | tf_op jit(solution)/shard_map/ppermute | solution.py:330
  86.6 0.0 collective-permute-start.6
  86.6 1.6 collective-permute-done.6
  88.2 0.1 pad_add_fusion
  88.3 0.8 reshape.28.lists_ref
  89.1 0.0 collective-permute-done.9.refs_2_
  89.1 0.0 collective-permute-done.8.refs_0_
  89.1 0.0 collective-permute-done.11.refs_8_
  89.1 0.0 collective-permute-done.10.refs_6_
  89.1 103.0 %pair_fields.1 = (f32[3,6,256,128]{3,2,1,0:T(8,128)}, f32[3,6,256,128]{3,2,1,0:T(8,128)}, f32[3,6,256,128]{3,2,1,0:T(8,128)}) custom-call(s32[27,2048]{1,0:T(8,128)} %reshape.28.lists_ref, f32[2560,128]{1,0:T(8,128)} %collective-permute-done.8.refs_0_, f32[2560,128]{1,0:T(8,128)} %collective-permute-done.refs_1_, ...), custom_call_target="tpu_custom_call" | custom-call | tf_op jit(solution)/shard_map/pair_fields/pallas_call | solution.py:299
  192.1 0.1 collective-permute-start.12
  192.2 1.7 collective-permute-start.13
  193.9 26.7 %collective-permute-done.12 = f32[3,6,256,128]{3,2,1,0:T(8,128)S(1)} collective-permute-done((f32[3,6,256,128]{3,2,1,0:T(8,128)}, f32[3,6,256,128]{3,2,1,0:T(8,128)S(1)}, u32[]{:S(2)}, u32[]{:S(2)}) %collective-permute-start.12) | collective-permute-done | bytes 2359328 | tf_op jit(solution)/shard_map/ppermute | solution.py:336
  220.7 0.0 collective-permute-done.13
  220.7 2.1 add_add_fusion
  222.8 0.1 slice_bitcast_fusion.1
  222.9 17.8 %collective-permute-start.14 = (f32[6,256,128]{2,1,0:T(8,128)S(1)}, f32[6,256,128]{2,1,0:T(8,128)S(1)}, u32[]{:S(2)}, u32[]{:S(2)}) collective-permute-start(f32[6,256,128]{2,1,0:T(8,128)S(1)} %get-tuple-element.30), channel_id=1, source_target_pairs={{0,112},{16,0},{32,16},{48,32},{64,48},{80,64},{96,80},{112,96},{1... | collective-permute-start | bytes 2359304 | tf_op jit(solution)/shard_map/ppermute | solution.py:336
  240.7 0.0 collective-permute-start.15
  240.7 11.1 %collective-permute-done.14 = f32[6,256,128]{2,1,0:T(8,128)S(1)} collective-permute-done((f32[6,256,128]{2,1,0:T(8,128)S(1)}, f32[6,256,128]{2,1,0:T(8,128)S(1)}, u32[]{:S(2)}, u32[]{:S(2)}) %collective-permute-start.14) | collective-permute-done | bytes 786464 | tf_op jit(solution)/shard_map/ppermute | solution.py:336
  251.8 2.2 collective-permute-done.15
  253.9 0.1 fusion.2
  254.1 0.0 copy-start.1
  254.1 0.0 copy-start.3
  254.1 0.0 copy-start.4
  254.1 0.2 reshape.29
  254.3 1.2 copy-done.3
  255.5 0.0 copy-done.4
  255.5 0.5 fusion
  256.0 0.0 copy-done.1
  256.0 1.7 copy.15
  (7 shorter events, 0.1 us)
Async XLA Ops:
  0.6 6.4 %copy-start.5 = (s32[1,1,2,2048]{3,2,1,0:T(2,128)S(1)}, s32[1,1,2,2048]{3,2,1,0:T(2,128)}, u32[]{:S(2)}) copy-start(s32[1,1,2,2048]{3,2,1,0:T(2,128)} %param.10) | copy-start | bytes 49156
  3.1 1.8 copy-start
  3.1 37.6 %collective-permute-start.5 = (f32[2560,128]{1,0:T(8,128)S(1)}, f32[2560,128]{1,0:T(8,128)S(1)}, u32[]{:S(2)}, u32[]{:S(2)}) collective-permute-start(f32[2560,128]{1,0:T(8,128)S(1)} %bitcast.25), channel_id=1, source_target_pairs={{1,0},{2,1},{3,2},{4,3},{5,4},{6,5},{7,6},{8,7},{9,8},{10,9},{11,1... | collective-permute-start | bytes 3932168 | tf_op jit(solution)/shard_map/ppermute | solution.py:330
  3.9 36.9 %collective-permute-start.4 = (f32[2560,128]{1,0:T(8,128)S(1)}, f32[2560,128]{1,0:T(8,128)}, u32[]{:S(2)}, u32[]{:S(2)}) collective-permute-start(f32[2560,128]{1,0:T(8,128)S(1)} %bitcast.26), channel_id=1, source_target_pairs={{0,1},{1,2},{2,3},{3,4},{4,5},{5,6},{6,7},{7,8},{8,9},{9,10},{10,1... | collective-permute-start | bytes 3932168 | tf_op jit(solution)/shard_map/ppermute | solution.py:330
  4.9 35.8 %collective-permute-start.1 = (f32[2560,128]{1,0:T(8,128)S(1)}, f32[2560,128]{1,0:T(8,128)}, u32[]{:S(2)}, u32[]{:S(2)}) collective-permute-start(f32[2560,128]{1,0:T(8,128)S(1)} %bitcast.27), channel_id=1, source_target_pairs={{16,0},{32,16},{48,32},{64,48},{80,64},{96,80},{112,96},{0,112},{1... | collective-permute-start | bytes 3932168 | tf_op jit(solution)/shard_map/ppermute | solution.py:330
  5.0 35.8 %collective-permute-start = (f32[2560,128]{1,0:T(8,128)S(1)}, f32[2560,128]{1,0:T(8,128)}, u32[]{:S(2)}, u32[]{:S(2)}) collective-permute-start(f32[2560,128]{1,0:T(8,128)S(1)} %bitcast.28), channel_id=1, source_target_pairs={{0,16},{16,32},{32,48},{48,64},{64,80},{80,96},{96,112},{112,0},{1... | collective-permute-start | bytes 3932168 | tf_op jit(solution)/shard_map/ppermute | solution.py:330
  12.5 23.7 %collective-permute-start.3 = (s32[1,3,2048]{2,1,0:T(4,128)S(1)}, s32[1,3,2048]{2,1,0:T(4,128)S(1)}, u32[]{:S(2)}, u32[]{:S(2)}) collective-permute-start(s32[1,3,2048]{2,1,0:T(4,128)S(1)} %add_bitcast_fusion.1), channel_id=1, source_target_pairs={{16,0},{32,16},{48,32},{64,48},{80,64},{96,80},{112,96},{0,112},{1... | collective-permute-start | bytes 73736 | tf_op jit(solution)/shard_map/ppermute | solution.py:330
  36.2 4.5 %collective-permute-start.2 = (s32[1,3,2048]{2,1,0:T(4,128)S(1)}, s32[1,3,2048]{2,1,0:T(4,128)S(1)}, u32[]{:S(2)}, u32[]{:S(2)}) collective-permute-start(s32[1,3,2048]{2,1,0:T(4,128)S(1)} %add_bitcast_fusion.1), channel_id=1, source_target_pairs={{0,16},{16,32},{32,48},{48,64},{64,80},{80,96},{96,112},{112,0},{1... | collective-permute-start | bytes 73736 | tf_op jit(solution)/shard_map/ppermute | solution.py:330
  40.8 1.1 copy-start.2
  41.8 47.3 %collective-permute-start.9 = (f32[2560,128]{1,0:T(8,128)}, f32[2560,128]{1,0:T(8,128)}, u32[]{:S(2)}, u32[]{:S(2)}) collective-permute-start(f32[2560,128]{1,0:T(8,128)} %collective-permute-done.refs_1_), channel_id=1, source_target_pairs={{1,0},{2,1},{3,2},{4,3},{5,4},{6,5},{7,6},{8,7},{9,8},{10,9},{11,1... | collective-permute-start | bytes 3932168 | tf_op jit(solution)/shard_map/ppermute | solution.py:330
  43.1 46.0 %collective-permute-start.8 = (f32[2560,128]{1,0:T(8,128)}, f32[2560,128]{1,0:T(8,128)}, u32[]{:S(2)}, u32[]{:S(2)}) collective-permute-start(f32[2560,128]{1,0:T(8,128)} %collective-permute-done.refs_1_), channel_id=1, source_target_pairs={{0,1},{1,2},{2,3},{3,4},{4,5},{5,6},{6,7},{7,8},{8,9},{9,10},{10,1... | collective-permute-start | bytes 3932168 | tf_op jit(solution)/shard_map/ppermute | solution.py:330
  56.0 33.1 %collective-permute-start.11 = (f32[2560,128]{1,0:T(8,128)}, f32[2560,128]{1,0:T(8,128)}, u32[]{:S(2)}, u32[]{:S(2)}) collective-permute-start(f32[2560,128]{1,0:T(8,128)} %collective-permute-done.1.refs_7_), channel_id=1, source_target_pairs={{1,0},{2,1},{3,2},{4,3},{5,4},{6,5},{7,6},{8,7},{9,8},{10,9},{11,1... | collective-permute-start | bytes 3932168 | tf_op jit(solution)/shard_map/ppermute | solution.py:330
  56.0 33.1 %collective-permute-start.10 = (f32[2560,128]{1,0:T(8,128)}, f32[2560,128]{1,0:T(8,128)}, u32[]{:S(2)}, u32[]{:S(2)}) collective-permute-start(f32[2560,128]{1,0:T(8,128)} %collective-permute-done.1.refs_7_), channel_id=1, source_target_pairs={{0,1},{1,2},{2,3},{3,4},{4,5},{5,6},{6,7},{7,8},{8,9},{9,10},{10,1... | collective-permute-start | bytes 3932168 | tf_op jit(solution)/shard_map/ppermute | solution.py:330
  57.7 28.8 %collective-permute-start.7 = (s32[3,1,3,2048]{3,2,1,0:T(4,128)S(1)}, s32[3,1,3,2048]{3,2,1,0:T(4,128)S(1)}, u32[]{:S(2)}, u32[]{:S(2)}) collective-permute-start(s32[3,1,3,2048]{3,2,1,0:T(4,128)S(1)} %add_bitcast_fusion), channel_id=1, source_target_pairs={{1,0},{2,1},{3,2},{4,3},{5,4},{6,5},{7,6},{8,7},{9,8},{10,9},{11,1... | collective-permute-start | bytes 221192 | tf_op jit(solution)/shard_map/ppermute | solution.py:330
  86.6 1.6 collective-permute-start.6
  192.1 28.5 %collective-permute-start.12 = (f32[3,6,256,128]{3,2,1,0:T(8,128)}, f32[3,6,256,128]{3,2,1,0:T(8,128)S(1)}, u32[]{:S(2)}, u32[]{:S(2)}) collective-permute-start(f32[3,6,256,128]{3,2,1,0:T(8,128)} %get-tuple-element.22), channel_id=1, source_target_pairs={{0,15},{1,0},{2,1},{3,2},{4,3},{5,4},{6,5},{7,6},{8,7},{9,8},{10,9... | collective-permute-start | bytes 7077896 | tf_op jit(solution)/shard_map/ppermute | solution.py:336
  192.2 28.5 %collective-permute-start.13 = (f32[3,6,256,128]{3,2,1,0:T(8,128)}, f32[3,6,256,128]{3,2,1,0:T(8,128)S(1)}, u32[]{:S(2)}, u32[]{:S(2)}) collective-permute-start(f32[3,6,256,128]{3,2,1,0:T(8,128)} %get-tuple-element.23), channel_id=1, source_target_pairs={{0,1},{1,2},{2,3},{3,4},{4,5},{5,6},{6,7},{7,8},{8,9},{9,10},{10,1... | collective-permute-start | bytes 7077896 | tf_op jit(solution)/shard_map/ppermute | solution.py:336
  222.9 28.9 %collective-permute-start.14 = (f32[6,256,128]{2,1,0:T(8,128)S(1)}, f32[6,256,128]{2,1,0:T(8,128)S(1)}, u32[]{:S(2)}, u32[]{:S(2)}) collective-permute-start(f32[6,256,128]{2,1,0:T(8,128)S(1)} %get-tuple-element.30), channel_id=1, source_target_pairs={{0,112},{16,0},{32,16},{48,32},{64,48},{80,64},{96,80},{112,96},{1... | collective-permute-start | bytes 2359304 | tf_op jit(solution)/shard_map/ppermute | solution.py:336
  240.7 13.3 %collective-permute-start.15 = (f32[6,256,128]{2,1,0:T(8,128)S(1)}, f32[6,256,128]{2,1,0:T(8,128)S(1)}, u32[]{:S(2)}, u32[]{:S(2)}) collective-permute-start(f32[6,256,128]{2,1,0:T(8,128)S(1)} %get-tuple-element.31), channel_id=1, source_target_pairs={{0,16},{16,32},{32,48},{48,64},{64,80},{80,96},{96,112},{112,0},{1... | collective-permute-start | bytes 2359304 | tf_op jit(solution)/shard_map/ppermute | solution.py:336
  254.1 2.0 copy-start.1
  254.1 1.4 copy-start.3
  254.1 1.4 copy-start.4

commit v5 on v4

--- a/solution.py
+++ b/solution.py
@@ -323,11 +323,99 @@
     )(lists, *sites)
 
 
-def around(value, axis):
-    count = lax.axis_size(axis)
-    forward = [(i, (i + 1) % count) for i in range(count)]
-    backward = [((i + 1) % count, i) for i in range(count)]
-    return [lax.ppermute(value, axis, forward), value, lax.ppermute(value, axis, backward)]
+CHUNKS = 4
+
+
+def halo_kernel(sites_ref, lists_ref, *refs):
+    outs, lists_out = refs[:8], refs[8]
+    send_sem, recv_sem, list_send, list_recv, own_sem = refs[9:]
+    outs = outs[:4] + (None,) + outs[4:]
+    gx, gy = lax.axis_index("gx"), lax.axis_index("gy")
+    n_gx, n_gy = lax.axis_size("gx"), lax.axis_size("gy")
+    mesh_id = pl.DeviceIdType.MESH
+    size = ROWS // CHUNKS
+
+    def device(g):
+        return (lax.rem(gx + g // 3 - 1 + n_gx, n_gx), lax.rem(gy + g % 3 - 1 + n_gy, n_gy))
+
+    barrier = pltpu.get_barrier_semaphore()
+    others = [g for g in range(9) if g != 4]
+    for g in others:
+        pl.semaphore_signal(barrier, inc=1, device_id=device(g), device_id_type=mesh_id)
+    pl.semaphore_wait(barrier, 8)
+
+    def piece(g, source, target, chunk):
+        rows = pl.ds(chunk * size, size)
+        return pltpu.make_async_remote_copy(
+            src_ref=source.at[rows, :],
+            dst_ref=outs[g].at[rows, :],
+            send_sem=send_sem.at[g, chunk],
+            recv_sem=recv_sem.at[g, chunk],
+            device_id=device(target),
+            device_id_type=mesh_id,
+        )
+
+    straight = {}
+    for chunk in range(CHUNKS):
+        for g in (1, 7, 3, 5):
+            straight[g, chunk] = piece(g, sites_ref, 8 - g, chunk)
+    for chunk in range(CHUNKS):
+        for g in (1, 7):
+            straight[g, chunk].start()
+    for chunk in range(CHUNKS):
+        for g in (3, 5):
+            straight[g, chunk].start()
+    listed = []
+    for g in others:
+        listed.append(
+            pltpu.make_async_remote_copy(
+                src_ref=lists_ref,
+                dst_ref=lists_out.at[g],
+                send_sem=list_send.at[g],
+                recv_sem=list_recv.at[g],
+                device_id=device(8 - g),
+                device_id_type=mesh_id,
+            )
+        )
+        listed[-1].start()
+    own = pltpu.make_async_copy(lists_ref, lists_out.at[4], own_sem)
+    own.start()
+    passed = []
+    for chunk in range(CHUNKS):
+        for g in (1, 7):
+            straight[g, chunk].wait_recv()
+            for side in (-1, 1):
+                passed.append(piece(g + side, outs[g], 4 - side, chunk))
+                passed[-1].start()
+    for chunk in range(CHUNKS):
+        for g in (3, 5):
+            straight[g, chunk].wait()
+        for g in (1, 7):
+            straight[g, chunk].wait_send()
+    for copy in passed + listed:
+        copy.wait()
+    own.wait()
+
+
+def halo_exchange(sites, lists):
+    away = pl.BlockSpec(memory_space=pl.ANY)
+    shapes = [jax.ShapeDtypeStruct(sites.shape, sites.dtype)] * 8
+    shapes.append(jax.ShapeDtypeStruct((9,) + lists.shape, lists.dtype))
+    return pl.pallas_call(
+        halo_kernel,
+        out_shape=shapes,
+        in_specs=[away] * 2,
+        out_specs=[away] * 9,
+        scratch_shapes=[
+            pltpu.SemaphoreType.DMA((9, CHUNKS)),
+            pltpu.SemaphoreType.DMA((9, CHUNKS)),
+            pltpu.SemaphoreType.DMA((9,)),
+            pltpu.SemaphoreType.DMA((9,)),
+            pltpu.SemaphoreType.DMA,
+        ],
+        compiler_params=pltpu.CompilerParams(collective_id=0, has_side_effects=True),
+        name="halo",
+    )(sites, lists)
 
 
 def shifted(value, axis, steps):
@@ -347,18 +435,11 @@
     bounds = jnp.arange(slot_total, dtype=jnp.int32)[:16] * TILES
     bounds = jnp.sum((far[None, :] < bounds[:, None]).astype(jnp.int32), 1)
     bounds = jnp.concatenate([bounds, jnp.zeros((slot_total - 16,), jnp.int32)])
-    lists = jnp.stack([far, near, bounds])[None]
-    lists = jnp.concatenate(around(lists, "gx"), 0)[:, None]
-
-    middle = around(sites, "gx")
-    sides = around(sites, "gy")
-    middle[0], middle[2], lists, sides[0], sides[2] = lax.optimization_barrier(
-        (middle[0], middle[2], lists, sides[0], sides[2])
+    lists = jnp.stack([far, near, bounds])
+    *around_sites, lists = halo_exchange(sites, lists)
+    low, mid, high = field_kernel(
+        lists.reshape(27, slot_total), *around_sites[:4], sites, *around_sites[4:]
     )
-    lists = jnp.concatenate(around(lists, "gy"), 1).reshape(27, slot_total)
-    upper = around(middle[0], "gy")
-    lower = around(middle[2], "gy")
-    low, mid, high = field_kernel(lists, *upper, *sides, *lower)
     column = mid + shifted(low, "gy", -1) + shifted(high, "gy", 1)
     field = column[1] + shifted(column[0], "gx", -1) + shifted(column[2], "gx", 1)
     field = field.reshape(6, 1, 1, TILES * TILE)

time: 258 us -> 255 us (0.988)
  the two profiles are of different devices: /device:TPU:85 before, /device:TPU:0 now
where the time goes in v5:
time: 255 us; the launch traced here: 254 us
  Pallas kernels  174 us (68%)
  waiting for transfers between devices  57.6 us (23%)
  other arithmetic  12.3 us (5%)
  local copies, waits for them, and re-layouts  5.8 us (2%)
  starting transfers between devices  2.66 us (1%)
    pallas_call x1, Pallas kernels, halo_exchange(): pl.pallas_call(halo_kernel, out_shape=shapes, in_specs=[away] * 2, out_sp...  91.5 us
    pallas_call x1, Pallas kernels, field_kernel(): pl.pallas_call(kernel, out_shape=[jax.ShapeDtypeStruct((3, 6, TILES, TILE...  82.9 us
    ppermute x4, waiting for transfers between devices, shifted(): return lax.ppermute(value, axis, pairs)  57.6 us
    sort x1, other arithmetic, local(): far, near = lax.sort((far, table[0]), num_keys=1)  5.14 us
  transfers between devices with their start and end apart: 4, of which 3 were waited for; matrix products, arithmetic and copies ran while one was open for 0% of the time, Pallas kernels for 0%

profile of v5, /device:TPU:0, one launch (start us, length us, event | category | flops | bytes accessed | tf_op | source)
XLA Modules:
  0.0 254.1 jit_solution(12983524627339318119)
XLA Ops:
  1.3 0.8 fusion.4
  2.1 5.1 %sort.23 = (s32[2048]{0:T(1024)S(1)}, s32[2048]{0:T(1024)S(1)}, s32[2048]{0:T(1024)}) sort(s32[2048]{0:T(1024)S(1)} %fusion.3, s32[2048]{0:T(1024)S(1)} %bitcast.28, s32[2048]{0:T(1024)S(1)} %iota.10), dimensions={0}, to_apply=%region_0.1 | sort | flops 22528 | bytes 49152 | tf_op jit(solution)/shard_map/sort | solution.py:434
  7.3 0.2 convert_reduce_fusion
  7.5 0.6 pad_add_fusion.lists_ref
  8.1 3.5 %pad_maximum_fusion = f32[10,1,1,32768]{3,2,1,0:T(1,128)} fusion(f32[1,1,1,32768]{3,2,1,0:T(1,128)} %bitcast.24, f32[3,1,1,32768]{3,2,1,0:T(1,128)} %param.6, f32[6,1,1,32768]{3,2,1,0:T(1,128)} %param.8), kind=kLoop, calls=%fused_computation.1 | loop fusion | flops 655360 | bytes 2621440 | tf_op jit(solution)/shard_map/concatenate | solution.py:429
  11.7 91.5 %halo.1 = (f32[2560,128]{1,0:T(8,128)}, f32[2560,128]{1,0:T(8,128)}, f32[2560,128]{1,0:T(8,128)}, f32[2560,128]{1,0:T(8,128)}, f32[2560,128]{1,0:T(8,128)}, /*in...) custom-call(f32[2560,128]{1,0:T(8,128)} %bitcast.21, ...), custom_call_target="tpu_custom_call" | custom-call | tf_op jit(solution)/shard_map/halo/pallas_call | solution.py:404
  103.2 1.8 reshape.28.lists_ref
  104.9 82.9 %pair_fields.1 = (f32[3,6,256,128]{3,2,1,0:T(8,128)}, f32[3,6,256,128]{3,2,1,0:T(8,128)}, f32[3,6,256,128]{3,2,1,0:T(8,128)}) custom-call(s32[27,2048]{1,0:T(8,128)} %reshape.28.lists_ref, f32[2560,128]{1,0:T(8,128)} %get-tuple-element.21.refs_0_, f32[2560,128]{1,0:T(8,128)} %get-tuple-element.22.refs_1_, f32[2560,128]{1,0:T(8,128)} %get-tuple-element.23.refs_2_, ...), custom_call_target="tpu_custom_call" | custom-call | tf_op jit(solution)/shard_map/pair_fields/pallas_call | solution.py:299
  187.9 0.1 collective-permute-start
  187.9 0.5 collective-permute-start.1
  188.4 26.2 %collective-permute-done = f32[3,6,256,128]{3,2,1,0:T(8,128)S(1)} collective-permute-done((f32[3,6,256,128]{3,2,1,0:T(8,128)}, f32[3,6,256,128]{3,2,1,0:T(8,128)S(1)}, u32[]{:S(2)}, u32[]{:S(2)}) %collective-permute-start) | collective-permute-done | bytes 2359328 | tf_op jit(solution)/shard_map/ppermute | solution.py:424
  214.6 5.5 %collective-permute-done.1 = f32[3,6,256,128]{3,2,1,0:T(8,128)S(1)} collective-permute-done((f32[3,6,256,128]{3,2,1,0:T(8,128)}, f32[3,6,256,128]{3,2,1,0:T(8,128)S(1)}, u32[]{:S(2)}, u32[]{:S(2)}) %collective-permute-start.1) | collective-permute-done | bytes 2359328 | tf_op jit(solution)/shard_map/ppermute | solution.py:424
  220.1 2.1 add_add_fusion
  222.2 0.1 slice_bitcast_fusion.1
  222.3 0.1 collective-permute-start.2
  222.4 2.0 collective-permute-start.3
  224.4 25.9 %collective-permute-done.2 = f32[6,256,128]{2,1,0:T(8,128)S(1)} collective-permute-done((f32[6,256,128]{2,1,0:T(8,128)S(1)}, f32[6,256,128]{2,1,0:T(8,128)S(1)}, u32[]{:S(2)}, u32[]{:S(2)}) %collective-permute-start.2) | collective-permute-done | bytes 786464 | tf_op jit(solution)/shard_map/ppermute | solution.py:424
  250.3 0.0 collective-permute-done.3
  250.4 0.1 fusion.2
  250.5 0.0 copy-start
  250.5 0.0 copy-start.1
  250.5 0.0 copy-start.2
  250.5 0.2 reshape.29
  250.7 1.2 copy-done.1
  251.9 0.0 copy-done.2
  251.9 0.5 fusion
  252.4 0.0 copy-done
  252.5 1.7 copy.15
  (4 shorter events, 0.0 us)
Async XLA Ops:
  187.9 26.8 %collective-permute-start = (f32[3,6,256,128]{3,2,1,0:T(8,128)}, f32[3,6,256,128]{3,2,1,0:T(8,128)S(1)}, u32[]{:S(2)}, u32[]{:S(2)}) collective-permute-start(f32[3,6,256,128]{3,2,1,0:T(8,128)} %get-tuple-element.30), channel_id=1, source_target_pairs={{0,15},{1,0},{2,1},{3,2},{4,3},{5,4},{6,5},{7,6},{8,7},{9,8},{10,9... | collective-permute-start | bytes 7077896 | tf_op jit(solution)/shard_map/ppermute | solution.py:424
  187.9 32.2 %collective-permute-start.1 = (f32[3,6,256,128]{3,2,1,0:T(8,128)}, f32[3,6,256,128]{3,2,1,0:T(8,128)S(1)}, u32[]{:S(2)}, u32[]{:S(2)}) collective-permute-start(f32[3,6,256,128]{3,2,1,0:T(8,128)} %get-tuple-element.31), channel_id=1, source_target_pairs={{0,1},{1,2},{2,3},{3,4},{4,5},{5,6},{6,7},{7,8},{8,9},{9,10},{10,1... | collective-permute-start | bytes 7077896 | tf_op jit(solution)/shard_map/ppermute | solution.py:424
  222.3 28.0 %collective-permute-start.2 = (f32[6,256,128]{2,1,0:T(8,128)S(1)}, f32[6,256,128]{2,1,0:T(8,128)S(1)}, u32[]{:S(2)}, u32[]{:S(2)}) collective-permute-start(f32[6,256,128]{2,1,0:T(8,128)S(1)} %get-tuple-element.38), channel_id=1, source_target_pairs={{0,112},{16,0},{32,16},{48,32},{64,48},{80,64},{96,80},{112,96},{1... | collective-permute-start | bytes 2359304 | tf_op jit(solution)/shard_map/ppermute | solution.py:424
  222.4 28.0 %collective-permute-start.3 = (f32[6,256,128]{2,1,0:T(8,128)S(1)}, f32[6,256,128]{2,1,0:T(8,128)S(1)}, u32[]{:S(2)}, u32[]{:S(2)}) collective-permute-start(f32[6,256,128]{2,1,0:T(8,128)S(1)} %get-tuple-element.39), channel_id=1, source_target_pairs={{0,16},{16,32},{32,48},{48,64},{64,80},{80,96},{96,112},{112,0},{1... | collective-permute-start | bytes 2359304 | tf_op jit(solution)/shard_map/ppermute | solution.py:424
  250.5 2.0 copy-start
  250.5 1.4 copy-start.1
  250.5 1.4 copy-start.2

commit v6 on v5

--- a/solution.py
+++ b/solution.py
@@ -324,6 +324,7 @@
 
 
 CHUNKS = 4
+EDGE = 8
 
 
 def halo_kernel(sites_ref, lists_ref, *refs):
@@ -360,10 +361,7 @@
         for g in (1, 7, 3, 5):
             straight[g, chunk] = piece(g, sites_ref, 8 - g, chunk)
     for chunk in range(CHUNKS):
-        for g in (1, 7):
-            straight[g, chunk].start()
-    for chunk in range(CHUNKS):
-        for g in (3, 5):
+        for g in (1, 7, 3, 5):
             straight[g, chunk].start()
     listed = []
     for g in others:
@@ -380,19 +378,33 @@
         listed[-1].start()
     own = pltpu.make_async_copy(lists_ref, lists_out.at[4], own_sem)
     own.start()
-    passed = []
+    first_edge = lax.rem(gy, EDGE) == 0
+    last_edge = lax.rem(gy, EDGE) == EDGE - 1
+    onward = {
+        1: ((~last_edge, 0, 1, 5), (~first_edge, 2, 1, 3)),
+        7: ((~last_edge, 6, 7, 5), (~first_edge, 8, 7, 3)),
+        3: ((first_edge, 0, 3, 7), (first_edge, 6, 3, 1)),
+        5: ((last_edge, 2, 5, 7), (last_edge, 8, 5, 1)),
+    }
+
+    def pass_on(g, chunk, action):
+        for condition, slot, here, target in onward[g]:
+
+            @pl.when(condition)
+            def _(slot=slot, here=here, target=target):
+                action(piece(slot, outs[here], target, chunk))
+
     for chunk in range(CHUNKS):
-        for g in (1, 7):
+        for g in (1, 7, 3, 5):
             straight[g, chunk].wait_recv()
-            for side in (-1, 1):
-                passed.append(piece(g + side, outs[g], 4 - side, chunk))
-                passed[-1].start()
+            pass_on(g, chunk, lambda copy: copy.start())
     for chunk in range(CHUNKS):
-        for g in (3, 5):
-            straight[g, chunk].wait()
-        for g in (1, 7):
+        for g in (1, 7, 3, 5):
             straight[g, chunk].wait_send()
-    for copy in passed + listed:
+            pass_on(g, chunk, lambda copy: copy.wait_send())
+        for g in (0, 2, 6, 8):
+            piece(g, sites_ref, 8 - g, chunk).wait_recv()
+    for copy in listed:
         copy.wait()
     own.wait()
 

time: 255 us -> 250 us (0.980)
  starting transfers between devices: 2.66 us -> 28.1 us
  Pallas kernels: 174 us -> 153 us
  waiting for transfers between devices: 57.6 us -> 46.9 us
    ppermute x4, starting transfers between devices: 2.66 us -> 28.1 us  [shifted(): return lax.ppermute(value, axis, pairs)]
    pallas_call x1, Pallas kernels: 91.5 us -> 67.4 us  [halo_exchange(): pl.pallas_call(halo_kernel, out_shape=shapes, in_specs=[away] * 2, out_sp...]
    ppermute x4, waiting for transfers between devices: 57.6 us -> 46.9 us  [shifted(): return lax.ppermute(value, axis, pairs)]
  transfers between devices with their start and end apart: 4 -> 4, of which waited for: 3 -> 4; matrix products, arithmetic and copies ran while one was open for 0% -> 0% of each run, Pallas kernels for 0% -> 0%
where the time goes in v6:
time: 250 us; the launch traced here: 247 us
  Pallas kernels  153 us (61%)
  waiting for transfers between devices  46.9 us (19%)
  starting transfers between devices  28.1 us (11%)
  other arithmetic  12.3 us (5%)
  local copies, waits for them, and re-layouts  5.8 us (2%)
    pallas_call x1, Pallas kernels, field_kernel(): pl.pallas_call(kernel, out_shape=[jax.ShapeDtypeStruct((3, 6, TILES, TILE...  85.4 us
    pallas_call x1, Pallas kernels, halo_exchange(): pl.pallas_call(halo_kernel, out_shape=shapes, in_specs=[away] * 2, out_sp...  67.4 us
    ppermute x4, waiting for transfers between devices, shifted(): return lax.ppermute(value, axis, pairs)  46.9 us
    ppermute x4, starting transfers between devices, shifted(): return lax.ppermute(value, axis, pairs)  28.1 us
    sort x1, other arithmetic, local(): far, near = lax.sort((far, table[0]), num_keys=1)  5.14 us
  transfers between devices with their start and end apart: 4, of which 4 were waited for; matrix products, arithmetic and copies ran while one was open for 0% of the time, Pallas kernels for 0%

profile of v6, /device:TPU:0, one launch (start us, length us, event | category | flops | bytes accessed | tf_op | source)
XLA Modules:
  0.0 247.3 jit_solution(12979845166110752320)
XLA Ops:
  1.3 0.8 fusion.4
  2.1 5.1 %sort.23 = (s32[2048]{0:T(1024)S(1)}, s32[2048]{0:T(1024)S(1)}, s32[2048]{0:T(1024)}) sort(s32[2048]{0:T(1024)S(1)} %fusion.3, s32[2048]{0:T(1024)S(1)} %bitcast.28, s32[2048]{0:T(1024)S(1)} %iota.10), dimensions={0}, to_apply=%region_0.1 | sort | flops 22528 | bytes 49152 | tf_op jit(solution)/shard_map/sort | solution.py:446
  7.3 0.2 convert_reduce_fusion
  7.5 0.6 pad_add_fusion.lists_ref
  8.1 3.5 %pad_maximum_fusion = f32[10,1,1,32768]{3,2,1,0:T(1,128)} fusion(f32[1,1,1,32768]{3,2,1,0:T(1,128)} %bitcast.24, f32[3,1,1,32768]{3,2,1,0:T(1,128)} %param.6, f32[6,1,1,32768]{3,2,1,0:T(1,128)} %param.8), kind=kLoop, calls=%fused_computation.1 | loop fusion | flops 655360 | bytes 2621440 | tf_op jit(solution)/shard_map/concatenate | solution.py:441
  11.7 67.4 %halo.1 = (f32[2560,128]{1,0:T(8,128)}, f32[2560,128]{1,0:T(8,128)}, f32[2560,128]{1,0:T(8,128)}, f32[2560,128]{1,0:T(8,128)}, f32[2560,128]{1,0:T(8,128)}, /*in...) custom-call(f32[2560,128]{1,0:T(8,128)} %bitcast.21, ...), custom_call_target="tpu_custom_call" | custom-call | tf_op jit(solution)/shard_map/halo/pallas_call | solution.py:416
  79.0 1.8 reshape.28.lists_ref
  80.8 85.4 %pair_fields.1 = (f32[3,6,256,128]{3,2,1,0:T(8,128)}, f32[3,6,256,128]{3,2,1,0:T(8,128)}, f32[3,6,256,128]{3,2,1,0:T(8,128)}) custom-call(s32[27,2048]{1,0:T(8,128)} %reshape.28.lists_ref, f32[2560,128]{1,0:T(8,128)} %get-tuple-element.21.refs_0_, f32[2560,128]{1,0:T(8,128)} %get-tuple-element.22.refs_1_, f32[2560,128]{1,0:T(8,128)} %get-tuple-element.23.refs_2_, ...), custom_call_target="tpu_custom_call" | custom-call | tf_op jit(solution)/shard_map/pair_fields/pallas_call | solution.py:299
  166.2 5.4 %collective-permute-start = (f32[3,6,256,128]{3,2,1,0:T(8,128)}, f32[3,6,256,128]{3,2,1,0:T(8,128)S(1)}, u32[]{:S(2)}, u32[]{:S(2)}) collective-permute-start(f32[3,6,256,128]{3,2,1,0:T(8,128)} %get-tuple-element.30), channel_id=1, source_target_pairs={{0,15},{1,0},{2,1},{3,2},{4,3},{5,4},{6,5},{7,6},{8,7},{9,8},{10,9... | collective-permute-start | bytes 7077896 | tf_op jit(solution)/shard_map/ppermute | solution.py:436
  171.6 0.0 collective-permute-start.1
  171.6 26.7 %collective-permute-done = f32[3,6,256,128]{3,2,1,0:T(8,128)S(1)} collective-permute-done((f32[3,6,256,128]{3,2,1,0:T(8,128)}, f32[3,6,256,128]{3,2,1,0:T(8,128)S(1)}, u32[]{:S(2)}, u32[]{:S(2)}) %collective-permute-start) | collective-permute-done | bytes 2359328 | tf_op jit(solution)/shard_map/ppermute | solution.py:436
  198.3 6.1 %collective-permute-done.1 = f32[3,6,256,128]{3,2,1,0:T(8,128)S(1)} collective-permute-done((f32[3,6,256,128]{3,2,1,0:T(8,128)}, f32[3,6,256,128]{3,2,1,0:T(8,128)S(1)}, u32[]{:S(2)}, u32[]{:S(2)}) %collective-permute-start.1) | collective-permute-done | bytes 2359328 | tf_op jit(solution)/shard_map/ppermute | solution.py:436
  204.5 2.1 add_add_fusion
  206.6 0.1 slice_bitcast_fusion.1
  206.7 22.7 %collective-permute-start.2 = (f32[6,256,128]{2,1,0:T(8,128)S(1)}, f32[6,256,128]{2,1,0:T(8,128)S(1)}, u32[]{:S(2)}, u32[]{:S(2)}) collective-permute-start(f32[6,256,128]{2,1,0:T(8,128)S(1)} %get-tuple-element.38), channel_id=1, source_target_pairs={{0,112},{16,0},{32,16},{48,32},{64,48},{80,64},{96,80},{112,96},{1... | collective-permute-start | bytes 2359304 | tf_op jit(solution)/shard_map/ppermute | solution.py:436
  229.4 0.0 collective-permute-start.3
  229.4 9.5 %collective-permute-done.2 = f32[6,256,128]{2,1,0:T(8,128)S(1)} collective-permute-done((f32[6,256,128]{2,1,0:T(8,128)S(1)}, f32[6,256,128]{2,1,0:T(8,128)S(1)}, u32[]{:S(2)}, u32[]{:S(2)}) %collective-permute-start.2) | collective-permute-done | bytes 786464 | tf_op jit(solution)/shard_map/ppermute | solution.py:436
  238.9 4.6 %collective-permute-done.3 = f32[6,256,128]{2,1,0:T(8,128)S(1)} collective-permute-done((f32[6,256,128]{2,1,0:T(8,128)S(1)}, f32[6,256,128]{2,1,0:T(8,128)S(1)}, u32[]{:S(2)}, u32[]{:S(2)}) %collective-permute-start.3) | collective-permute-done | bytes 786464 | tf_op jit(solution)/shard_map/ppermute | solution.py:436
  243.5 0.1 fusion.2
  243.6 0.0 copy-start
  243.6 0.0 copy-start.1
  243.7 0.0 copy-start.2
  243.7 0.2 reshape.29
  243.9 1.2 copy-done.1
  245.1 0.0 copy-done.2
  245.1 0.5 fusion
  245.6 0.0 copy-done
  245.6 1.7 copy.15
  (4 shorter events, 0.0 us)
Async XLA Ops:
  166.2 32.1 %collective-permute-start = (f32[3,6,256,128]{3,2,1,0:T(8,128)}, f32[3,6,256,128]{3,2,1,0:T(8,128)S(1)}, u32[]{:S(2)}, u32[]{:S(2)}) collective-permute-start(f32[3,6,256,128]{3,2,1,0:T(8,128)} %get-tuple-element.30), channel_id=1, source_target_pairs={{0,15},{1,0},{2,1},{3,2},{4,3},{5,4},{6,5},{7,6},{8,7},{9,8},{10,9... | collective-permute-start | bytes 7077896 | tf_op jit(solution)/shard_map/ppermute | solution.py:436
  171.6 32.8 %collective-permute-start.1 = (f32[3,6,256,128]{3,2,1,0:T(8,128)}, f32[3,6,256,128]{3,2,1,0:T(8,128)S(1)}, u32[]{:S(2)}, u32[]{:S(2)}) collective-permute-start(f32[3,6,256,128]{3,2,1,0:T(8,128)} %get-tuple-element.31), channel_id=1, source_target_pairs={{0,1},{1,2},{2,3},{3,4},{4,5},{5,6},{6,7},{7,8},{8,9},{9,10},{10,1... | collective-permute-start | bytes 7077896 | tf_op jit(solution)/shard_map/ppermute | solution.py:436
  206.7 32.3 %collective-permute-start.2 = (f32[6,256,128]{2,1,0:T(8,128)S(1)}, f32[6,256,128]{2,1,0:T(8,128)S(1)}, u32[]{:S(2)}, u32[]{:S(2)}) collective-permute-start(f32[6,256,128]{2,1,0:T(8,128)S(1)} %get-tuple-element.38), channel_id=1, source_target_pairs={{0,112},{16,0},{32,16},{48,32},{64,48},{80,64},{96,80},{112,96},{1... | collective-permute-start | bytes 2359304 | tf_op jit(solution)/shard_map/ppermute | solution.py:436
  229.4 14.1 %collective-permute-start.3 = (f32[6,256,128]{2,1,0:T(8,128)S(1)}, f32[6,256,128]{2,1,0:T(8,128)S(1)}, u32[]{:S(2)}, u32[]{:S(2)}) collective-permute-start(f32[6,256,128]{2,1,0:T(8,128)S(1)} %get-tuple-element.39), channel_id=1, source_target_pairs={{0,16},{16,32},{32,48},{48,64},{64,80},{80,96},{96,112},{112,0},{1... | collective-permute-start | bytes 2359304 | tf_op jit(solution)/shard_map/ppermute | solution.py:436
  243.6 2.0 copy-start
  243.6 1.4 copy-start.1
  243.7 1.4 copy-start.2

commit v7 on v6

--- a/solution.py
+++ b/solution.py
@@ -94,7 +94,7 @@
 
 
 def kernel(
-    lists_ref, *refs
+    lists_ref, split_ref, *refs
 ):
     sources, refs = refs[:9], refs[9:]
     outs, refs = refs[:3], refs[3:]
@@ -167,11 +167,21 @@
     for g in range(9):
         first = lists_ref[3 * g + 2, 8 - g]
         last = lists_ref[3 * g + 2, 9 - g]
+        if g != 4:
+            last = first + split_ref[g, 0]
 
         def incoming(p, at, g=g):
             return put(at, lists_ref[3 * g, p] & (TILES - 1), lists_ref[3 * g + 1, p], g)
 
         total = lax.fori_loop(first, last, incoming, total)
+        if g != 4:
+            first = lists_ref[14, g] + split_ref[9 + g, 0]
+            last = lists_ref[14, g + 1]
+
+            def kept(p, at, g=g):
+                return put(at, lists_ref[13, p], lists_ref[12, p] & (TILES - 1), g)
+
+            total = lax.fori_loop(first, last, kept, total)
     for k in range((HALVES + 2) * UNROLL):
         blank(total + k)
     groups = (total - 2 * UNROLL + UNROLL - 1) // UNROLL
@@ -293,13 +303,13 @@
 UNUSED = 4 * OUT_ROWS + DUMMY
 
 
-def field_kernel(lists, *sites):
+def field_kernel(lists, split, *sites):
     smem = pl.BlockSpec(memory_space=pltpu.SMEM)
     away = pl.BlockSpec(memory_space=pl.ANY)
     return pl.pallas_call(
         kernel,
         out_shape=[jax.ShapeDtypeStruct((3, 6, TILES, TILE), F32)] * 3,
-        in_specs=[smem] + [away] * 9,
+        in_specs=[smem, smem] + [away] * 9,
         out_specs=[away] * 3,
         scratch_shapes=[
             pltpu.VMEM((9 * OUT_ROWS, TILE), F32),
@@ -320,16 +330,18 @@
         ],
         compiler_params=pltpu.CompilerParams(vmem_limit_bytes=63 * 1024 * 1024),
         name="pair_fields",
-    )(lists, *sites)
+    )(lists, split, *sites)
 
 
 CHUNKS = 4
+TURNS = 5
 EDGE = 8
 
 
-def halo_kernel(sites_ref, lists_ref, *refs):
-    outs, lists_out = refs[:8], refs[8]
-    send_sem, recv_sem, list_send, list_recv, own_sem = refs[9:]
+def halo_kernel(sites_ref, lists_ref, counts_ref, *refs):
+    outs, lists_out, split_ref = refs[:8], refs[8], refs[9]
+    send_sem, recv_sem, list_send, list_recv, own_sem, *refs = refs[10:]
+    nbr_counts, loads, mine, share_send, share_recv = refs
     outs = outs[:4] + (None,) + outs[4:]
     gx, gy = lax.axis_index("gx"), lax.axis_index("gy")
     n_gx, n_gy = lax.axis_size("gx"), lax.axis_size("gy")
@@ -356,6 +368,22 @@
             device_id_type=mesh_id,
         )
 
+    shared = []
+
+    def share(turn, source, dest):
+        for g in others:
+            copy = pltpu.make_async_remote_copy(
+                src_ref=source,
+                dst_ref=dest.at[g],
+                send_sem=share_send.at[turn, g],
+                recv_sem=share_recv.at[turn, g],
+                device_id=device(8 - g),
+                device_id_type=mesh_id,
+            )
+            copy.start()
+            shared.append(copy)
+
+    share(0, counts_ref, nbr_counts)
     straight = {}
     for chunk in range(CHUNKS):
         for g in (1, 7, 3, 5):
@@ -394,10 +422,42 @@
             def _(slot=slot, here=here, target=target):
                 action(piece(slot, outs[here], target, chunk))
 
+    incoming, outgoing, given, kept = {}, {}, {}, {}
+
+    def balance(turn):
+        for copy in shared[8 * turn:8 * turn + 8]:
+            copy.wait_recv()
+        if turn == 0:
+            for g in others:
+                given[g] = incoming[g] = nbr_counts[g, 8 - g:9 - g, :]
+                kept[g] = outgoing[g] = counts_ref[g:g + 1, :]
+        else:
+            before = mine[turn - 1, 0:1, :]
+            for g in others:
+                theirs = loads[turn - 1, g, 0:1, :]
+                come = jnp.floor((theirs - before) * (1.0 / 16.0))
+                given[g] = jnp.clip(given[g] + come, 0.0, incoming[g])
+                leave = jnp.floor((before - theirs) * (1.0 / 16.0))
+                kept[g] = jnp.clip(kept[g] + leave, 0.0, outgoing[g])
+        if turn < TURNS:
+            load = counts_ref[4:5, :]
+            for g in others:
+                load = load + (outgoing[g] - kept[g]) + given[g]
+            mine[turn] = jnp.broadcast_to(load, (8, TILE))
+            share(turn + 1, mine.at[turn], loads.at[turn])
+
     for chunk in range(CHUNKS):
+        balance(chunk)
         for g in (1, 7, 3, 5):
             straight[g, chunk].wait_recv()
             pass_on(g, chunk, lambda copy: copy.start())
+    for turn in range(CHUNKS, TURNS + 1):
+        balance(turn)
+    blank = jnp.zeros((1, TILE), F32)
+    rows = [given.get(g, blank) for g in range(9)] + [kept.get(g, blank) for g in range(9)]
+    split_ref[...] = jnp.concatenate(rows + [blank] * 6, 0).astype(jnp.int32)
+    for copy in shared:
+        copy.wait_send()
     for chunk in range(CHUNKS):
         for g in (1, 7, 3, 5):
             straight[g, chunk].wait_send()
@@ -409,25 +469,32 @@
     own.wait()
 
 
-def halo_exchange(sites, lists):
+def halo_exchange(sites, lists, counts):
     away = pl.BlockSpec(memory_space=pl.ANY)
     shapes = [jax.ShapeDtypeStruct(sites.shape, sites.dtype)] * 8
     shapes.append(jax.ShapeDtypeStruct((9,) + lists.shape, lists.dtype))
+    shapes.append(jax.ShapeDtypeStruct((24, TILE), jnp.int32))
+    vmem = pl.BlockSpec(memory_space=pltpu.VMEM)
     return pl.pallas_call(
         halo_kernel,
         out_shape=shapes,
-        in_specs=[away] * 2,
-        out_specs=[away] * 9,
+        in_specs=[away, away, vmem],
+        out_specs=[away] * 9 + [vmem],
         scratch_shapes=[
             pltpu.SemaphoreType.DMA((9, CHUNKS)),
             pltpu.SemaphoreType.DMA((9, CHUNKS)),
             pltpu.SemaphoreType.DMA((9,)),
             pltpu.SemaphoreType.DMA((9,)),
             pltpu.SemaphoreType.DMA,
+            pltpu.VMEM((9, 16, TILE), F32),
+            pltpu.VMEM((TURNS, 9, 8, TILE), F32),
+            pltpu.VMEM((TURNS, 8, TILE), F32),
+            pltpu.SemaphoreType.DMA((TURNS + 1, 9)),
+            pltpu.SemaphoreType.DMA((TURNS + 1, 9)),
         ],
         compiler_params=pltpu.CompilerParams(collective_id=0, has_side_effects=True),
         name="halo",
-    )(sites, lists)
+    )(sites, lists, counts)
 
 
 def shifted(value, axis, steps):
@@ -446,11 +513,13 @@
     far, near = lax.sort((far, table[0]), num_keys=1)
     bounds = jnp.arange(slot_total, dtype=jnp.int32)[:16] * TILES
     bounds = jnp.sum((far[None, :] < bounds[:, None]).astype(jnp.int32), 1)
+    counts = (bounds[1:10] - bounds[:9]).astype(F32)
+    counts = jnp.broadcast_to(jnp.pad(counts, (0, 7))[:, None], (16, TILE))
     bounds = jnp.concatenate([bounds, jnp.zeros((slot_total - 16,), jnp.int32)])
     lists = jnp.stack([far, near, bounds])
-    *around_sites, lists = halo_exchange(sites, lists)
+    *around_sites, lists, split = halo_exchange(sites, lists, counts)
     low, mid, high = field_kernel(
-        lists.reshape(27, slot_total), *around_sites[:4], sites, *around_sites[4:]
+        lists.reshape(27, slot_total), split, *around_sites[:4], sites, *around_sites[4:]
     )
     column = mid + shifted(low, "gy", -1) + shifted(high, "gy", 1)
     field = column[1] + shifted(column[0], "gx", -1) + shifted(column[2], "gx", 1)

time: 250 us -> 247 us (0.988)
  the two profiles are of different devices: /device:TPU:0 before, /device:TPU:18 now
where the time goes in v7:
time: 247 us
  Pallas kernels  175 us (71%)
  waiting for transfers between devices  45.6 us (18%)
  other arithmetic  12.3 us (5%)
  local copies, waits for them, and re-layouts  6.47 us (3%)
  starting transfers between devices  6.27 us (3%)
    pallas_call x1, Pallas kernels, field_kernel(): pl.pallas_call(kernel, out_shape=[jax.ShapeDtypeStruct((3, 6, TILES, TILE...  92 us
    pallas_call x1, Pallas kernels, halo_exchange(): pl.pallas_call(halo_kernel, out_shape=shapes, in_specs=[away, away, vmem]...  82.7 us
    ppermute x4, waiting for transfers between devices, shifted(): return lax.ppermute(value, axis, pairs)  45.6 us
    ppermute x4, starting transfers between devices, shifted(): return lax.ppermute(value, axis, pairs)  6.27 us
    sort x1, other arithmetic, local(): far, near = lax.sort((far, table[0]), num_keys=1)  5.14 us
  transfers between devices with their start and end apart: 4, of which 3 were waited for; matrix products, arithmetic and copies ran while one was open for 0% of the time, Pallas kernels for 0%

profile of v7, /device:TPU:18, one launch (start us, length us, event | category | flops | bytes accessed | tf_op | source)
XLA Modules:
  0.0 246.7 jit_solution(10328955288405963280)
XLA Ops:
  1.3 0.8 fusion.4
  2.1 5.1 %sort.23 = (s32[2048]{0:T(1024)S(1)}, s32[2048]{0:T(1024)S(1)}, s32[2048]{0:T(1024)}) sort(s32[2048]{0:T(1024)S(1)} %fusion.3, s32[2048]{0:T(1024)S(1)} %bitcast.28, s32[2048]{0:T(1024)S(1)} %iota.10), dimensions={0}, to_apply=%region_0.1 | sort | flops 22528 | bytes 49152 | tf_op jit(solution)/shard_map/sort | solution.py:513
  7.3 0.2 convert_reduce_fusion
  7.5 0.1 subtract_convert_fusion
  7.5 0.6 pad_add_fusion.lists_ref
  8.2 3.5 %pad_maximum_fusion = f32[10,1,1,32768]{3,2,1,0:T(1,128)} fusion(f32[1,1,1,32768]{3,2,1,0:T(1,128)} %bitcast.24, f32[3,1,1,32768]{3,2,1,0:T(1,128)} %param.6, f32[6,1,1,32768]{3,2,1,0:T(1,128)} %param.8), kind=kLoop, calls=%fused_computation.1 | loop fusion | flops 655360 | bytes 2621440 | tf_op jit(solution)/shard_map/concatenate | solution.py:508
  11.7 0.7 broadcast_in_dim.10.counts_ref
  12.4 82.7 %halo.1 = (f32[2560,128]{1,0:T(8,128)}, f32[2560,128]{1,0:T(8,128)}, f32[2560,128]{1,0:T(8,128)}, f32[2560,128]{1,0:T(8,128)}, f32[2560,128]{1,0:T(8,128)}, /*in...) custom-call(f32[2560,128]{1,0:T(8,128)} %bitcast.21, ...), custom_call_target="tpu_custom_call" | custom-call | tf_op jit(solution)/shard_map/halo/pallas_call | solution.py:478
  95.1 1.8 reshape.29.lists_ref
  96.8 92.0 %pair_fields.1 = (f32[3,6,256,128]{3,2,1,0:T(8,128)}, f32[3,6,256,128]{3,2,1,0:T(8,128)}, f32[3,6,256,128]{3,2,1,0:T(8,128)}) custom-call(s32[27,2048]{1,0:T(8,128)} %reshape.29.lists_ref, s32[24,128]{1,0:T(8,128)} %get-tuple-element.22.split_ref, f32[2560,128]{1,0:T(8,128)} %get-tuple-element.23.refs_0_, f32[2560,128]{1,0:T(8,128)} %get-tuple-element.24.refs_1_, ...), custom_call_target="tpu_custom_call" | custom-call | tf_op jit(solution)/shard_map/pair_fields/pallas_call | solution.py:309
  188.9 0.1 collective-permute-start
  189.0 0.5 collective-permute-start.1
  189.5 26.2 %collective-permute-done = f32[3,6,256,128]{3,2,1,0:T(8,128)S(1)} collective-permute-done((f32[3,6,256,128]{3,2,1,0:T(8,128)}, f32[3,6,256,128]{3,2,1,0:T(8,128)S(1)}, u32[]{:S(2)}, u32[]{:S(2)}) %collective-permute-start) | collective-permute-done | bytes 2359328 | tf_op jit(solution)/shard_map/ppermute | solution.py:503
  215.6 1.9 collective-permute-done.1
  217.5 2.1 add_add_fusion
  219.6 0.1 slice_bitcast_fusion.1
  219.7 0.1 collective-permute-start.2
  219.8 5.6 %collective-permute-start.3 = (f32[6,256,128]{2,1,0:T(8,128)S(1)}, f32[6,256,128]{2,1,0:T(8,128)S(1)}, u32[]{:S(2)}, u32[]{:S(2)}) collective-permute-start(f32[6,256,128]{2,1,0:T(8,128)S(1)} %get-tuple-element.41), channel_id=1, source_target_pairs={{0,16},{16,32},{32,48},{48,64},{64,80},{80,96},{96,112},{112,0},{1... | collective-permute-start | bytes 2359304 | tf_op jit(solution)/shard_map/ppermute | solution.py:503
  225.4 17.5 %collective-permute-done.2 = f32[6,256,128]{2,1,0:T(8,128)S(1)} collective-permute-done((f32[6,256,128]{2,1,0:T(8,128)S(1)}, f32[6,256,128]{2,1,0:T(8,128)S(1)}, u32[]{:S(2)}, u32[]{:S(2)}) %collective-permute-start.2) | collective-permute-done | bytes 786464 | tf_op jit(solution)/shard_map/ppermute | solution.py:503
  242.9 0.0 collective-permute-done.3
  242.9 0.1 fusion.2
  243.0 0.0 copy-start
  243.1 0.0 copy-start.1
  243.1 0.0 copy-start.2
  243.1 0.2 reshape.30
  243.3 1.2 copy-done.1
  244.5 0.0 copy-done.2
  244.5 0.5 fusion
  245.0 0.0 copy-done
  245.0 1.7 copy.15
  (5 shorter events, 0.0 us)
Async XLA Ops:
  188.9 26.8 %collective-permute-start = (f32[3,6,256,128]{3,2,1,0:T(8,128)}, f32[3,6,256,128]{3,2,1,0:T(8,128)S(1)}, u32[]{:S(2)}, u32[]{:S(2)}) collective-permute-start(f32[3,6,256,128]{3,2,1,0:T(8,128)} %get-tuple-element.32), channel_id=1, source_target_pairs={{0,15},{1,0},{2,1},{3,2},{4,3},{5,4},{6,5},{7,6},{8,7},{9,8},{10,9... | collective-permute-start | bytes 7077896 | tf_op jit(solution)/shard_map/ppermute | solution.py:503
  189.0 28.5 %collective-permute-start.1 = (f32[3,6,256,128]{3,2,1,0:T(8,128)}, f32[3,6,256,128]{3,2,1,0:T(8,128)S(1)}, u32[]{:S(2)}, u32[]{:S(2)}) collective-permute-start(f32[3,6,256,128]{3,2,1,0:T(8,128)} %get-tuple-element.33), channel_id=1, source_target_pairs={{0,1},{1,2},{2,3},{3,4},{4,5},{5,6},{6,7},{7,8},{8,9},{9,10},{10,1... | collective-permute-start | bytes 7077896 | tf_op jit(solution)/shard_map/ppermute | solution.py:503
  219.7 23.2 %collective-permute-start.2 = (f32[6,256,128]{2,1,0:T(8,128)S(1)}, f32[6,256,128]{2,1,0:T(8,128)S(1)}, u32[]{:S(2)}, u32[]{:S(2)}) collective-permute-start(f32[6,256,128]{2,1,0:T(8,128)S(1)} %get-tuple-element.40), channel_id=1, source_target_pairs={{0,112},{16,0},{32,16},{48,32},{64,48},{80,64},{96,80},{112,96},{1... | collective-permute-start | bytes 2359304 | tf_op jit(solution)/shard_map/ppermute | solution.py:503
  219.8 23.1 %collective-permute-start.3 = (f32[6,256,128]{2,1,0:T(8,128)S(1)}, f32[6,256,128]{2,1,0:T(8,128)S(1)}, u32[]{:S(2)}, u32[]{:S(2)}) collective-permute-start(f32[6,256,128]{2,1,0:T(8,128)S(1)} %get-tuple-element.41), channel_id=1, source_target_pairs={{0,16},{16,32},{32,48},{48,64},{64,80},{80,96},{96,112},{112,0},{1... | collective-permute-start | bytes 2359304 | tf_op jit(solution)/shard_map/ppermute | solution.py:503
  243.0 2.0 copy-start
  243.1 1.4 copy-start.1
  243.1 1.4 copy-start.2

commit v8 on v7

--- a/solution.py
+++ b/solution.py
@@ -276,7 +276,7 @@
     for g in range(9):
         for k in range(6):
             source = out_ref.at[pl.ds(g * OUT_ROWS + k * OUT_STRIDE, TILES), :]
-            place = outs[g % 3].at[g // 3, k]
+            place = outs[g % 3].at[k, g // 3]
             sends.append(pltpu.make_async_copy(source, place, out_sem.at[6 * g + k]))
     for k, send in enumerate(sends):
         if k // 6 != 4:
@@ -308,7 +308,7 @@
     away = pl.BlockSpec(memory_space=pl.ANY)
     return pl.pallas_call(
         kernel,
-        out_shape=[jax.ShapeDtypeStruct((3, 6, TILES, TILE), F32)] * 3,
+        out_shape=[jax.ShapeDtypeStruct((6, 3, TILES, TILE), F32)] * 3,
         in_specs=[smem, smem] + [away] * 9,
         out_specs=[away] * 3,
         scratch_shapes=[
@@ -497,10 +497,99 @@
     )(sites, lists, counts)
 
 
-def shifted(value, axis, steps):
-    count = lax.axis_size(axis)
-    pairs = [(source, (source + steps) % count) for source in range(count)]
-    return lax.ppermute(value, axis, pairs)
+def return_kernel(
+    low_ref, mid_ref, high_ref, perm_ref, pol_ref, field_ref, induced_ref,
+    column, left, right, up, down, mid_sem, gy_send, gy_recv, gx_send, gx_recv,
+):
+    gx, gy = lax.axis_index("gx"), lax.axis_index("gy")
+    n_gx, n_gy = lax.axis_size("gx"), lax.axis_size("gy")
+    mesh_id = pl.DeviceIdType.MESH
+
+    def device(row, col):
+        return (lax.rem(gx + row + n_gx, n_gx), lax.rem(gy + col + n_gy, n_gy))
+
+    barrier = pltpu.get_barrier_semaphore()
+    for row, col in ((-1, 0), (1, 0), (0, -1), (0, 1)):
+        pl.semaphore_signal(barrier, inc=1, device_id=device(row, col), device_id_type=mesh_id)
+    pl.semaphore_wait(barrier, 4)
+
+    def remote(source, dest, send, recv, way, k, target):
+        return pltpu.make_async_remote_copy(
+            src_ref=source.at[k],
+            dst_ref=dest.at[k],
+            send_sem=send.at[way, k],
+            recv_sem=recv.at[way, k],
+            device_id=target,
+            device_id_type=mesh_id,
+        )
+
+    first, second, own = [], [], []
+    for k in range(6):
+        first.append(
+            (
+                remote(low_ref, right, gy_send, gy_recv, 0, k, device(0, -1)),
+                remote(high_ref, left, gy_send, gy_recv, 1, k, device(0, 1)),
+            )
+        )
+        own.append(pltpu.make_async_copy(mid_ref.at[k], column.at[k], mid_sem.at[k]))
+        for copy in first[k]:
+            copy.start()
+        own[k].start()
+
+    def finish(k):
+        for copy in second[k]:
+            copy.wait_recv()
+        total = column[k, 1] + up[k] + down[k]
+        field_ref[k] = total
+        induced_ref[k] = pol_ref[...] * (perm_ref[k] + total)
+
+    for k in range(6):
+        own[k].wait()
+        for copy in first[k]:
+            copy.wait_recv()
+        column[k] = column[k] + left[k] + right[k]
+        second.append(
+            (
+                remote(column.at[:, 0], down, gx_send, gx_recv, 0, k, device(-1, 0)),
+                remote(column.at[:, 2], up, gx_send, gx_recv, 1, k, device(1, 0)),
+            )
+        )
+        for copy in second[k]:
+            copy.start()
+        if k >= 2:
+            finish(k - 2)
+    finish(4)
+    finish(5)
+    for pairs in first + second:
+        for copy in pairs:
+            copy.wait_send()
+
+
+def return_terms(low, mid, high, perm, pol):
+    away = pl.BlockSpec(memory_space=pl.ANY)
+    vmem = pl.BlockSpec(memory_space=pltpu.VMEM)
+    return pl.pallas_call(
+        return_kernel,
+        out_shape=[jax.ShapeDtypeStruct((6, TILES, TILE), F32)] * 2,
+        in_specs=[away] * 3 + [vmem] * 2,
+        out_specs=[vmem] * 2,
+        scratch_shapes=[
+            pltpu.VMEM((6, 3, TILES, TILE), F32),
+            pltpu.VMEM((6, 3, TILES, TILE), F32),
+            pltpu.VMEM((6, 3, TILES, TILE), F32),
+            pltpu.VMEM((6, TILES, TILE), F32),
+            pltpu.VMEM((6, TILES, TILE), F32),
+            pltpu.SemaphoreType.DMA((6,)),
+            pltpu.SemaphoreType.DMA((2, 6)),
+            pltpu.SemaphoreType.DMA((2, 6)),
+            pltpu.SemaphoreType.DMA((2, 6)),
+            pltpu.SemaphoreType.DMA((2, 6)),
+        ],
+        compiler_params=pltpu.CompilerParams(
+            collective_id=1, has_side_effects=True, vmem_limit_bytes=32 * 1024 * 1024
+        ),
+        name="return_terms",
+    )(low, mid, high, perm, pol)
 
 
 def local(positions, polarity, dipoles, perm_fields, pair_list, tile_counts):
@@ -521,10 +610,10 @@
     low, mid, high = field_kernel(
         lists.reshape(27, slot_total), split, *around_sites[:4], sites, *around_sites[4:]
     )
-    column = mid + shifted(low, "gy", -1) + shifted(high, "gy", 1)
-    field = column[1] + shifted(column[0], "gx", -1) + shifted(column[2], "gx", 1)
+    perm = perm_fields.reshape(6, TILES, TILE)
+    field, induced = return_terms(low, mid, high, perm, polarity.reshape(TILES, TILE))
     field = field.reshape(6, 1, 1, TILES * TILE)
-    induced = polarity[None] * (perm_fields + field)
+    induced = induced.reshape(6, 1, 1, TILES * TILE)
     return (field, induced)
 
 

time: 247 us -> 243 us (0.984)
  the two profiles are of different devices: /device:TPU:18 before, /device:TPU:0 now
where the time goes in v8:
time: 243 us; the launch traced here: 241 us
  Pallas kernels  220 us (91%)
  local copies, waits for them, and re-layouts  10 us (4%)
  other arithmetic  9.6 us (4%)
    pallas_call x1, Pallas kernels, field_kernel(): pl.pallas_call(kernel, out_shape=[jax.ShapeDtypeStruct((6, 3, TILES, TILE...  78.4 us
    pallas_call x1, Pallas kernels, halo_exchange(): pl.pallas_call(halo_kernel, out_shape=shapes, in_specs=[away, away, vmem]...  77.7 us
    pallas_call x1, Pallas kernels, return_terms(): pl.pallas_call(return_kernel, out_shape=[jax.ShapeDtypeStruct((6, TILES,...  64.1 us
    unnamed x12, local copies, waits for them, and re-layouts  6.76 us
    sort x1, other arithmetic, local(): far, near = lax.sort((far, table[0]), num_keys=1)  5.14 us

profile of v8, /device:TPU:0, one launch (start us, length us, event | category | flops | bytes accessed | tf_op | source)
XLA Modules:
  0.0 241.2 jit_solution(3662766956708590114)
XLA Ops:
  1.3 0.8 fusion.1
  2.1 5.1 %sort.23 = (s32[2048]{0:T(1024)S(1)}, s32[2048]{0:T(1024)S(1)}, s32[2048]{0:T(1024)}) sort(s32[2048]{0:T(1024)S(1)} %fusion, s32[2048]{0:T(1024)S(1)} %bitcast.22, s32[2048]{0:T(1024)S(1)} %iota.10), dimensions={0}, to_apply=%region_0.1 | sort | flops 22528 | bytes 49152 | tf_op jit(solution)/shard_map/sort | solution.py:602
  7.3 0.2 convert_reduce_fusion
  7.5 0.1 subtract_convert_fusion
  7.5 0.7 broadcast_in_dim.18.counts_ref
  8.2 0.6 pad_add_fusion.lists_ref
  8.9 3.5 %pad_maximum_fusion = f32[10,1,1,32768]{3,2,1,0:T(1,128)} fusion(f32[1,1,1,32768]{3,2,1,0:T(1,128)} %bitcast.16, f32[3,1,1,32768]{3,2,1,0:T(1,128)} %param.6, f32[6,1,1,32768]{3,2,1,0:T(1,128)} %param.8), kind=kLoop, calls=%fused_computation | loop fusion | flops 655360 | bytes 2621440 | tf_op jit(solution)/shard_map/concatenate | solution.py:597
  12.4 77.7 %halo.1 = (f32[2560,128]{1,0:T(8,128)}, f32[2560,128]{1,0:T(8,128)}, f32[2560,128]{1,0:T(8,128)}, f32[2560,128]{1,0:T(8,128)}, f32[2560,128]{1,0:T(8,128)}, /*in...) custom-call(f32[2560,128]{1,0:T(8,128)} %bitcast.18, ...), custom_call_target="tpu_custom_call" | custom-call | tf_op jit(solution)/shard_map/halo/pallas_call | solution.py:478
  90.1 1.8 reshape.35.lists_ref
  91.9 0.0 copy-start.3
  91.9 0.0 copy-start.4
  91.9 78.4 %pair_fields.1 = (f32[6,3,256,128]{3,2,1,0:T(8,128)}, f32[6,3,256,128]{3,2,1,0:T(8,128)}, f32[6,3,256,128]{3,2,1,0:T(8,128)}) custom-call(s32[27,2048]{1,0:T(8,128)} %reshape.35.lists_ref, s32[24,128]{1,0:T(8,128)} %get-tuple-element.24.split_ref, f32[2560,128]{1,0:T(8,128)} %get-tuple-element.25.refs_0_, f32[2560,128]{1,0:T(8,128)} %get-tuple-element.26.refs_1_, ...), custom_call_target="tpu_custom_call" | custom-call | tf_op jit(solution)/shard_map/pair_fields/pallas_call | solution.py:309
  170.3 0.0 copy-done.3
  170.3 0.0 copy-done.4
  170.3 0.0 copy-start
  170.3 1.7 copy-done
  172.0 0.0 copy-start.1
  172.0 1.7 copy-done.1
  173.7 0.0 copy-start.2
  173.7 1.7 copy-done.2
  175.3 64.1 %return_terms.1 = (f32[6,256,128]{2,1,0:T(8,128)S(1)}, f32[6,256,128]{2,1,0:T(8,128)S(1)}) custom-call(f32[6,3,256,128]{3,2,1,0:T(8,128)S(1)} %copy-done, f32[6,3,256,128]{3,2,1,0:T(8,128)S(1)} %copy-done.1, f32[6,3,256,128]{3,2,1,0:T(8,128)S(1)} %copy-done.2, f32[6,256,128]{2,1,0:T(8,128)S(1)} %bitcast.15, f32[256,128]{1,0:T(8,128)S(1)} %bitcast.17), custom_call_target="tpu_custom_call" | custom-call | tf_op jit(solution)/shard_map/return_terms/pallas_call | solution.py:571
  239.5 0.9 copy.17
  240.4 0.9 copy.18
  (5 shorter events, 0.0 us)
Async XLA Ops:
  91.9 78.4 %copy-start.3 = (f32[6,1,1,32768]{3,2,1,0:T(1,128)S(1)}, f32[6,1,1,32768]{3,2,1,0:T(1,128)}, u32[]{:S(2)}) copy-start(f32[6,1,1,32768]{3,2,1,0:T(1,128)} %param.9) | copy-start | bytes 2359300
  91.9 78.4 %copy-start.4 = (f32[1,1,32768]{2,1,0:T(1,128)S(1)}, f32[1,1,32768]{2,1,0:T(1,128)}, u32[]{:S(2)}) copy-start(f32[1,1,32768]{2,1,0:T(1,128)} %param.7) | copy-start | bytes 393220
  170.3 1.7 copy-start
  172.0 1.7 copy-start.1
  173.7 1.7 copy-start.2

commit v9 on v8

--- a/solution.py
+++ b/solution.py
@@ -334,7 +334,8 @@
 
 
 CHUNKS = 4
-TURNS = 5
+TURNS = 3
+AHEAD = 2
 EDGE = 8
 
 
@@ -388,9 +389,12 @@
     for chunk in range(CHUNKS):
         for g in (1, 7, 3, 5):
             straight[g, chunk] = piece(g, sites_ref, 8 - g, chunk)
-    for chunk in range(CHUNKS):
+    def begin(chunk):
         for g in (1, 7, 3, 5):
             straight[g, chunk].start()
+
+    for chunk in range(AHEAD):
+        begin(chunk)
     listed = []
     for g in others:
         listed.append(
@@ -451,6 +455,8 @@
         for g in (1, 7, 3, 5):
             straight[g, chunk].wait_recv()
             pass_on(g, chunk, lambda copy: copy.start())
+        if chunk + AHEAD < CHUNKS:
+            begin(chunk + AHEAD)
     for turn in range(CHUNKS, TURNS + 1):
         balance(turn)
     blank = jnp.zeros((1, TILE), F32)
@@ -586,7 +592,7 @@
             pltpu.SemaphoreType.DMA((2, 6)),
         ],
         compiler_params=pltpu.CompilerParams(
-            collective_id=1, has_side_effects=True, vmem_limit_bytes=32 * 1024 * 1024
+            collective_id=1, has_side_effects=True, vmem_limit_bytes=63 * 1024 * 1024
         ),
         name="return_terms",
     )(low, mid, high, perm, pol)

time: 243 us -> 246 us (1.012)
  Pallas kernels: 220 us -> 228 us
  local copies, waits for them, and re-layouts: 10 us -> 6.29 us
    pallas_call x1, Pallas kernels: 78.4 us -> 95.9 us  [field_kernel(): pl.pallas_call(kernel, out_shape=[jax.ShapeDtypeStruct((6, 3, TILES, TILE...]
    pallas_call x1, Pallas kernels: 77.7 us -> 72.6 us  [halo_exchange(): pl.pallas_call(halo_kernel, out_shape=shapes, in_specs=[away, away, vmem]...]
    pallas_call x1, Pallas kernels: 64.1 us -> 59.5 us  [return_terms(): pl.pallas_call(return_kernel, out_shape=[jax.ShapeDtypeStruct((6, TILES,...]
    unnamed x12 -> x4, local copies, waits for them, and re-layouts: 6.76 us -> 3.02 us
where the time goes in v9:
time: 246 us; the launch traced here: 245 us
  Pallas kernels  228 us (93%)
  other arithmetic  9.6 us (4%)
  local copies, waits for them, and re-layouts  6.29 us (3%)
    pallas_call x1, Pallas kernels, field_kernel(): pl.pallas_call(kernel, out_shape=[jax.ShapeDtypeStruct((6, 3, TILES, TILE...  95.9 us
    pallas_call x1, Pallas kernels, halo_exchange(): pl.pallas_call(halo_kernel, out_shape=shapes, in_specs=[away, away, vmem]...  72.6 us
    pallas_call x1, Pallas kernels, return_terms(): pl.pallas_call(return_kernel, out_shape=[jax.ShapeDtypeStruct((6, TILES,...  59.5 us
    sort x1, other arithmetic, local(): far, near = lax.sort((far, table[0]), num_keys=1)  5.14 us

profile of v9, /device:TPU:0, one launch (start us, length us, event | category | flops | bytes accessed | tf_op | source)
XLA Modules:
  0.0 245.2 jit_solution(16499395391774801120)
XLA Ops:
  1.3 0.8 fusion.1
  2.1 5.1 %sort.23 = (s32[2048]{0:T(1024)S(1)}, s32[2048]{0:T(1024)S(1)}, s32[2048]{0:T(1024)}) sort(s32[2048]{0:T(1024)S(1)} %fusion, s32[2048]{0:T(1024)S(1)} %bitcast.22, s32[2048]{0:T(1024)S(1)} %iota.10), dimensions={0}, to_apply=%region_0.1 | sort | flops 22528 | bytes 49152 | tf_op jit(solution)/shard_map/sort | solution.py:608
  7.3 0.2 convert_reduce_fusion
  7.5 0.1 subtract_convert_fusion
  7.5 0.7 broadcast_in_dim.18.counts_ref
  8.2 0.6 pad_add_fusion.lists_ref
  8.9 3.5 %pad_maximum_fusion = f32[10,1,1,32768]{3,2,1,0:T(1,128)} fusion(f32[1,1,1,32768]{3,2,1,0:T(1,128)} %bitcast.18, f32[3,1,1,32768]{3,2,1,0:T(1,128)} %param.6, f32[6,1,1,32768]{3,2,1,0:T(1,128)} %param.8), kind=kLoop, calls=%fused_computation | loop fusion | flops 655360 | bytes 2621440 | tf_op jit(solution)/shard_map/concatenate | solution.py:603
  12.4 72.6 %halo.1 = (f32[2560,128]{1,0:T(8,128)}, f32[2560,128]{1,0:T(8,128)}, f32[2560,128]{1,0:T(8,128)}, f32[2560,128]{1,0:T(8,128)}, f32[2560,128]{1,0:T(8,128)}, /*in...) custom-call(f32[2560,128]{1,0:T(8,128)} %bitcast.13, ...), custom_call_target="tpu_custom_call" | custom-call | tf_op jit(solution)/shard_map/halo/pallas_call | solution.py:484
  85.1 1.8 reshape.35.lists_ref
  86.8 95.9 %pair_fields.1 = (f32[6,3,256,128]{3,2,1,0:T(8,128)}, f32[6,3,256,128]{3,2,1,0:T(8,128)}, f32[6,3,256,128]{3,2,1,0:T(8,128)}) custom-call(s32[27,2048]{1,0:T(8,128)} %reshape.35.lists_ref, s32[24,128]{1,0:T(8,128)} %get-tuple-element.24.split_ref, f32[2560,128]{1,0:T(8,128)} %get-tuple-element.25.refs_0_, f32[2560,128]{1,0:T(8,128)} %get-tuple-element.26.refs_1_, ...), custom_call_target="tpu_custom_call" | custom-call | tf_op jit(solution)/shard_map/pair_fields/pallas_call | solution.py:309
  182.7 59.5 %return_terms.1 = (f32[6,256,128]{2,1,0:T(8,128)}, f32[6,256,128]{2,1,0:T(8,128)}) custom-call(f32[6,3,256,128]{3,2,1,0:T(8,128)} %get-tuple-element.33.low_ref, f32[6,3,256,128]{3,2,1,0:T(8,128)} %get-tuple-element.34.mid_ref, f32[6,3,256,128]{3,2,1,0:T(8,128)} %get-tuple-element.35.high_ref, f32[6,256,128]{2,1,0:T(8,128)} %bitcast.17, f32[256,128]{1,0:T(8,128)} %bitcast.19), custom_call_target="tpu_custom_call" | custom-call | tf_op jit(solution)/shard_map/return_terms/pallas_call | solution.py:577
  242.2 0.0 copy-start
  242.2 2.1 copy.17
  244.3 0.0 copy-done
  244.3 0.9 copy.18
  (5 shorter events, 0.0 us)
Async XLA Ops:
  242.2 2.1 copy-start

commit v10 on v9

--- a/solution.py
+++ b/solution.py
@@ -505,7 +505,8 @@
 
 def return_kernel(
     low_ref, mid_ref, high_ref, perm_ref, pol_ref, field_ref, induced_ref,
-    column, left, right, up, down, mid_sem, gy_send, gy_recv, gx_send, gx_recv,
+    column, left, right, up, down, edge_in, edge_own, edge_sum,
+    mid_sem, gy_send, gy_recv, gx_send, gx_recv, edge_send, edge_recv, edge_sem,
 ):
     gx, gy = lax.axis_index("gx"), lax.axis_index("gy")
     n_gx, n_gy = lax.axis_size("gx"), lax.axis_size("gy")
@@ -529,18 +530,71 @@
             device_id_type=mesh_id,
         )
 
-    first, second, own = [], [], []
+    edges = (lax.rem(gy, EDGE) == 0, lax.rem(gy, EDGE) == EDGE - 1)
+    sources, dests = (low_ref, high_ref), (right, left)
+    targets = (device(0, -1), device(0, 1))
+    second, own = [], []
+
+    def either(condition, yes, no):
+        pl.when(condition)(yes)
+        pl.when(jnp.logical_not(condition))(no)
+
+    def whole(way, k):
+        return remote(sources[way], dests[way], gy_send, gy_recv, way, k, targets[way])
+
+    def summed(way, k):
+        return pltpu.make_async_remote_copy(
+            src_ref=edge_sum.at[k],
+            dst_ref=dests[way].at[k, 1],
+            send_sem=gy_send.at[way, k],
+            recv_sem=gy_recv.at[way, k],
+            device_id=targets[way],
+            device_id_type=mesh_id,
+        )
+
+    def along(way, k, slot):
+        return pltpu.make_async_remote_copy(
+            src_ref=sources[way].at[k, 2 - 2 * slot],
+            dst_ref=edge_in.at[slot, k],
+            send_sem=edge_send.at[slot, k],
+            recv_sem=edge_recv.at[slot, k],
+            device_id=device(1 - 2 * slot, 0),
+            device_id_type=mesh_id,
+        )
+
+    def centre(way, k):
+        return pltpu.make_async_copy(sources[way].at[k, 1], edge_own.at[k], edge_sem.at[k])
+
     for k in range(6):
-        first.append(
-            (
-                remote(low_ref, right, gy_send, gy_recv, 0, k, device(0, -1)),
-                remote(high_ref, left, gy_send, gy_recv, 1, k, device(0, 1)),
-            )
-        )
+        for way in range(2):
+
+            def start_edge(way=way, k=k):
+                along(way, k, 0).start()
+                along(way, k, 1).start()
+                centre(way, k).start()
+
+            either(edges[way], start_edge, lambda way=way, k=k: whole(way, k).start())
         own.append(pltpu.make_async_copy(mid_ref.at[k], column.at[k], mid_sem.at[k]))
-        for copy in first[k]:
-            copy.start()
         own[k].start()
+
+    for way in range(2):
+
+        @pl.when(edges[1 - way])
+        def _(way=way):
+            for k in range(6):
+                for row in (0, 2):
+                    dests[way][k, row] = jnp.zeros((TILES, TILE), F32)
+
+    def edge_stage(k):
+        for way in range(2):
+
+            @pl.when(edges[way])
+            def _(way=way):
+                centre(way, k).wait()
+                along(way, k, 0).wait_recv()
+                along(way, k, 1).wait_recv()
+                edge_sum[k] = edge_own[k] + edge_in[0, k] + edge_in[1, k]
+                summed(way, k).start()
 
     def finish(k):
         for copy in second[k]:
@@ -549,10 +603,16 @@
         field_ref[k] = total
         induced_ref[k] = pol_ref[...] * (perm_ref[k] + total)
 
+    edge_stage(0)
+    edge_stage(1)
     for k in range(6):
         own[k].wait()
-        for copy in first[k]:
-            copy.wait_recv()
+        for way in range(2):
+            either(
+                edges[1 - way],
+                lambda way=way: summed(way, k).wait_recv(),
+                lambda way=way: whole(way, k).wait_recv(),
+            )
         column[k] = column[k] + left[k] + right[k]
         second.append(
             (
@@ -562,12 +622,22 @@
         )
         for copy in second[k]:
             copy.start()
+        if k + 2 < 6:
+            edge_stage(k + 2)
         if k >= 2:
             finish(k - 2)
     finish(4)
     finish(5)
-    for pairs in first + second:
-        for copy in pairs:
+    for k in range(6):
+        for way in range(2):
+
+            def end_edge(way=way, k=k):
+                along(way, k, 0).wait_send()
+                along(way, k, 1).wait_send()
+                summed(way, k).wait_send()
+
+            either(edges[way], end_edge, lambda way=way, k=k: whole(way, k).wait_send())
+        for copy in second[k]:
             copy.wait_send()
 
 
@@ -585,11 +655,17 @@
             pltpu.VMEM((6, 3, TILES, TILE), F32),
             pltpu.VMEM((6, TILES, TILE), F32),
             pltpu.VMEM((6, TILES, TILE), F32),
+            pltpu.VMEM((2, 6, TILES, TILE), F32),
+            pltpu.VMEM((6, TILES, TILE), F32),
+            pltpu.VMEM((6, TILES, TILE), F32),
             pltpu.SemaphoreType.DMA((6,)),
             pltpu.SemaphoreType.DMA((2, 6)),
             pltpu.SemaphoreType.DMA((2, 6)),
             pltpu.SemaphoreType.DMA((2, 6)),
             pltpu.SemaphoreType.DMA((2, 6)),
+            pltpu.SemaphoreType.DMA((2, 6)),
+            pltpu.SemaphoreType.DMA((2, 6)),
+            pltpu.SemaphoreType.DMA((6,)),
         ],
         compiler_params=pltpu.CompilerParams(
             collective_id=1, has_side_effects=True, vmem_limit_bytes=63 * 1024 * 1024

time: 246 us -> 227 us (0.923)
  the two profiles are of different devices: /device:TPU:0 before, /device:TPU:6 now
where the time goes in v10:
time: 227 us; the launch traced here: 231 us
  Pallas kernels  213 us (94%)
  other arithmetic  9.6 us (4%)
  local copies, waits for them, and re-layouts  6.29 us (3%)
    pallas_call x1, Pallas kernels, field_kernel(): pl.pallas_call(kernel, out_shape=[jax.ShapeDtypeStruct((6, 3, TILES, TILE...  98.5 us
    pallas_call x1, Pallas kernels, halo_exchange(): pl.pallas_call(halo_kernel, out_shape=shapes, in_specs=[away, away, vmem]...  71.4 us
    pallas_call x1, Pallas kernels, return_terms(): pl.pallas_call(return_kernel, out_shape=[jax.ShapeDtypeStruct((6, TILES,...  43.5 us
    sort x1, other arithmetic, local(): far, near = lax.sort((far, table[0]), num_keys=1)  5.14 us

profile of v10, /device:TPU:6, one launch (start us, length us, event | category | flops | bytes accessed | tf_op | source)
XLA Modules:
  0.0 230.7 jit_solution(4038251248238314537)
XLA Ops:
  1.3 0.8 fusion.1
  2.1 5.1 %sort.23 = (s32[2048]{0:T(1024)S(1)}, s32[2048]{0:T(1024)S(1)}, s32[2048]{0:T(1024)}) sort(s32[2048]{0:T(1024)S(1)} %fusion, s32[2048]{0:T(1024)S(1)} %bitcast.22, s32[2048]{0:T(1024)S(1)} %iota.10), dimensions={0}, to_apply=%region_0.1 | sort | flops 22528 | bytes 49152 | tf_op jit(solution)/shard_map/sort | solution.py:684
  7.3 0.2 convert_reduce_fusion
  7.5 0.1 subtract_convert_fusion
  7.5 0.7 broadcast_in_dim.18.counts_ref
  8.2 0.6 pad_add_fusion.lists_ref
  8.9 3.5 %pad_maximum_fusion = f32[10,1,1,32768]{3,2,1,0:T(1,128)} fusion(f32[1,1,1,32768]{3,2,1,0:T(1,128)} %bitcast.18, f32[3,1,1,32768]{3,2,1,0:T(1,128)} %param.6, f32[6,1,1,32768]{3,2,1,0:T(1,128)} %param.8), kind=kLoop, calls=%fused_computation | loop fusion | flops 655360 | bytes 2621440 | tf_op jit(solution)/shard_map/concatenate | solution.py:679
  12.4 71.4 %halo.1 = (f32[2560,128]{1,0:T(8,128)}, f32[2560,128]{1,0:T(8,128)}, f32[2560,128]{1,0:T(8,128)}, f32[2560,128]{1,0:T(8,128)}, f32[2560,128]{1,0:T(8,128)}, /*in...) custom-call(f32[2560,128]{1,0:T(8,128)} %bitcast.13, ...), custom_call_target="tpu_custom_call" | custom-call | tf_op jit(solution)/shard_map/halo/pallas_call | solution.py:484
  83.8 1.8 reshape.35.lists_ref
  85.6 98.5 %pair_fields.1 = (f32[6,3,256,128]{3,2,1,0:T(8,128)}, f32[6,3,256,128]{3,2,1,0:T(8,128)}, f32[6,3,256,128]{3,2,1,0:T(8,128)}) custom-call(s32[27,2048]{1,0:T(8,128)} %reshape.35.lists_ref, s32[24,128]{1,0:T(8,128)} %get-tuple-element.24.split_ref, f32[2560,128]{1,0:T(8,128)} %get-tuple-element.25.refs_0_, f32[2560,128]{1,0:T(8,128)} %get-tuple-element.26.refs_1_, ...), custom_call_target="tpu_custom_call" | custom-call | tf_op jit(solution)/shard_map/pair_fields/pallas_call | solution.py:309
  184.1 43.5 %return_terms.1 = (f32[6,256,128]{2,1,0:T(8,128)}, f32[6,256,128]{2,1,0:T(8,128)}) custom-call(f32[6,3,256,128]{3,2,1,0:T(8,128)} %get-tuple-element.33.low_ref, f32[6,3,256,128]{3,2,1,0:T(8,128)} %get-tuple-element.34.mid_ref, f32[6,3,256,128]{3,2,1,0:T(8,128)} %get-tuple-element.35.high_ref, f32[6,256,128]{2,1,0:T(8,128)} %bitcast.17, f32[256,128]{1,0:T(8,128)} %bitcast.19), custom_call_target="tpu_custom_call" | custom-call | tf_op jit(solution)/shard_map/return_terms/pallas_call | solution.py:647
  227.6 0.0 copy-start
  227.6 2.1 copy.17
  229.8 0.0 copy-done
  229.8 0.9 copy.18
  (5 shorter events, 0.0 us)
Async XLA Ops:
  227.6 2.1 copy-start

commit v11 on v10

--- a/solution.py
+++ b/solution.py
@@ -333,7 +333,7 @@
     )(lists, split, *sites)
 
 
-CHUNKS = 4
+CHUNKS = 8
 TURNS = 3
 AHEAD = 2
 EDGE = 8
@@ -451,7 +451,8 @@
             share(turn + 1, mine.at[turn], loads.at[turn])
 
     for chunk in range(CHUNKS):
-        balance(chunk)
+        if chunk <= TURNS:
+            balance(chunk)
         for g in (1, 7, 3, 5):
             straight[g, chunk].wait_recv()
             pass_on(g, chunk, lambda copy: copy.start())

time: 227 us -> 236 us (1.040)
  the two profiles are of different devices: /device:TPU:6 before, /device:TPU:0 now
where the time goes in v11:
time: 236 us; the launch traced here: 235 us
  Pallas kernels  218 us (92%)
  other arithmetic  9.6 us (4%)
  local copies, waits for them, and re-layouts  6.29 us (3%)
    pallas_call x1, Pallas kernels, field_kernel(): pl.pallas_call(kernel, out_shape=[jax.ShapeDtypeStruct((6, 3, TILES, TILE...  95.8 us
    pallas_call x1, Pallas kernels, halo_exchange(): pl.pallas_call(halo_kernel, out_shape=shapes, in_specs=[away, away, vmem]...  75.1 us
    pallas_call x1, Pallas kernels, return_terms(): pl.pallas_call(return_kernel, out_shape=[jax.ShapeDtypeStruct((6, TILES,...  46.7 us
    sort x1, other arithmetic, local(): far, near = lax.sort((far, table[0]), num_keys=1)  5.14 us

profile of v11, /device:TPU:0, one launch (start us, length us, event | category | flops | bytes accessed | tf_op | source)
XLA Modules:
  0.0 234.8 jit_solution(11709979500634934128)
XLA Ops:
  1.3 0.8 fusion.1
  2.1 5.1 %sort.23 = (s32[2048]{0:T(1024)S(1)}, s32[2048]{0:T(1024)S(1)}, s32[2048]{0:T(1024)}) sort(s32[2048]{0:T(1024)S(1)} %fusion, s32[2048]{0:T(1024)S(1)} %bitcast.22, s32[2048]{0:T(1024)S(1)} %iota.10), dimensions={0}, to_apply=%region_0.1 | sort | flops 22528 | bytes 49152 | tf_op jit(solution)/shard_map/sort | solution.py:685
  7.3 0.2 convert_reduce_fusion
  7.5 0.1 subtract_convert_fusion
  7.5 0.7 broadcast_in_dim.18.counts_ref
  8.2 0.6 pad_add_fusion.lists_ref
  8.9 3.5 %pad_maximum_fusion = f32[10,1,1,32768]{3,2,1,0:T(1,128)} fusion(f32[1,1,1,32768]{3,2,1,0:T(1,128)} %bitcast.18, f32[3,1,1,32768]{3,2,1,0:T(1,128)} %param.6, f32[6,1,1,32768]{3,2,1,0:T(1,128)} %param.8), kind=kLoop, calls=%fused_computation | loop fusion | flops 655360 | bytes 2621440 | tf_op jit(solution)/shard_map/concatenate | solution.py:680
  12.4 75.1 %halo.1 = (f32[2560,128]{1,0:T(8,128)}, f32[2560,128]{1,0:T(8,128)}, f32[2560,128]{1,0:T(8,128)}, f32[2560,128]{1,0:T(8,128)}, f32[2560,128]{1,0:T(8,128)}, /*in...) custom-call(f32[2560,128]{1,0:T(8,128)} %bitcast.13, ...), custom_call_target="tpu_custom_call" | custom-call | tf_op jit(solution)/shard_map/halo/pallas_call | solution.py:485
  87.5 1.8 reshape.35.lists_ref
  89.3 95.8 %pair_fields.1 = (f32[6,3,256,128]{3,2,1,0:T(8,128)}, f32[6,3,256,128]{3,2,1,0:T(8,128)}, f32[6,3,256,128]{3,2,1,0:T(8,128)}) custom-call(s32[27,2048]{1,0:T(8,128)} %reshape.35.lists_ref, s32[24,128]{1,0:T(8,128)} %get-tuple-element.24.split_ref, f32[2560,128]{1,0:T(8,128)} %get-tuple-element.25.refs_0_, f32[2560,128]{1,0:T(8,128)} %get-tuple-element.26.refs_1_, ...), custom_call_target="tpu_custom_call" | custom-call | tf_op jit(solution)/shard_map/pair_fields/pallas_call | solution.py:309
  185.1 46.7 %return_terms.1 = (f32[6,256,128]{2,1,0:T(8,128)}, f32[6,256,128]{2,1,0:T(8,128)}) custom-call(f32[6,3,256,128]{3,2,1,0:T(8,128)} %get-tuple-element.33.low_ref, f32[6,3,256,128]{3,2,1,0:T(8,128)} %get-tuple-element.34.mid_ref, f32[6,3,256,128]{3,2,1,0:T(8,128)} %get-tuple-element.35.high_ref, f32[6,256,128]{2,1,0:T(8,128)} %bitcast.17, f32[256,128]{1,0:T(8,128)} %bitcast.19), custom_call_target="tpu_custom_call" | custom-call | tf_op jit(solution)/shard_map/return_terms/pallas_call | solution.py:648
  231.8 0.0 copy-start
  231.8 2.1 copy.17
  233.9 0.0 copy-done
  233.9 0.9 copy.18
  (5 shorter events, 0.0 us)
Async XLA Ops:
  231.8 2.1 copy-start

commit v12 on v11

--- a/solution.py
+++ b/solution.py
@@ -334,8 +334,8 @@
 
 
 CHUNKS = 8
-TURNS = 3
-AHEAD = 2
+TURNS = 2
+AHEAD = 4
 EDGE = 8
 
 

time: 236 us -> 233 us (0.987)
  the two profiles are of different devices: /device:TPU:0 before, /device:TPU:8 now
where the time goes in v12:
time: 233 us; the launch traced here: 232 us
  Pallas kernels  215 us (92%)
  other arithmetic  9.6 us (4%)
  local copies, waits for them, and re-layouts  6.29 us (3%)
    pallas_call x1, Pallas kernels, field_kernel(): pl.pallas_call(kernel, out_shape=[jax.ShapeDtypeStruct((6, 3, TILES, TILE...  92.1 us
    pallas_call x1, Pallas kernels, halo_exchange(): pl.pallas_call(halo_kernel, out_shape=shapes, in_specs=[away, away, vmem]...  71.4 us
    pallas_call x1, Pallas kernels, return_terms(): pl.pallas_call(return_kernel, out_shape=[jax.ShapeDtypeStruct((6, TILES,...  51.5 us
    sort x1, other arithmetic, local(): far, near = lax.sort((far, table[0]), num_keys=1)  5.14 us

profile of v12, /device:TPU:8, one launch (start us, length us, event | category | flops | bytes accessed | tf_op | source)
XLA Modules:
  0.0 232.2 jit_solution(7674232867860504791)
XLA Ops:
  1.3 0.8 fusion.1
  2.1 5.1 %sort.23 = (s32[2048]{0:T(1024)S(1)}, s32[2048]{0:T(1024)S(1)}, s32[2048]{0:T(1024)}) sort(s32[2048]{0:T(1024)S(1)} %fusion, s32[2048]{0:T(1024)S(1)} %bitcast.22, s32[2048]{0:T(1024)S(1)} %iota.10), dimensions={0}, to_apply=%region_0.1 | sort | flops 22528 | bytes 49152 | tf_op jit(solution)/shard_map/sort | solution.py:685
  7.3 0.2 convert_reduce_fusion
  7.5 0.1 subtract_convert_fusion
  7.5 0.7 broadcast_in_dim.18.counts_ref
  8.2 0.6 pad_add_fusion.lists_ref
  8.9 3.5 %pad_maximum_fusion = f32[10,1,1,32768]{3,2,1,0:T(1,128)} fusion(f32[1,1,1,32768]{3,2,1,0:T(1,128)} %bitcast.18, f32[3,1,1,32768]{3,2,1,0:T(1,128)} %param.6, f32[6,1,1,32768]{3,2,1,0:T(1,128)} %param.8), kind=kLoop, calls=%fused_computation | loop fusion | flops 655360 | bytes 2621440 | tf_op jit(solution)/shard_map/concatenate | solution.py:680
  12.4 71.4 %halo.1 = (f32[2560,128]{1,0:T(8,128)}, f32[2560,128]{1,0:T(8,128)}, f32[2560,128]{1,0:T(8,128)}, f32[2560,128]{1,0:T(8,128)}, f32[2560,128]{1,0:T(8,128)}, /*in...) custom-call(f32[2560,128]{1,0:T(8,128)} %bitcast.13, ...), custom_call_target="tpu_custom_call" | custom-call | tf_op jit(solution)/shard_map/halo/pallas_call | solution.py:485
  83.8 1.8 reshape.35.lists_ref
  85.6 92.1 %pair_fields.1 = (f32[6,3,256,128]{3,2,1,0:T(8,128)}, f32[6,3,256,128]{3,2,1,0:T(8,128)}, f32[6,3,256,128]{3,2,1,0:T(8,128)}) custom-call(s32[27,2048]{1,0:T(8,128)} %reshape.35.lists_ref, s32[24,128]{1,0:T(8,128)} %get-tuple-element.24.split_ref, f32[2560,128]{1,0:T(8,128)} %get-tuple-element.25.refs_0_, f32[2560,128]{1,0:T(8,128)} %get-tuple-element.26.refs_1_, ...), custom_call_target="tpu_custom_call" | custom-call | tf_op jit(solution)/shard_map/pair_fields/pallas_call | solution.py:309
  177.7 51.5 %return_terms.1 = (f32[6,256,128]{2,1,0:T(8,128)}, f32[6,256,128]{2,1,0:T(8,128)}) custom-call(f32[6,3,256,128]{3,2,1,0:T(8,128)} %get-tuple-element.33.low_ref, f32[6,3,256,128]{3,2,1,0:T(8,128)} %get-tuple-element.34.mid_ref, f32[6,3,256,128]{3,2,1,0:T(8,128)} %get-tuple-element.35.high_ref, f32[6,256,128]{2,1,0:T(8,128)} %bitcast.17, f32[256,128]{1,0:T(8,128)} %bitcast.19), custom_call_target="tpu_custom_call" | custom-call | tf_op jit(solution)/shard_map/return_terms/pallas_call | solution.py:648
  229.2 0.0 copy-start
  229.2 2.1 copy.17
  231.4 0.0 copy-done
  231.4 0.9 copy.18
  (5 shorter events, 0.0 us)
Async XLA Ops:
  229.2 2.1 copy-start
